TPU v7x, 32 devices: a whole 2x2x4 slice. The times are simulated.
32 devices in a mesh: dp: 8 (over z, x), fsdp: 4 (over y, core).
Axes of the slice: x: 2, y: 2, z: 4, core: 2. Of those that a mesh axis runs over, the one named last changes fastest.
Arguments:
- patches: bfloat16 [256, 100, 1024], P(('dp', 'fsdp')), may hold values from -6 to 6
- cotangent: bfloat16 [256, 100, 1024], P(('dp', 'fsdp')), may hold values from -6 to 6
- pad_mask: int32 [256, 100], P(('dp', 'fsdp')), may hold values from 0 to 1, as said below
- attend_weight: float32 [1024, 3072], P(('dp', 'fsdp'))
- attend_first: float32 [1024, 3072], P(('dp', 'fsdp'))
- attend_second: float32 [1024, 3072], P(('dp', 'fsdp')), may hold values from 1.9868215e-13 to 7.947286e-13
- output_weight: float32 [1024, 1024], P(('dp', 'fsdp'))
- output_first: float32 [1024, 1024], P(('dp', 'fsdp'))
- output_second: float32 [1024, 1024], P(('dp', 'fsdp')), may hold values from 1.9868215e-13 to 7.947286e-13
- expand_weight: float32 [1024, 4096], P(('dp', 'fsdp'))
- expand_first: float32 [1024, 4096], P(('dp', 'fsdp'))
- expand_second: float32 [1024, 4096], P(('dp', 'fsdp')), may hold values from 1.9868215e-13 to 7.947286e-13
- shrink_weight: float32 [4096, 1024], P(('dp', 'fsdp'))
- shrink_first: float32 [4096, 1024], P(('dp', 'fsdp'))
- shrink_second: float32 [4096, 1024], P(('dp', 'fsdp')), may hold values from 1.9868215e-13 to 7.947286e-13
- vector_params: float32 [12, 1024], replicated
- vector_first: float32 [12, 1024], replicated, may hold values from -9.536743e-06 to 9.536743e-06
- vector_second: float32 [12, 1024], replicated, may hold values from 1.9868215e-13 to 7.947286e-13
- position_table: float32 [361, 32], replicated, may hold values from -5 to 5
- table_first: float32 [361, 32], replicated, may hold values from -9.536743e-06 to 9.536743e-06
- table_second: float32 [361, 32], replicated, may hold values from 1.9868215e-13 to 7.947286e-13
Outputs:
- block_out: bfloat16 [256, 100, 1024], P(('dp', 'fsdp'))
- input_grad: float32 [256, 100, 1024], P(('dp', 'fsdp'))
- attend_grad: float32 [1024, 3072], P(('dp', 'fsdp'))
- attend_first_new: float32 [1024, 3072], P(('dp', 'fsdp'))
- attend_second_new: float32 [1024, 3072], P(('dp', 'fsdp'))
- attend_new: float32 [1024, 3072], P(('dp', 'fsdp'))
- attend_copy: bfloat16 [1024, 3072], P(('dp', 'fsdp'))
- output_grad: float32 [1024, 1024], P(('dp', 'fsdp'))
- output_first_new: float32 [1024, 1024], P(('dp', 'fsdp'))
- output_second_new: float32 [1024, 1024], P(('dp', 'fsdp'))
- output_new: float32 [1024, 1024], P(('dp', 'fsdp'))
- output_copy: bfloat16 [1024, 1024], P(('dp', 'fsdp'))
- expand_grad: float32 [1024, 4096], P(('dp', 'fsdp'))
- expand_first_new: float32 [1024, 4096], P(('dp', 'fsdp'))
- expand_second_new: float32 [1024, 4096], P(('dp', 'fsdp'))
- expand_new: float32 [1024, 4096], P(('dp', 'fsdp'))
- expand_copy: bfloat16 [1024, 4096], P(('dp', 'fsdp'))
- shrink_grad: float32 [4096, 1024], P(('dp', 'fsdp'))
- shrink_first_new: float32 [4096, 1024], P(('dp', 'fsdp'))
- shrink_second_new: float32 [4096, 1024], P(('dp', 'fsdp'))
- shrink_new: float32 [4096, 1024], P(('dp', 'fsdp'))
- shrink_copy: bfloat16 [4096, 1024], P(('dp', 'fsdp'))
- vector_grad: float32 [12, 1024], replicated
- vector_first_new: float32 [12, 1024], replicated
- vector_second_new: float32 [12, 1024], replicated
- vector_new: float32 [12, 1024], replicated
- table_grad: float32 [361, 32], replicated
- table_first_new: float32 [361, 32], replicated
- table_second_new: float32 [361, 32], replicated
- table_new: float32 [361, 32], replicated
- clip_norm: float32 [], replicated
- matrix_norms: float32 [2, 4], replicated
Inputs may be any that keep to these rules, and one draw needn't show every extreme that they name: `pad_mask`: patch 0 of every window is 1.
All inputs are finite; a program needn't handle non-finite values.
Results may differ from a plain program's by a relative error of at most 0.013.
The roundings to bfloat16 on the way count: a program that leaves them out, or rounds other values in their place, can miss the bound.
Values may be sent and summed in bfloat16 or wider, within the bound.
A program may use at most 256 MiB of HBM per device.

v0:
```python
import jax
import jax.numpy as jnp
from jax import lax
from jax.sharding import PartitionSpec as P

HEADS = 32
WS = 10
STEP = 10


EPSILON = 1e-05
MOMENT_ONE = 0.9
MOMENT_TWO = 0.999
LEARN_RATE = 0.3
DECAY = 0.01
ADAM_EPS = 1e-06
CLIP_LIMIT = 0.05
MASK_FILL = 10000.0
HIGH = lax.Precision.HIGHEST


def position_index(size):
    cells = jnp.arange(size * size, dtype=jnp.int32)
    rows = cells // size
    cols = cells % size
    drow = rows[:, None] - rows[None, :] + size - 1
    dcol = cols[:, None] - cols[None, :] + size - 1
    return drow * (2 * size - 1) + dcol


def normalize(value):
    centre = value - jnp.mean(value, axis=-1, keepdims=True)
    spread = lax.rsqrt(jnp.mean(centre * centre, axis=-1, keepdims=True) + EPSILON)
    return (centre * spread, spread)


def norm_back(grad_out, normed, spread, gain):
    scaled = grad_out * gain
    mean_one = jnp.mean(scaled, axis=-1, keepdims=True)
    mean_two = jnp.mean(scaled * normed, axis=-1, keepdims=True)
    return spread * (scaled - mean_one - normed * mean_two)


def gelu_slope(value):
    return (
        0.5 * (1.0 + lax.erf(value * 0.7071067811865476))
        + value * jnp.exp(-0.5 * value * value) * 0.3989422804014327
    )


def inner_product(left, right):
    return lax.dot_general(
        left, right, (((0,), (0,)), ((), ())), preferred_element_type=jnp.float32
    )


def times_transpose(left, right):
    return lax.dot_general(
        left, right, (((1,), (1,)), ((), ())), preferred_element_type=jnp.float32
    )


def moments(grad, first, second, weight, factor):
    clipped = grad * factor
    first_new = MOMENT_ONE * first + (1.0 - MOMENT_ONE) * clipped
    second_new = MOMENT_TWO * second + (1.0 - MOMENT_TWO) * clipped * clipped
    update = (
        first_new
        / (1.0 - MOMENT_ONE**STEP)
        / (jnp.sqrt(second_new / (1.0 - MOMENT_TWO**STEP)) + ADAM_EPS)
        + DECAY * weight
    )
    return (first_new, second_new, update)


def local(
    patches,
    cotangent,
    pad_mask,
    attend_weight,
    attend_first,
    attend_second,
    output_weight,
    output_first,
    output_second,
    expand_weight,
    expand_first,
    expand_second,
    shrink_weight,
    shrink_first,
    shrink_second,
    vector_params,
    vector_first,
    vector_second,
    position_table,
    table_first,
    table_second,
):
    windows, cells, width = patches.shape
    rows = windows * cells
    head_dim = width // HEADS
    scale = head_dim ** (-0.5)
    keep = pad_mask.astype(jnp.float32)
    local_count = jnp.sum(keep)
    total = lax.psum(local_count, ("dp", "fsdp"))
    masters = (attend_weight, output_weight, expand_weight, shrink_weight)
    copy_attend = attend_weight.astype(jnp.bfloat16)
    copy_output = output_weight.astype(jnp.bfloat16)
    copy_expand = expand_weight.astype(jnp.bfloat16)
    copy_shrink = shrink_weight.astype(jnp.bfloat16)
    gathered = (
        lax.all_gather(copy_attend, ("dp", "fsdp"), axis=0, tiled=True),
        lax.all_gather(copy_output, ("dp", "fsdp"), axis=0, tiled=True),
        lax.all_gather(copy_expand, ("dp", "fsdp"), axis=0, tiled=True),
        lax.all_gather(copy_shrink, ("dp", "fsdp"), axis=0, tiled=True),
    )
    w_attend, w_output, w_expand, w_shrink = gathered
    gain_one, shift_one = (vector_params[0], vector_params[1])
    query_bias, value_bias, output_bias = (vector_params[2], vector_params[3], vector_params[4])
    gain_two, shift_two, shrink_bias = (vector_params[5], vector_params[6], vector_params[7])
    expand_bias = vector_params[8:].reshape(-1)
    source = patches.reshape(rows, width).astype(jnp.float32)
    normed_one, spread_one = normalize(source)
    hidden_one = (normed_one * gain_one + shift_one).astype(jnp.bfloat16)
    joint = jnp.dot(hidden_one, w_attend, preferred_element_type=jnp.float32)
    query = (
        (joint[:, :width] + query_bias)
        .astype(jnp.bfloat16)
        .reshape(windows, cells, HEADS, head_dim)
    )
    keys = joint[:, width : 2 * width].astype(jnp.bfloat16).reshape(windows, cells, HEADS, head_dim)
    values = (
        (joint[:, 2 * width :] + value_bias)
        .astype(jnp.bfloat16)
        .reshape(windows, cells, HEADS, head_dim)
    )
    relative = position_table.shape[0]
    onehot = (
        position_index(WS).reshape(-1)[:, None] == jnp.arange(relative, dtype=jnp.int32)[None, :]
    ).astype(jnp.float32)
    bias = (
        jnp.dot(onehot, position_table, precision=HIGH)
        .reshape(cells, cells, HEADS)
        .transpose(2, 0, 1)
    )
    scores = jnp.einsum("wihd,wjhd->whij", query, keys, preferred_element_type=jnp.float32) * scale
    scores = scores + bias[None] + (keep[:, None, None, :] - 1.0) * MASK_FILL
    probs = jax.nn.softmax(scores, axis=-1)
    probs_low = probs.astype(jnp.bfloat16)
    attended = jnp.einsum("whij,wjhd->wihd", probs_low, values, preferred_element_type=jnp.float32)
    attended = attended.reshape(rows, width).astype(jnp.bfloat16)
    middle = source + jnp.dot(attended, w_output, preferred_element_type=jnp.float32) + output_bias
    normed_two, spread_two = normalize(middle)
    hidden_two = (normed_two * gain_two + shift_two).astype(jnp.bfloat16)
    before = jnp.dot(hidden_two, w_expand, preferred_element_type=jnp.float32) + expand_bias
    activated = jax.nn.gelu(before, approximate=False).astype(jnp.bfloat16)
    result = middle + jnp.dot(activated, w_shrink, preferred_element_type=jnp.float32) + shrink_bias
    block_out = result.astype(jnp.bfloat16).reshape(windows, cells, width)
    w_attend, w_output, w_expand, w_shrink = (
        lax.all_gather(copy_attend, ("dp", "fsdp"), axis=0, tiled=True),
        lax.all_gather(copy_output, ("dp", "fsdp"), axis=0, tiled=True),
        lax.all_gather(copy_expand, ("dp", "fsdp"), axis=0, tiled=True),
        lax.all_gather(copy_shrink, ("dp", "fsdp"), axis=0, tiled=True),
    )
    upstream = cotangent.reshape(rows, width).astype(jnp.float32) * keep.reshape(rows, 1)
    upstream_low = upstream.astype(jnp.bfloat16)
    grad_shrink = inner_product(activated, upstream_low)
    grad_shrink_bias = jnp.sum(upstream, axis=0)
    grad_act = times_transpose(upstream_low, w_shrink)
    grad_before = (grad_act * gelu_slope(before)).astype(jnp.bfloat16)
    grad_expand = inner_product(hidden_two, grad_before)
    grad_expand_bias = jnp.sum(grad_before.astype(jnp.float32), axis=0)
    grad_hidden_two = times_transpose(grad_before, w_expand)
    grad_gain_two = jnp.sum(grad_hidden_two * normed_two, axis=0)
    grad_shift_two = jnp.sum(grad_hidden_two, axis=0)
    grad_middle = upstream + norm_back(grad_hidden_two, normed_two, spread_two, gain_two)
    grad_branch = grad_middle.astype(jnp.bfloat16)
    grad_output = inner_product(attended, grad_branch)
    grad_output_bias = jnp.sum(grad_branch.astype(jnp.float32), axis=0)
    grad_attended = (
        times_transpose(grad_branch, w_output)
        .astype(jnp.bfloat16)
        .reshape(windows, cells, HEADS, head_dim)
    )
    grad_probs = jnp.einsum(
        "wihd,wjhd->whij", grad_attended, values, preferred_element_type=jnp.float32
    )
    grad_scores = (
        probs * (grad_probs - jnp.sum(probs * grad_probs, axis=-1, keepdims=True))
    ).astype(jnp.bfloat16)
    grad_query = (
        jnp.einsum("whij,wjhd->wihd", grad_scores, keys, preferred_element_type=jnp.float32) * scale
    ).astype(jnp.bfloat16)
    grad_keys = (
        jnp.einsum("whij,wihd->wjhd", grad_scores, query, preferred_element_type=jnp.float32)
        * scale
    ).astype(jnp.bfloat16)
    grad_values = jnp.einsum(
        "whij,wihd->wjhd", probs_low, grad_attended, preferred_element_type=jnp.float32
    ).astype(jnp.bfloat16)
    grad_bias = (
        jnp.sum(grad_scores.astype(jnp.float32), axis=0)
        .transpose(1, 2, 0)
        .reshape(cells * cells, HEADS)
    )
    grad_table = lax.dot_general(onehot, grad_bias, (((0,), (0,)), ((), ())), precision=HIGH)
    grad_joint = jnp.concatenate(
        [
            grad_query.reshape(rows, width),
            grad_keys.reshape(rows, width),
            grad_values.reshape(rows, width),
        ],
        axis=1,
    )
    grad_attend = inner_product(hidden_one, grad_joint)
    grad_query_bias = jnp.sum(grad_query.reshape(rows, width).astype(jnp.float32), axis=0)
    grad_value_bias = jnp.sum(grad_values.reshape(rows, width).astype(jnp.float32), axis=0)
    grad_hidden_one = times_transpose(grad_joint, w_attend)
    grad_gain_one = jnp.sum(grad_hidden_one * normed_one, axis=0)
    grad_shift_one = jnp.sum(grad_hidden_one, axis=0)
    grad_source = grad_middle + norm_back(grad_hidden_one, normed_one, spread_one, gain_one)
    owned = (
        lax.psum_scatter(grad_attend, ("dp", "fsdp"), scatter_dimension=0, tiled=True),
        lax.psum_scatter(grad_output, ("dp", "fsdp"), scatter_dimension=0, tiled=True),
        lax.psum_scatter(grad_expand, ("dp", "fsdp"), scatter_dimension=0, tiled=True),
        lax.psum_scatter(grad_shrink, ("dp", "fsdp"), scatter_dimension=0, tiled=True),
    )
    vector_local = jnp.concatenate(
        [
            jnp.stack(
                [
                    grad_gain_one,
                    grad_shift_one,
                    grad_query_bias,
                    grad_value_bias,
                    grad_output_bias,
                    grad_gain_two,
                    grad_shift_two,
                    grad_shrink_bias,
                ]
            ),
            grad_expand_bias.reshape(-1, width),
        ],
        axis=0,
    )
    vector_sum, table_sum = lax.psum((vector_local, grad_table), ("dp", "fsdp"))
    input_grad = (grad_source / total).reshape(windows, cells, width)
    matrix_grads = tuple((g / total for g in owned))
    vector_grad = vector_sum / total
    table_grad = table_sum / total
    grad_squares = jnp.stack([jnp.sum(g * g) for g in matrix_grads])
    weight_squares = jnp.stack([jnp.sum(m * m) for m in masters])
    grad_total, weight_total = lax.psum((grad_squares, weight_squares), ("dp", "fsdp"))
    clip_norm = jnp.sqrt(
        jnp.sum(grad_total) + jnp.sum(vector_grad * vector_grad) + jnp.sum(table_grad * table_grad)
    )
    factor = jnp.minimum(1.0, CLIP_LIMIT / clip_norm)
    firsts = (attend_first, output_first, expand_first, shrink_first)
    seconds = (attend_second, output_second, expand_second, shrink_second)
    sectioned = [
        moments(matrix_grads[k], firsts[k], seconds[k], masters[k], factor) for k in range(4)
    ]
    update_squares = jnp.stack([jnp.sum(s[2] * s[2]) for s in sectioned])
    update_total = lax.psum(update_squares, ("dp", "fsdp"))
    weight_norms = jnp.sqrt(weight_total)
    update_norms = jnp.sqrt(update_total)
    matrix_outs = []
    for k in range(4):
        fresh = masters[k] - LEARN_RATE * (weight_norms[k] / update_norms[k]) * sectioned[k][2]
        matrix_outs.append(
            (matrix_grads[k], sectioned[k][0], sectioned[k][1], fresh, fresh.astype(jnp.bfloat16))
        )
    vec_first, vec_second, vec_update = moments(
        vector_grad, vector_first, vector_second, vector_params, factor
    )
    vec_ratio = jnp.sqrt(jnp.sum(vector_params * vector_params, axis=1, keepdims=True)) / jnp.sqrt(
        jnp.sum(vec_update * vec_update, axis=1, keepdims=True)
    )
    vec_fresh = vector_params - LEARN_RATE * vec_ratio * vec_update
    tab_first, tab_second, tab_update = moments(
        table_grad, table_first, table_second, position_table, factor
    )
    tab_ratio = jnp.sqrt(jnp.sum(position_table * position_table)) / jnp.sqrt(
        jnp.sum(tab_update * tab_update)
    )
    tab_fresh = position_table - LEARN_RATE * tab_ratio * tab_update
    matrix_norms = jnp.stack([weight_norms, update_norms])
    attend_o, output_o, expand_o, shrink_o = matrix_outs
    return (
        block_out,
        input_grad,
        attend_o[0],
        attend_o[1],
        attend_o[2],
        attend_o[3],
        attend_o[4],
        output_o[0],
        output_o[1],
        output_o[2],
        output_o[3],
        output_o[4],
        expand_o[0],
        expand_o[1],
        expand_o[2],
        expand_o[3],
        expand_o[4],
        shrink_o[0],
        shrink_o[1],
        shrink_o[2],
        shrink_o[3],
        shrink_o[4],
        vector_grad,
        vec_first,
        vec_second,
        vec_fresh,
        table_grad,
        tab_first,
        tab_second,
        tab_fresh,
        clip_norm,
        matrix_norms,
    )


def solution(mesh):
    in_specs = (
        P(("dp", "fsdp"), None, None),
        P(("dp", "fsdp"), None, None),
        P(("dp", "fsdp"), None),
        P(("dp", "fsdp"), None),
        P(("dp", "fsdp"), None),
        P(("dp", "fsdp"), None),
        P(("dp", "fsdp"), None),
        P(("dp", "fsdp"), None),
        P(("dp", "fsdp"), None),
        P(("dp", "fsdp"), None),
        P(("dp", "fsdp"), None),
        P(("dp", "fsdp"), None),
        P(("dp", "fsdp"), None),
        P(("dp", "fsdp"), None),
        P(("dp", "fsdp"), None),
        P(),
        P(),
        P(),
        P(),
        P(),
        P(),
    )
    out_specs = (
        P(("dp", "fsdp"), None, None),
        P(("dp", "fsdp"), None, None),
        P(("dp", "fsdp"), None),
        P(("dp", "fsdp"), None),
        P(("dp", "fsdp"), None),
        P(("dp", "fsdp"), None),
        P(("dp", "fsdp"), None),
        P(("dp", "fsdp"), None),
        P(("dp", "fsdp"), None),
        P(("dp", "fsdp"), None),
        P(("dp", "fsdp"), None),
        P(("dp", "fsdp"), None),
        P(("dp", "fsdp"), None),
        P(("dp", "fsdp"), None),
        P(("dp", "fsdp"), None),
        P(("dp", "fsdp"), None),
        P(("dp", "fsdp"), None),
        P(("dp", "fsdp"), None),
        P(("dp", "fsdp"), None),
        P(("dp", "fsdp"), None),
        P(("dp", "fsdp"), None),
        P(("dp", "fsdp"), None),
        P(),
        P(),
        P(),
        P(),
        P(),
        P(),
        P(),
        P(),
        P(),
        P(),
    )
    return jax.shard_map(local, mesh=mesh, in_specs=in_specs, out_specs=out_specs, check_vma=False)
```

profile of v0, /device:TPU:0, one launch (start us, length us, event | category | flops | bytes accessed | tf_op | source)
XLA Modules:
  0.0 1242.0 jit_solution(12158565402579934840)
XLA Ops:
  23.9 11.2 fusion.2
  41.8 3.5 reshape.303
  47.3 36.5 %all-gather.5.cloned.1.call-done = bf16[1024,3072]{1,0:T(8,128)(2,1)} async-done(((bf16[32,3072]{1,0:T(8,128)(2,1)}), bf16[1024,3072]{1,0:T(8,128)(2,1)}) %all-gather.5.cloned.1.call-update) | async-done | bytes 6291472 | tf_op jit(solution)/shard_map/all_gather | solution.py:112
  83.9 8.6 fusion.67
  99.8 4.1 reshape.292
  103.9 5.4 reshape.291
  109.3 3.7 copy.131
  113.0 5.0 reshape.290
  118.0 11.4 fusion.83
  130.0 7.5 convert_bitcast_fusion.1
  137.6 3.8 copy.139
  141.4 4.5 convert_element_type.139
  145.9 4.3 fusion.88
  152.4 69.7 %all-gather.9.cloned.1.call-done = bf16[1024,4096]{1,0:T(8,128)(2,1)} async-done(((bf16[32,4096]{1,0:T(8,128)(2,1)}), bf16[1024,4096]{1,0:T(8,128)(2,1)}) %all-gather.9.cloned.1.call-update) | async-done | bytes 8388624 | tf_op jit(solution)/shard_map/all_gather | solution.py:114
  222.1 40.3 %fusion.5 = (bf16[800,4096]{1,0:T(8,128)(2,1)}, f32[800,4096]{1,0:T(8,128)}) fusion(f32[4096]{0:T(1024)S(1)} %bitcast.111, bf16[1024,4096]{1,0:T(8,128)(2,1)} %all-gather.9.cloned.1.call-done, f32[800,1024]{1,0:T(8,128)} %copy-done.6, f32[1024]{0:T(1024)S(1)} %bitcast.114, f32[1024]{0:T(1024)S(1)} %bitcast.103, f32[800]{0:T(1024)S(1)} %add_rsqrt_fusion, ...), kind=kOutput, calls=%fused_computation.13 | convolution fusion | flops 6931251200 | bytes 31357184 | tf_op jit(solution)/shard_map/dot_general | solution.py:155
  262.4 39.1 %all-gather.11.cloned.1.call-done = bf16[4096,1024]{1,0:T(8,128)(2,1)} async-done(((bf16[128,1024]{1,0:T(8,128)(2,1)}), bf16[4096,1024]{1,0:T(8,128)(2,1)}) %all-gather.11.cloned.1.call-update) | async-done | bytes 8388624 | tf_op jit(solution)/shard_map/all_gather | solution.py:115
  301.6 16.8 %convert_reduce_fusion.1 = (f32[4096]{0:T(1024)S(1)}, bf16[800,4096]{1,0:T(8,128)(2,1)}) fusion(f32[800,4096]{1,0:T(8,128)} %get-tuple-element.250, f32[4096]{0:T(1024)S(1)} %bitcast.112, bf16[4096,1024]{1,0:T(8,128)(2,1)} %all-gather.11.cloned.1.call-done, f32[800,1024]{1,0:T(8,128)S(1)} %copy-done.9, f32[800]{0:T(1024)S(1)} %copy-done.46), kind=kOutput, calls=%fused_computation.20 | convolution fusion | flops 6755119104 | bytes 31362176 | tf_op jit(solution)/shard_map/dot_general | solution.py:58
  318.4 10.9 multiply_reduce_fusion.2
  330.9 4.3 fusion.61
  335.2 4.7 convolution_convert_fusion
  342.9 3.4 reshape.295
  347.9 8.7 convert_reduce_fusion.2
  361.8 14.9 %multiply_reduce_fusion = (f32[8,32,100]{2,1,0:T(8,128)S(1)}, f32[8,32,100,100]{2,3,1,0:T(8,128)}) fusion(f32[8,32,100,100]{2,3,1,0:T(8,128)} %get-tuple-element.246, f32[8,32,100]{2,1,0:T(8,128)S(1)} %copy-done.35, bf16[8,100,32,32]{1,0,3,2:T(8,128)(2,1)} %reshape.290, bf16[8,100,32,32]{1,0,3,2:T(8,128)(2,1)} %reshape.295), kind=kOutput, calls=%fused_computation.8 | convolution fusion | flops 171494400 | bytes 23961600 | tf_op jit(solution)/shard_map/wihd,wjhd->whij/dot_general | solution.py:185
  376.7 11.8 convert_reduce_fusion
  388.5 3.8 fusion.43
  392.3 3.7 copy.149
  396.0 4.8 reshape.297
  400.9 5.1 convert_reduce_fusion.3
  416.5 10.2 fusion.66
  426.7 16.0 %fusion.68 = f32[1024,4096]{1,0:T(8,128)} fusion(bf16[800,4096]{1,0:T(8,128)(2,1)} %get-tuple-element.260, f32[800,1024]{1,0:T(8,128)} %copy-done.6, f32[1024]{0:T(1024)S(1)} %bitcast.115, f32[1024]{0:T(1024)S(1)} %bitcast.106, f32[800]{0:T(1024)S(1)} %add_rsqrt_fusion, f32[800]{0:T(1024)S(1)} %broadcast_multiply_fusion.4), kind=kOutput, calls=%fused_computation.183 | convolution fusion | flops 6714982400 | bytes 26622208 | tf_op jit(solution)/shard_map/dot_general | solution.py:52
  442.8 16.1 %fusion.65 = f32[4096,1024]{1,0:T(8,128)} fusion(bf16[800,4096]{1,0:T(8,128)(2,1)} %get-tuple-element.249, f32[800,1024]{1,0:T(8,128)} %reshape.303, f32[800]{0:T(1024)S(1)} %copy-done.46), kind=kOutput, calls=%fused_computation.180 | convolution fusion | flops 6712524800 | bytes 26610816 | tf_op jit(solution)/shard_map/dot_general | solution.py:52
  458.9 39.8 %psum.42 = f32[]{:T(128)} all-reduce(f32[]{:T(128)} %get-tuple-element.231), channel_id=1, replica_groups=mesh['dp'=8,'fsdp'=4] {'dp','fsdp'}, use_global_device_ids=true, to_apply=%region_12.13 | all-reduce | flops 1 | bytes 8 | tf_op jit(solution)/shard_map/psum | solution.py:105
  506.6 12.2 multiply_reduce_fusion.3
  520.1 7.5 fusion.1
  527.6 13.0 %add_convert_fusion = bf16[800,1024]{1,0:T(8,128)(2,1)} fusion(f32[800,1024]{1,0:T(8,128)S(1)} %copy-done.8, f32[1024]{0:T(1024)S(1)} %bitcast.113, bf16[800,4096]{1,0:T(8,128)(2,1)} %get-tuple-element.249, bf16[4096,1024]{1,0:T(8,128)(2,1)} %all-gather.11.cloned.1.call-done), kind=kOutput, calls=%fused_computation.64 | convolution fusion | flops 6713344000 | bytes 19861504 | tf_op jit(solution)/shard_map/dot_general | solution.py:157
  543.4 100.9 %reduce-scatter.5.cloned.1.call-done = f32[32,3072]{1,0:T(8,128)} async-done(((f32[1024,3072]{1,0:T(8,128)}), f32[32,3072]{1,0:T(8,128)}) %reduce-scatter.5.cloned.1.call-update) | async-done | bytes 393232 | tf_op jit(solution)/shard_map/reduce_scatter | solution.py:223
  644.3 3.0 multiply_reduce_fusion.18
  647.3 181.5 %reduce-scatter.9.cloned.1.call-done = f32[32,4096]{1,0:T(8,128)} async-done(((f32[1024,4096]{1,0:T(8,128)}), f32[32,4096]{1,0:T(8,128)}) %reduce-scatter.9.cloned.1.call-update) | async-done | bytes 524304 | tf_op jit(solution)/shard_map/reduce_scatter | solution.py:225
  828.8 3.1 multiply_reduce_fusion.15
  832.0 183.8 %reduce-scatter.11.cloned.1.call-done = f32[128,1024]{1,0:T(8,128)} async-done(((f32[4096,1024]{1,0:T(8,128)}), f32[128,1024]{1,0:T(8,128)}) %reduce-scatter.11.cloned.1.call-update) | async-done | bytes 524304 | tf_op jit(solution)/shard_map/reduce_scatter | solution.py:226
  1015.8 3.2 multiply_reduce_fusion.14
  1019.0 3.2 pad_maximum_fusion.1
  1022.2 5.4 add_divide_fusion
  1033.3 3.6 copy.156
  1036.9 109.9 %all-reduce.4.cloned.1.call-done = (f32[4]{0:T(128)}, f32[12,1024]{1,0:T(8,128)}, f32[361,32]{0,1:T(8,128)}) async-done(((f32[4]{0:T(128)}, f32[12,1024]{1,0:T(8,128)}, f32[361,32]{0,1:T(8,128)}), (f32[4]{0:T(128)}, f32[12,1024]{1,0:T(8,128)}, f32[361,32]{0,1:T(8,128)})) %all-reduce.4.cloned.1.call-update) | async-done | bytes 95392 | tf_op jit(solution)/shard_map/psum | solution.py:253
  1160.3 3.1 multiply_reduce_fusion.16
  1165.8 3.4 multiply_reduce_fusion.11
  1175.3 41.1 %all-reduce = (f32[4]{0:T(128)S(1)}, f32[4]{0:T(128)S(1)}) all-reduce(f32[4]{0:T(128)S(1)} %pad_maximum_fusion.2, f32[4]{0:T(128)S(1)} %pad_maximum_fusion.3), channel_id=1, replica_groups=mesh['dp'=8,'fsdp'=4] {'dp','fsdp'}, use_global_device_ids=true, to_apply=%region_41.42 | all-reduce | flops 8 | bytes 64 | tf_op jit(solution)/shard_map/psum | solution.py:253
  (202 shorter events, 105.9 us)
Async XLA Ops:
  7.2 11.7 copy-start.1
  7.2 76.6 %all-gather.5.cloned.1.call-start = ((), (), s32[]{:S(2)}) async-start(), calls=%async_computation.4 | async-start | bytes 6488064 | tf_op jit(solution)/shard_map/all_gather | solution.py:112
  9.1 136.8 %all-gather.7.cloned.1.call-start = ((), (), s32[]{:S(2)}) async-start(), calls=%async_computation.5 | async-start | bytes 2162688 | tf_op jit(solution)/shard_map/all_gather | solution.py:113
  10.7 211.4 %all-gather.9.cloned.1.call-start = ((), (), s32[]{:S(2)}) async-start(), calls=%async_computation.6 | async-start | bytes 8650752 | tf_op jit(solution)/shard_map/all_gather | solution.py:114
  12.6 289.0 %all-gather.11.cloned.1.call-start = ((), (), s32[]{:S(2)}) async-start(), calls=%async_computation.7 | async-start | bytes 8650752 | tf_op jit(solution)/shard_map/all_gather | solution.py:115
  14.4 526.2 %reduce-scatter.7.cloned.1.call-start = ((), (), s32[]{:S(2)}) async-start(), calls=%async_computation.9 | async-start | bytes 4325376 | tf_op jit(solution)/shard_map/reduce_scatter | solution.py:224
  15.2 7.0 copy-start.38
  18.9 64.9 %copy-start.40 = (f32[1,1024]{1,0:T(1,128)}, f32[1,1024]{1,0:T(1,128)S(1)}, u32[]{:S(2)}) copy-start(f32[1,1024]{1,0:T(1,128)S(1)} %get-tuple-element.230) | copy-start | bytes 12292
  18.9 64.9 %copy-start.48 = (f32[1,1024]{1,0:T(1,128)}, f32[1,1024]{1,0:T(1,128)S(1)}, u32[]{:S(2)}) copy-start(f32[1,1024]{1,0:T(1,128)S(1)} %get-tuple-element.229) | copy-start | bytes 12292
  19.3 64.5 %copy-start.42 = (f32[800]{0:T(1024)}, f32[800]{0:T(1024)S(1)}, u32[]{:S(2)}) copy-start(f32[800]{0:T(1024)S(1)} %div.208) | copy-start | bytes 9604
  19.5 4.4 copy-start.33
  23.9 60.0 %copy-start.44 = (f32[800]{0:T(1024)}, f32[800]{0:T(1024)S(1)}, u32[]{:S(2)}) copy-start(f32[800]{0:T(1024)S(1)} %rsqrt.27) | copy-start | bytes 9604
  35.1 4.0 copy-start.16
  41.8 3.7 copy-start.2
  103.9 14.1 %copy-start.11 = (bf16[8,100,32,32]{1,0,3,2:T(8,128)(2,1)}, bf16[8,100,32,32]{1,0,3,2:T(8,128)(2,1)S(1)}, u32[]{:S(2)}) copy-start(bf16[8,100,32,32]{1,0,3,2:T(8,128)(2,1)S(1)} %reshape.292) | copy-start | bytes 4915204
  137.5 8.4 copy-start.3
  222.1 79.5 %copy-start.9 = (f32[800,1024]{1,0:T(8,128)S(1)}, f32[800,1024]{1,0:T(8,128)}, u32[]{:S(2)}) copy-start(f32[800,1024]{1,0:T(8,128)} %reshape.303) | copy-start | bytes 9830404
  222.1 79.5 %copy-start.46 = (f32[800]{0:T(1024)S(1)}, f32[800]{0:T(1024)}, u32[]{:S(2)}) copy-start(f32[800]{0:T(1024)} %mul.568) | copy-start | bytes 9604
  301.6 16.8 %copy-start.7 = (f32[800,1024]{1,0:T(8,128)S(1)}, f32[800,1024]{1,0:T(8,128)}, u32[]{:S(2)}) copy-start(f32[800,1024]{1,0:T(8,128)} %copy-done.6) | copy-start | bytes 9830404
  301.6 16.8 %copy-start.50 = (bf16[1024,4096]{1,0:T(8,128)(2,1)S(1)}, bf16[1024,4096]{1,0:T(8,128)(2,1)}, u32[]{:S(2)}) copy-start(bf16[1024,4096]{1,0:T(8,128)(2,1)} %all-gather.9.cloned.1.call-done) | copy-start | bytes 25165828
  318.4 11.0 copy-start.10
  330.9 4.4 copy-start.5
  342.9 3.7 copy-start.35
  346.3 298.0 %reduce-scatter.5.cloned.1.call-start = ((), (), s32[]{:S(2)}) async-start(), calls=%async_computation.8 | async-start | bytes 12976128 | tf_op jit(solution)/shard_map/reduce_scatter | solution.py:223
  376.7 11.8 copy-start.13
  388.5 3.8 copy-start
  392.3 8.6 copy-start.12
  413.3 3.2 copy-start.49
  426.7 402.2 %reduce-scatter.9.cloned.1.call-start = ((), (), s32[]{:S(2)}) async-start(), calls=%async_computation.10 | async-start | bytes 17301504 | tf_op jit(solution)/shard_map/reduce_scatter | solution.py:225
  442.7 573.1 %reduce-scatter.11.cloned.1.call-start = ((), (), s32[]{:S(2)}) async-start(), calls=%async_computation.11 | async-start | bytes 17301504 | tf_op jit(solution)/shard_map/reduce_scatter | solution.py:226
  458.9 39.9 %copy-start.39 = (f32[8,100]{1,0:T(8,128)S(1)}, f32[8,100]{1,0:T(8,128)}, u32[]{:S(2)}) copy-start(f32[8,100]{1,0:T(8,128)} %copy-done.38) | copy-start | bytes 9604
  458.9 687.9 %all-reduce.4.cloned.1.call-start = ((), (), s32[]{:S(2)}) async-start(), calls=%async_computation.12 | async-start | bytes 230400 | tf_op jit(solution)/shard_map/psum | solution.py:253
  506.6 13.6 %copy-start.37 = (s32[10000]{0:T(1024)S(1)}, s32[10000]{0:T(1024)}, u32[]{:S(2)}) copy-start(s32[10000]{0:T(1024)} %copy-done.36) | copy-start | bytes 120004
  518.8 8.8 copy-start.47
  520.1 7.5 copy-start.8
  1033.3 124.6 %copy-start.28 = (f32[32,1024]{1,0:T(8,128)S(1)}, f32[32,1024]{1,0:T(8,128)}, u32[]{:S(2)}) copy-start(f32[32,1024]{1,0:T(8,128)} %param.27) | copy-start | bytes 393220
  1036.9 126.6 %copy-start.17 = (f32[128,1024]{1,0:T(8,128)S(1)}, f32[128,1024]{1,0:T(8,128)}, u32[]{:S(2)}) copy-start(f32[128,1024]{1,0:T(8,128)} %param.33) | copy-start | bytes 1572868
  1036.9 126.6 %copy-start.21 = (f32[128,1024]{1,0:T(8,128)S(1)}, f32[128,1024]{1,0:T(8,128)}, u32[]{:S(2)}) copy-start(f32[128,1024]{1,0:T(8,128)} %get-tuple-element.220) | copy-start | bytes 1572868
  1148.9 14.6 %copy-start.32 = (f32[361,32]{0,1:T(8,128)}, f32[361,32]{0,1:T(8,128)S(1)}, u32[]{:S(2)}) copy-start(f32[361,32]{0,1:T(8,128)S(1)} %get-tuple-element.206) | copy-start | bytes 138628
  1154.9 10.9 copy-start.18
  1154.9 10.8 copy-start.20
  1163.5 66.1 %copy-start.19 = (f32[32,3072]{1,0:T(8,128)S(1)}, f32[32,3072]{1,0:T(8,128)}, u32[]{:S(2)}) copy-start(f32[32,3072]{1,0:T(8,128)} %param.24) | copy-start | bytes 1179652
  1165.8 67.1 %copy-start.22 = (f32[128,1024]{1,0:T(8,128)}, f32[128,1024]{1,0:T(8,128)S(1)}, u32[]{:S(2)}) copy-start(f32[128,1024]{1,0:T(8,128)S(1)} %get-tuple-element.203) | copy-start | bytes 1572868
  1165.8 67.1 %copy-start.23 = (f32[128,1024]{1,0:T(8,128)}, f32[128,1024]{1,0:T(8,128)S(1)}, u32[]{:S(2)}) copy-start(f32[128,1024]{1,0:T(8,128)S(1)} %get-tuple-element.204) | copy-start | bytes 1572868
  1169.2 64.8 %copy-start.24 = (f32[32,4096]{1,0:T(8,128)}, f32[32,4096]{1,0:T(8,128)S(1)}, u32[]{:S(2)}) copy-start(f32[32,4096]{1,0:T(8,128)S(1)} %get-tuple-element.201) | copy-start | bytes 1572868
  1169.2 63.7 %copy-start.25 = (f32[32,4096]{1,0:T(8,128)S(1)}, f32[32,4096]{1,0:T(8,128)}, u32[]{:S(2)}) copy-start(f32[32,4096]{1,0:T(8,128)} %get-tuple-element.202) | copy-start | bytes 1572868
  1224.1 9.9 copy-start.30
  1224.1 9.9 copy-start.31
  (12 other events, 26.0 us)
Sparse Core Ops, SparseCore 0:
  11.5 72.2 all-gather.4
  87.3 54.8 all-gather.6
  145.7 76.4 all-gather.8
  225.4 76.1 all-gather.10
  346.4 140.5 reduce-scatter.6
  492.9 151.3 reduce-scatter.4
  646.7 182.1 reduce-scatter.8
  831.2 184.5 reduce-scatter.10
  1023.4 123.3 all-reduce.3
where the time goes:
time: 1250 us; the launch traced here: 1240 us
  waiting for transfers between devices  722 us (58%)
  matrix products  227 us (18%)
  local copies, waits for them, and re-layouts  102 us (8%)
  other arithmetic  84.5 us (7%)
  blocking collectives  80.9 us (6%)
  between operations  24.6 us (2%)
    reduce_scatter x1, waiting for transfers between devices, local(): lax.psum_scatter(grad_shrink, ('dp', 'fsdp'), scatter_dimension=0, tiled=...  184 us
    reduce_scatter x1, waiting for transfers between devices, local(): lax.psum_scatter(grad_expand, ('dp', 'fsdp'), scatter_dimension=0, tiled=...  182 us
    psum x1, waiting for transfers between devices, local(): lax.psum((grad_squares, weight_squares), ('dp', 'fsdp'))  110 us
    reduce_scatter x1, waiting for transfers between devices, local(): lax.psum_scatter(grad_attend, ('dp', 'fsdp'), scatter_dimension=0, tiled=...  101 us
    all_gather x1, waiting for transfers between devices, local(): lax.all_gather(copy_expand, ('dp', 'fsdp'), axis=0, tiled=True)  69.7 us
    dot_general x4, matrix products, inner_product(): lax.dot_general(left, right, (((0,), (0,)), ((), ())), preferred_element_...  46.6 us
    dot_general x4, matrix products, times_transpose(): lax.dot_general(left, right, (((1,), (1,)), ((), ())), preferred_element_...  44.6 us
    psum x1, blocking collectives, local(): lax.psum((grad_squares, weight_squares), ('dp', 'fsdp'))  41.1 us
  transfers between devices with their start and end apart: 9, of which 7 were waited for; matrix products, arithmetic and copies ran while one was open for 26% of the time, Pallas kernels for 0%

commit v1 on v0

--- a/solution.py
+++ b/solution.py
@@ -1,7 +1,15 @@
+import functools
+
 import jax
 import jax.numpy as jnp
 from jax import lax
+from jax.experimental import pallas as pl
+from jax.experimental.pallas import tpu as pltpu
 from jax.sharding import PartitionSpec as P
+
+MESH = pl.DeviceIdType.MESH
+AXES = ("dp", "fsdp")
+VMEM_LIMIT = 60 * 1024 * 1024
 
 HEADS = 32
 WS = 10
@@ -73,7 +81,414 @@
     return (first_new, second_new, update)
 
 
+class Place:
+    def __init__(self, nz, sems):
+        dp = lax.axis_index("dp")
+        fsdp = lax.axis_index("fsdp")
+        self.nz = nz
+        self.z, self.x = dp // 2, dp % 2
+        self.y, self.c = fsdp // 2, fsdp % 2
+        self.sems = sems
+        self.used = 0
+
+    def sem(self):
+        self.used += 1
+        return self.sems.at[self.used - 1]
+
+    def zplus(self, k):
+        return lax.rem(self.z + k, self.nz)
+
+    def to(self, z=None, x=None, y=None, c=None):
+        z = self.z if z is None else z
+        x = self.x if x is None else x
+        y = self.y if y is None else y
+        c = self.c if c is None else c
+        return (z * 2 + x, y * 2 + c)
+
+    def peers(self):
+        found = [self.to(z=self.zplus(k)) for k in range(1, self.nz)]
+        found.append(self.to(x=1 - self.x))
+        found.append(self.to(y=1 - self.y))
+        found.append(self.to(c=1 - self.c))
+        return found
+
+    def greet(self):
+        barrier = pltpu.get_barrier_semaphore()
+        peers = self.peers()
+        for peer in peers:
+            pl.semaphore_signal(barrier, inc=1, device_id=peer, device_id_type=MESH)
+        pl.semaphore_wait(barrier, len(peers))
+
+    def send(self, source, target, device):
+        return pltpu.make_async_remote_copy(
+            src_ref=source,
+            dst_ref=target,
+            send_sem=self.sem(),
+            recv_sem=self.sem(),
+            device_id=device,
+            device_id_type=MESH,
+        )
+
+    def move(self, source, target):
+        return pltpu.make_async_copy(source, target, self.sem())
+
+
+def gather_sems(nz):
+    return 2 * (nz - 1) + 18 * nz + 1
+
+
+def gather_events(place, own, out):
+    nz, z, x, y, c = place.nz, place.z, place.x, place.y, place.c
+    half = own.shape[0] // 2
+    ox, oy, oc = 1 - x, 1 - y, 1 - c
+    xp, yp, cp = place.to(x=ox), place.to(y=oy), place.to(c=oc)
+    zs = [lax.rem(z - k + nz, nz) for k in range(nz)]
+    low, high = pl.ds(0, half), pl.ds(half, half)
+
+    def forward(slot, device, part=None, source=None):
+        if part is not None:
+            slot = slot.at[part]
+        return place.send(slot if source is None else source, slot, device)
+
+    mine = place.move(own, out.at[z, x, y, c])
+    along = [None] + [
+        place.send(own, out.at[z, x, y, c], place.to(z=place.zplus(k))) for k in range(1, nz)
+    ]
+    line = [out.at[zs[k], x, y, c] for k in range(nz)]
+    beside = [out.at[zs[k], ox, y, c] for k in range(nz)]
+    across = [out.at[zs[k], x, oy, c] for k in range(nz)]
+    corner = [out.at[zs[k], ox, oy, c] for k in range(nz)]
+    first = lambda k: own if k == 0 else None
+    x_full = [forward(line[k], xp, source=first(k)) for k in range(nz)]
+    y_full = [forward(line[k], yp, source=first(k)) for k in range(nz)]
+    c_line = [forward(line[k], cp, source=first(k)) for k in range(nz)]
+    x_half = [forward(beside[k], yp, low) for k in range(nz)]
+    y_half = [forward(across[k], xp, high) for k in range(nz)]
+    c_beside = [forward(beside[k], cp) for k in range(nz)]
+    c_across = [forward(across[k], cp) for k in range(nz)]
+    c_low = [forward(corner[k], cp, low) for k in range(nz)]
+    c_high = [forward(corner[k], cp, high) for k in range(nz)]
+
+    def begin():
+        for k in range(1, nz):
+            along[k].start()
+        x_full[0].start()
+        y_full[0].start()
+        c_line[0].start()
+        mine.start()
+
+    def on_line(k):
+        along[k].wait_recv()
+        x_full[k].start()
+        y_full[k].start()
+        c_line[k].start()
+
+    def on_beside(k):
+        x_full[k].wait_recv()
+        x_half[k].start()
+        c_beside[k].start()
+
+    def on_across(k):
+        y_full[k].wait_recv()
+        y_half[k].start()
+        c_across[k].start()
+
+    def on_corner(k):
+        x_half[k].wait_recv()
+        c_low[k].start()
+        y_half[k].wait_recv()
+        c_high[k].start()
+
+    def finish():
+        mine.wait()
+        for copies in (c_line, c_beside, c_across, c_low, c_high):
+            for copy in copies:
+                copy.wait_recv()
+        for copies in (along[1:], x_full, y_full, c_line, x_half, y_half, c_beside, c_across, c_low, c_high):
+            for copy in copies:
+                copy.wait_send()
+
+    events = [begin]
+    for k in range(nz + 2):
+        if 1 <= k < nz:
+            events.append(functools.partial(on_line, k))
+        if 1 <= k <= nz:
+            events.append(functools.partial(on_beside, k - 1))
+            events.append(functools.partial(on_across, k - 1))
+        if 2 <= k:
+            events.append(functools.partial(on_corner, k - 2))
+    events.append(finish)
+    return events
+
+
+def scatter_sems(nz):
+    return 4 * nz + 8 * nz + 8 * nz + 2 * (nz - 1)
+
+
+def scatter_scratch(nz, rows, columns):
+    shape = lambda *lead: pltpu.VMEM(lead + (columns,), jnp.bfloat16)
+    return [
+        shape(nz, 2, 2, rows),
+        shape(nz, 2, 2, rows),
+        shape(nz, rows // 2),
+        shape(nz, rows // 2),
+        shape(nz, rows),
+        shape(nz, rows),
+        shape(max(nz - 1, 1), rows),
+    ]
+
+
+def scatter_events(place, grads, total, scratch):
+    nz, z, x, y, c = place.nz, place.z, place.x, place.y, place.c
+    held, twin, corner_low, corner_high, from_x, from_y, from_z = scratch
+    rows = total.shape[0]
+    half = rows // 2
+    ox, oy, oc = 1 - x, 1 - y, 1 - c
+    xp, yp, cp = place.to(x=ox), place.to(y=oy), place.to(c=oc)
+    order = list(range(1, nz)) + [0]
+    zs = [place.zplus(k) for k in range(nz)]
+    cell = {(0, 0): (x, y), (1, 0): (ox, y), (0, 1): (x, oy), (1, 1): (ox, oy)}
+    quads = [(1, 1), (1, 0), (0, 1), (0, 0)]
+    loads, twins = {}, {}
+    for k in order:
+        for q in quads:
+            cx, cy = cell[q]
+            loads[q, k] = place.move(grads.at[zs[k], cx, cy, c], held.at[zs[k], q[0], q[1]])
+            twins[q, k] = place.send(grads.at[zs[k], cx, cy, oc], twin.at[zs[k], q[0], q[1]], cp)
+    low, high = pl.ds(0, half), pl.ds(half, half)
+    out_low = [place.send(held.at[zs[k], 1, 1, low], corner_low.at[zs[k]], xp) for k in range(nz)]
+    out_high = [place.send(held.at[zs[k], 1, 1, high], corner_high.at[zs[k]], yp) for k in range(nz)]
+    out_x = [place.send(held.at[zs[k], 1, 0], from_x.at[zs[k]], xp) for k in range(nz)]
+    out_y = [place.send(held.at[zs[k], 0, 1], from_y.at[zs[k]], yp) for k in range(nz)]
+    out_z = [None] + [
+        place.send(held.at[zs[k], 0, 0], from_z.at[k - 1], place.to(z=zs[k])) for k in range(1, nz)
+    ]
+
+    def summed(target, parts):
+        lo, n = target[1], target[2]
+
+        def step(i, carry):
+            at = pl.multiple_of(i * 16, 16)
+            value = parts[0](at)
+            for part in parts[1:]:
+                value = value + part(at)
+            target[0](lo + at, value)
+            return carry
+
+        lax.fori_loop(0, n // 16, step, 0)
+
+    def read(ref, *index, lo=0):
+        return lambda at: ref[index + (pl.ds(lo + at, 16),)].astype(jnp.float32)
+
+    def write(ref, *index):
+        def store(at, value):
+            ref[index + (pl.ds(at, 16),)] = value.astype(ref.dtype)
+
+        return store
+
+    def begin():
+        for k in order:
+            for q in quads:
+                twins[q, k].start()
+                loads[q, k].start()
+
+    def arrived(q, k):
+        loads[q, k].wait()
+        twins[q, k].wait_recv()
+
+    def on_corner(k):
+        arrived((1, 1), k)
+        at = (zs[k], 1, 1)
+        summed((write(held, *at), 0, rows), [read(held, *at), read(twin, *at)])
+        out_low[k].start()
+        out_high[k].start()
+
+    def on_beside(k):
+        arrived((1, 0), k)
+        at = (zs[k], 1, 0)
+        summed((write(held, *at), 0, half), [read(held, *at), read(twin, *at)])
+        out_high[k].wait_recv()
+        summed(
+            (write(held, *at), half, half),
+            [read(held, *at, lo=half), read(twin, *at, lo=half), read(corner_high, zs[k])],
+        )
+        out_x[k].start()
+
+    def on_across(k):
+        arrived((0, 1), k)
+        at = (zs[k], 0, 1)
+        summed((write(held, *at), half, half), [read(held, *at, lo=half), read(twin, *at, lo=half)])
+        out_low[k].wait_recv()
+        summed(
+            (write(held, *at), 0, half),
+            [read(held, *at), read(twin, *at), read(corner_low, zs[k])],
+        )
+        out_y[k].start()
+
+    def on_line(k):
+        arrived((0, 0), k)
+        out_x[k].wait_recv()
+        out_y[k].wait_recv()
+        at = (zs[k], 0, 0)
+        parts = [read(held, *at), read(twin, *at), read(from_x, zs[k]), read(from_y, zs[k])]
+        if k:
+            summed((write(held, *at), 0, rows), parts)
+            out_z[k].start()
+        else:
+            for j in range(1, nz):
+                out_z[j].wait_recv()
+            parts = parts + [read(from_z, j) for j in range(nz - 1)]
+            summed((write(total), 0, rows), parts)
+
+    def finish():
+        for copies in (list(twins.values()), out_low, out_high, out_x, out_y, out_z[1:]):
+            for copy in copies:
+                copy.wait_send()
+
+    events = [begin]
+    for i in range(nz + 2):
+        if i < nz:
+            events.append(functools.partial(on_corner, order[i]))
+        if 1 <= i <= nz:
+            events.append(functools.partial(on_beside, order[i - 1]))
+            events.append(functools.partial(on_across, order[i - 1]))
+        if 2 <= i:
+            events.append(functools.partial(on_line, order[i - 2]))
+    events.append(finish)
+    return events
+
+
+def interleave(lists):
+    merged = []
+    for i in range(max(len(events) for events in lists)):
+        for events in lists:
+            if i < len(events):
+                merged.append(events[i])
+    return merged
+
+
+def gather_kernel(nz, count, *refs):
+    owns, outs, lows = refs[:count], refs[count : 2 * count], refs[2 * count : 3 * count]
+    place = Place(nz, refs[-1])
+    for own, low in zip(owns, lows):
+        low[...] = own[...].astype(low.dtype)
+    place.greet()
+    for event in interleave([gather_events(place, low, out) for low, out in zip(lows, outs)]):
+        event()
+
+
+def gather_all(nz, shards, collective):
+    count = len(shards)
+    return pl.pallas_call(
+        functools.partial(gather_kernel, nz, count),
+        name="gather_weights",
+        out_shape=[jax.ShapeDtypeStruct((nz, 2, 2, 2) + s.shape, jnp.bfloat16) for s in shards],
+        in_specs=[pl.BlockSpec(memory_space=pltpu.VMEM)] * count,
+        out_specs=[pl.BlockSpec(memory_space=pl.ANY)] * count,
+        scratch_shapes=[pltpu.VMEM(s.shape, jnp.bfloat16) for s in shards]
+        + [pltpu.SemaphoreType.DMA((gather_sems(nz) * count,))],
+        compiler_params=pltpu.CompilerParams(
+            collective_id=collective, has_side_effects=True, vmem_limit_bytes=VMEM_LIMIT
+        ),
+    )(*shards)
+
+
+def scatter_kernel(nz, count, *refs):
+    grads, totals = refs[:count], refs[count : 2 * count]
+    place = Place(nz, refs[-1])
+    place.greet()
+    lists = []
+    for i in range(count):
+        scratch = refs[2 * count + 7 * i : 2 * count + 7 * (i + 1)]
+        lists.append(scatter_events(place, grads[i], totals[i], scratch))
+    for event in interleave(lists):
+        event()
+
+
+def scatter_all(nz, grads, collective, name):
+    count = len(grads)
+    scratch = []
+    for g in grads:
+        scratch += scatter_scratch(nz, g.shape[4], g.shape[5])
+    return pl.pallas_call(
+        functools.partial(scatter_kernel, nz, count),
+        name=name,
+        out_shape=[jax.ShapeDtypeStruct(g.shape[4:], jnp.float32) for g in grads],
+        in_specs=[pl.BlockSpec(memory_space=pl.ANY)] * count,
+        out_specs=[pl.BlockSpec(memory_space=pltpu.VMEM)] * count,
+        scratch_shapes=scratch + [pltpu.SemaphoreType.DMA((scatter_sems(nz) * count,))],
+        compiler_params=pltpu.CompilerParams(
+            collective_id=collective, has_side_effects=True, vmem_limit_bytes=VMEM_LIMIT
+        ),
+    )(*grads)
+
+
+def spread_kernel(ndp, nfs, own, out, send_sems, recv_sems, sem):
+    n = ndp * nfs
+    dp, fsdp = lax.axis_index("dp"), lax.axis_index("fsdp")
+    me = dp * nfs + fsdp
+    barrier = pltpu.get_barrier_semaphore()
+
+    def peer(k):
+        other = lax.rem(me + k, n)
+        return (other // nfs, lax.rem(other, nfs))
+
+    def hello(k, carry):
+        pl.semaphore_signal(barrier, inc=1, device_id=peer(k), device_id_type=MESH)
+        return carry
+
+    lax.fori_loop(1, n, hello, 0)
+    pl.semaphore_wait(barrier, n - 1)
+
+    def copy(k):
+        return pltpu.make_async_remote_copy(
+            src_ref=own,
+            dst_ref=out.at[me],
+            send_sem=send_sems.at[k],
+            recv_sem=recv_sems.at[k],
+            device_id=peer(k),
+            device_id_type=MESH,
+        )
+
+    def start(k, carry):
+        copy(k).start()
+        return carry
+
+    def done(k, carry):
+        copy(k).wait()
+        return carry
+
+    lax.fori_loop(1, n, start, 0)
+    mine = pltpu.make_async_copy(own, out.at[me], sem)
+    mine.start()
+    mine.wait()
+    lax.fori_loop(1, n, done, 0)
+
+
+def spread(ndp, nfs, block, collective, name):
+    n = ndp * nfs
+    return pl.pallas_call(
+        functools.partial(spread_kernel, ndp, nfs),
+        name=name,
+        out_shape=jax.ShapeDtypeStruct((n,) + block.shape, block.dtype),
+        in_specs=[pl.BlockSpec(memory_space=pltpu.VMEM)],
+        out_specs=pl.BlockSpec(memory_space=pltpu.VMEM),
+        scratch_shapes=[
+            pltpu.SemaphoreType.DMA((n,)),
+            pltpu.SemaphoreType.DMA((n,)),
+            pltpu.SemaphoreType.DMA(()),
+        ],
+        compiler_params=pltpu.CompilerParams(collective_id=collective, has_side_effects=True),
+    )(block)
+
+
+def as_rows(values, rows):
+    return jnp.pad(values, (0, rows * 128 - values.shape[0])).reshape(rows, 128)
+
+
 def local(
+    ndp,
+    nfs,
     patches,
     cotangent,
     pad_mask,
@@ -102,25 +517,28 @@
     scale = head_dim ** (-0.5)
     keep = pad_mask.astype(jnp.float32)
     local_count = jnp.sum(keep)
-    total = lax.psum(local_count, ("dp", "fsdp"))
+    devices = ndp * nfs
+    nz = ndp // 2
+    shard_rows = min(attend_weight.shape[0], shrink_weight.shape[0])
+    direct = ndp % 2 == 0 and nfs == 4 and shard_rows % 32 == 0
+    counts = spread(ndp, nfs, as_rows(local_count[None], 8), 0, "spread_count")
+    total = jnp.sum(counts[:, 0, 0])
     masters = (attend_weight, output_weight, expand_weight, shrink_weight)
-    copy_attend = attend_weight.astype(jnp.bfloat16)
-    copy_output = output_weight.astype(jnp.bfloat16)
-    copy_expand = expand_weight.astype(jnp.bfloat16)
-    copy_shrink = shrink_weight.astype(jnp.bfloat16)
-    gathered = (
-        lax.all_gather(copy_attend, ("dp", "fsdp"), axis=0, tiled=True),
-        lax.all_gather(copy_output, ("dp", "fsdp"), axis=0, tiled=True),
-        lax.all_gather(copy_expand, ("dp", "fsdp"), axis=0, tiled=True),
-        lax.all_gather(copy_shrink, ("dp", "fsdp"), axis=0, tiled=True),
-    )
+    if direct:
+        gathered = [
+            w.reshape(-1, w.shape[-1]) for w in gather_all(nz, masters, 1)
+        ]
+    else:
+        gathered = [
+            lax.all_gather(m.astype(jnp.bfloat16), AXES, axis=0, tiled=True) for m in masters
+        ]
     w_attend, w_output, w_expand, w_shrink = gathered
     gain_one, shift_one = (vector_params[0], vector_params[1])
     query_bias, value_bias, output_bias = (vector_params[2], vector_params[3], vector_params[4])
     gain_two, shift_two, shrink_bias = (vector_params[5], vector_params[6], vector_params[7])
     expand_bias = vector_params[8:].reshape(-1)
     source = patches.reshape(rows, width).astype(jnp.float32)
-    normed_one, spread_one = normalize(source)
+    normed_one, rstd_one = normalize(source)
     hidden_one = (normed_one * gain_one + shift_one).astype(jnp.bfloat16)
     joint = jnp.dot(hidden_one, w_attend, preferred_element_type=jnp.float32)
     query = (
@@ -150,18 +568,12 @@
     attended = jnp.einsum("whij,wjhd->wihd", probs_low, values, preferred_element_type=jnp.float32)
     attended = attended.reshape(rows, width).astype(jnp.bfloat16)
     middle = source + jnp.dot(attended, w_output, preferred_element_type=jnp.float32) + output_bias
-    normed_two, spread_two = normalize(middle)
+    normed_two, rstd_two = normalize(middle)
     hidden_two = (normed_two * gain_two + shift_two).astype(jnp.bfloat16)
     before = jnp.dot(hidden_two, w_expand, preferred_element_type=jnp.float32) + expand_bias
     activated = jax.nn.gelu(before, approximate=False).astype(jnp.bfloat16)
     result = middle + jnp.dot(activated, w_shrink, preferred_element_type=jnp.float32) + shrink_bias
     block_out = result.astype(jnp.bfloat16).reshape(windows, cells, width)
-    w_attend, w_output, w_expand, w_shrink = (
-        lax.all_gather(copy_attend, ("dp", "fsdp"), axis=0, tiled=True),
-        lax.all_gather(copy_output, ("dp", "fsdp"), axis=0, tiled=True),
-        lax.all_gather(copy_expand, ("dp", "fsdp"), axis=0, tiled=True),
-        lax.all_gather(copy_shrink, ("dp", "fsdp"), axis=0, tiled=True),
-    )
     upstream = cotangent.reshape(rows, width).astype(jnp.float32) * keep.reshape(rows, 1)
     upstream_low = upstream.astype(jnp.bfloat16)
     grad_shrink = inner_product(activated, upstream_low)
@@ -173,7 +585,7 @@
     grad_hidden_two = times_transpose(grad_before, w_expand)
     grad_gain_two = jnp.sum(grad_hidden_two * normed_two, axis=0)
     grad_shift_two = jnp.sum(grad_hidden_two, axis=0)
-    grad_middle = upstream + norm_back(grad_hidden_two, normed_two, spread_two, gain_two)
+    grad_middle = upstream + norm_back(grad_hidden_two, normed_two, rstd_two, gain_two)
     grad_branch = grad_middle.astype(jnp.bfloat16)
     grad_output = inner_product(attended, grad_branch)
     grad_output_bias = jnp.sum(grad_branch.astype(jnp.float32), axis=0)
@@ -218,13 +630,7 @@
     grad_hidden_one = times_transpose(grad_joint, w_attend)
     grad_gain_one = jnp.sum(grad_hidden_one * normed_one, axis=0)
     grad_shift_one = jnp.sum(grad_hidden_one, axis=0)
-    grad_source = grad_middle + norm_back(grad_hidden_one, normed_one, spread_one, gain_one)
-    owned = (
-        lax.psum_scatter(grad_attend, ("dp", "fsdp"), scatter_dimension=0, tiled=True),
-        lax.psum_scatter(grad_output, ("dp", "fsdp"), scatter_dimension=0, tiled=True),
-        lax.psum_scatter(grad_expand, ("dp", "fsdp"), scatter_dimension=0, tiled=True),
-        lax.psum_scatter(grad_shrink, ("dp", "fsdp"), scatter_dimension=0, tiled=True),
-    )
+    grad_source = grad_middle + norm_back(grad_hidden_one, normed_one, rstd_one, gain_one)
     vector_local = jnp.concatenate(
         [
             jnp.stack(
@@ -243,14 +649,36 @@
         ],
         axis=0,
     )
-    vector_sum, table_sum = lax.psum((vector_local, grad_table), ("dp", "fsdp"))
+    table_rows, table_heads = grad_table.shape
+    small = jnp.concatenate([vector_local.reshape(-1), grad_table.reshape(-1)])
+    block_rows = -(-small.shape[0] // (devices * 128))
+    if direct:
+        block_rows = -(-block_rows // 32) * 32
+        grads = [
+            g.astype(jnp.bfloat16).reshape(nz, 2, 2, 2, -1, g.shape[-1])
+            for g in (grad_attend, grad_output, grad_expand, grad_shrink)
+        ]
+        packed = as_rows(small, devices * block_rows).astype(jnp.bfloat16)
+        grads.append(packed.reshape(nz, 2, 2, 2, block_rows, 128))
+        *owned, small_owned = scatter_all(nz, grads, 2, "scatter_grads")
+    else:
+        owned = [
+            lax.psum_scatter(g, AXES, scatter_dimension=0, tiled=True)
+            for g in (grad_attend, grad_output, grad_expand, grad_shrink)
+        ]
+        packed = as_rows(small, devices * block_rows)
+        small_owned = lax.psum_scatter(packed, AXES, scatter_dimension=0, tiled=True)
     input_grad = (grad_source / total).reshape(windows, cells, width)
     matrix_grads = tuple((g / total for g in owned))
-    vector_grad = vector_sum / total
-    table_grad = table_sum / total
     grad_squares = jnp.stack([jnp.sum(g * g) for g in matrix_grads])
     weight_squares = jnp.stack([jnp.sum(m * m) for m in masters])
-    grad_total, weight_total = lax.psum((grad_squares, weight_squares), ("dp", "fsdp"))
+    sums = as_rows(jnp.concatenate([grad_squares, weight_squares]), 8)
+    spread_one = spread(ndp, nfs, jnp.concatenate([sums, small_owned]), 3, "spread_small")
+    totals = jnp.sum(spread_one[:, 0, :8], axis=0)
+    grad_total, weight_total = totals[:4], totals[4:]
+    small_sum = spread_one[:, 8:].reshape(-1) / total
+    vector_grad = small_sum[: vector_local.size].reshape(vector_local.shape)
+    table_grad = small_sum[vector_local.size : small.shape[0]].reshape(table_rows, table_heads)
     clip_norm = jnp.sqrt(
         jnp.sum(grad_total) + jnp.sum(vector_grad * vector_grad) + jnp.sum(table_grad * table_grad)
     )
@@ -261,7 +689,8 @@
         moments(matrix_grads[k], firsts[k], seconds[k], masters[k], factor) for k in range(4)
     ]
     update_squares = jnp.stack([jnp.sum(s[2] * s[2]) for s in sectioned])
-    update_total = lax.psum(update_squares, ("dp", "fsdp"))
+    spread_two = spread(ndp, nfs, as_rows(update_squares, 8), 4, "spread_updates")
+    update_total = jnp.sum(spread_two[:, 0, :4], axis=0)
     weight_norms = jnp.sqrt(weight_total)
     update_norms = jnp.sqrt(update_total)
     matrix_outs = []
@@ -380,4 +809,5 @@
         P(),
         P(),
     )
-    return jax.shard_map(local, mesh=mesh, in_specs=in_specs, out_specs=out_specs, check_vma=False)
+    sizes = (mesh.shape["dp"], mesh.shape["fsdp"])
+    return jax.shard_map(functools.partial(local, *sizes), mesh=mesh, in_specs=in_specs, out_specs=out_specs, check_vma=False)

time: 1250 us -> 728 us (0.58)
  waiting for transfers between devices: 722 us -> 0 us
  Pallas kernels: 0 us -> 311 us
  blocking collectives: 80.9 us -> 0 us
  matrix products: 227 us -> 205 us
  local copies, waits for them, and re-layouts: 102 us -> 117 us
  between operations: 24.6 us -> 11.8 us
    reduce_scatter x4 -> x0, waiting for transfers between devices: 466 us -> none  [the longest x1 184 us: local(): lax.psum_scatter(grad_shrink, ('dp', 'fsdp'), scatter_dimension=0, tiled=...]
    pallas_call x0 -> x5, Pallas kernels: none -> 311 us  [the longest x1 127 us: gather_all(): pl.pallas_call(functools.partial(gather_kernel, nz, count), name='gather_...]
    all_gather x4 -> x0, waiting for transfers between devices: 145 us -> none  [the longest x1 69.7 us: local(): lax.all_gather(copy_expand, ('dp', 'fsdp'), axis=0, tiled=True)]
    psum x1 -> x0, waiting for transfers between devices: 110 us -> none  [local(): lax.psum((grad_squares, weight_squares), ('dp', 'fsdp'))]
    psum x2 -> x0, blocking collectives: 80.9 us -> none  [the longest x1 41.1 us: local(): lax.psum((grad_squares, weight_squares), ('dp', 'fsdp'))]
  transfers between devices with their start and end apart: 9 -> 0, of which waited for: 7 -> 0; matrix products, arithmetic and copies ran while one was open for 26% -> 0% of each run, Pallas kernels for 0% -> 0%
where the time goes in v1:
time: 728 us; the launch traced here: 717 us
  Pallas kernels  311 us (43%)
  matrix products  205 us (28%)
  local copies, waits for them, and re-layouts  117 us (16%)
  other arithmetic  72.6 us (10%)
  between operations  11.8 us (2%)
    pallas_call x1, Pallas kernels, gather_all(): pl.pallas_call(functools.partial(gather_kernel, nz, count), name='gather_...  127 us
    pallas_call x1, Pallas kernels, scatter_all(): pl.pallas_call(functools.partial(scatter_kernel, nz, count), name=name, o...  124 us
    pallas_call x3, Pallas kernels, spread(): pl.pallas_call(functools.partial(spread_kernel, ndp, nfs), name=name, out...  59.4 us
    dot_general x4, matrix products, times_transpose(): lax.dot_general(left, right, (((1,), (1,)), ((), ())), preferred_element_...  46.7 us
    dot_general x4, matrix products, inner_product(): lax.dot_general(left, right, (((0,), (0,)), ((), ())), preferred_element_...  39 us
    dot_general x1, matrix products, local(): jnp.dot(hidden_two, w_expand, preferred_element_type=jnp.float32)  37.2 us
    unnamed x169, local copies, waits for them, and re-layouts  20.6 us

profile of v1, /device:TPU:0, one launch (start us, length us, event | category | flops | bytes accessed | tf_op | source)
XLA Modules:
  0.0 717.0 jit_solution(13105434681831764189)
XLA Ops:
  2.4 4.1 copy.151
  6.5 3.5 reshape.409
  13.8 127.2 %gather_weights.1 = (bf16[4,2,2,2,32,3072]{5,4,3,2,1,0:T(8,128)(2,1)}, bf16[4,2,2,2,32,1024]{5,4,3,2,1,0:T(8,128)(2,1)}, bf16[4,2,2,2,32,4096]{5,4,3,2,1,0:T(8,128)(2,1)}, bf16[4,2,2,2,128,1024]{5,4,3,2,1,0:T(8,128)(2,1)}) custom-call(f32[32,3072]{1,0:T(8,128)} %refs_0_.1, f32[32,1024]{1,0:T(8,128)} %refs_1_.1, f32[32,4096]{1,0:T(8,128)} %refs_2_.1, ...), custom_call_target="tpu_custom_call" | custom-call | tf_op jit(solution)/shard_map/gather_weights/pallas_call | solution.py:382
  140.9 7.3 %fusion.98 = f32[800,3072]{1,0:T(8,128)S(1)} fusion(bf16[800,1024]{1,0:T(8,128)(2,1)S(1)} %convert_element_type.159, bf16[1024,3072]{1,0:T(8,128)(2,1)} %bitcast.140), kind=kOutput, calls=%fused_computation.214 | convolution fusion | flops 5033164800 | bytes 17760256 | tf_op jit(solution)/shard_map/dot_general | solution.py:543
  154.2 3.4 reshape.385
  158.4 9.7 %fusion.2 = f32[10000,32]{0,1:T(8,128)S(1)} fusion(f32[361,32]{0,1:T(8,128)S(1)} %copy-done.42, s32[10000]{0:T(1024)S(1)} %add.304), kind=kOutput, calls=%fused_computation.5 | convolution fusion | flops 1389849984 | bytes 1366208 | tf_op jit(solution)/shard_map/dot_general | solution.py:560
  175.4 4.2 reshape.387
  179.6 4.2 copy.158
  183.8 5.0 reshape.386
  188.9 11.2 %fusion.89 = (f32[8,32,100]{2,1,0:T(8,128)S(1)}, f32[8,32,100,100]{2,3,1,0:T(8,128)}) fusion(f32[8,100]{1,0:T(8,128)S(1)} %get-tuple-element.239, f32[32,100,100]{1,2,0:T(8,128)} %copy.162, bf16[8,100,32,32]{1,0,3,2:T(8,128)(2,1)S(1)} %reshape.387, bf16[8,100,32,32]{1,0,3,2:T(8,128)(2,1)} %reshape.386), kind=kOutput, calls=%fused_computation.209 | convolution fusion | flops 176640096 | bytes 14902400 | tf_op jit(solution)/shard_map/sub | solution.py:566
  200.7 7.5 %convert_bitcast_fusion.1 = bf16[8,100,32,32]{1,3,2,0:T(8,128)(2,1)S(1)} fusion(bf16[8,100,32,32]{1,0,3,2:T(8,128)(2,1)} %reshape.385, f32[8,32,100,100]{2,3,1,0:T(8,128)} %get-tuple-element.254, f32[8,32,100]{2,1,0:T(8,128)S(1)} %get-tuple-element.253), kind=kOutput, calls=%fused_computation.78 | convolution fusion | flops 169779200 | bytes 13619200 | tf_op jit(solution)/shard_map/whij,wjhd->wihd/dot_general | solution.py:568
  208.2 3.8 copy.165
  211.9 4.8 convert_element_type.166
  216.8 4.5 fusion.94
  222.6 37.2 %fusion.5 = (bf16[800,4096]{1,0:T(8,128)(2,1)S(1)}, f32[800,4096]{1,0:T(8,128)}) fusion(f32[4096]{0:T(1024)S(1)} %bitcast.128, bf16[1024,4096]{1,0:T(8,128)(2,1)S(1)} %bitcast.137, f32[800,1024]{1,0:T(8,128)S(1)} %get-tuple-element.256, f32[1024]{0:T(1024)S(1)} %bitcast.130, f32[1024]{0:T(1024)S(1)} %bitcast.120, f32[800]{0:T(1024)S(1)} %add_rsqrt_fusion, ...), kind=kOutput, calls=%fused_computation.13 | convolution fusion | flops 6931251200 | bytes 31357184 | tf_op jit(solution)/shard_map/dot_general | solution.py:573
  262.5 8.2 %add_convert_fusion.1 = bf16[800,1024]{1,0:T(8,128)(2,1)} fusion(f32[800,1024]{1,0:T(8,128)S(1)} %get-tuple-element.256, f32[1024]{0:T(1024)S(1)} %bitcast.132, bf16[800,4096]{1,0:T(8,128)(2,1)S(1)} %get-tuple-element.260, bf16[4096,1024]{1,0:T(8,128)(2,1)S(1)} %bitcast.139), kind=kOutput, calls=%fused_computation.64 | convolution fusion | flops 6713344000 | bytes 19861504 | tf_op jit(solution)/shard_map/dot_general | solution.py:575
  276.9 14.9 %fusion.97 = (bf16[4096]{0:T(1024)(128)(2,1)}, bf16[800,4096]{1,0:T(8,128)(2,1)S(1)}) fusion(f32[800,4096]{1,0:T(8,128)} %get-tuple-element.261, f32[4096]{0:T(1024)S(1)} %bitcast.129, bf16[800,1024]{1,0:T(8,128)(2,1)S(1)} %convert_element_type.174, bf16[4096,1024]{1,0:T(8,128)(2,1)} %bitcast.138), kind=kOutput, calls=%fused_computation.213 | convolution fusion | flops 6750203904 | bytes 29712384 | tf_op jit(solution)/shard_map/dot_general | solution.py:66
  291.8 14.4 %multiply_reduce_fusion.1 = (bf16[1024]{0:T(1024)(128)(2,1)S(1)}, f32[800]{0:T(1024)S(1)}, f32[800]{0:T(1024)S(1)}, bf16[1024]{0:T(1024)(128)(2,1)S(1)}, f32[800,1024]{1,0:T(8,128)}) fusion(f32[800,1024]{1,0:T(8,128)S(1)} %copy-done.6, f32[800]{0:T(1024)S(1)} %add_rsqrt_fusion, f32[800]{0:T(1024)S(1)} %broadcast_multiply_fusion.4, f32[1024]{0:T(1024)S(1)} %bitcast.121, ...), kind=kOutput, calls=%fused_computation.56 | convolution fusion | flops 6718255104 | bytes 21516800 | tf_op jit(solution)/shard_map/dot_general | solution.py:66
  309.3 4.6 convert_reduce_fusion.2
  314.1 5.7 convolution_convert_fusion.4
  319.7 3.7 copy.169
  323.5 5.2 reshape.393
  328.6 10.4 %multiply_reduce_fusion = (f32[8,32,100]{2,1,0:T(8,128)S(1)}, f32[8,32,100,100]{2,3,1,0:T(8,128)}) fusion(f32[8,32,100,100]{2,3,1,0:T(8,128)} %get-tuple-element.254, f32[8,32,100]{2,1,0:T(8,128)S(1)} %copy-done.47, bf16[8,100,32,32]{1,0,3,2:T(8,128)(2,1)S(1)} %copy-done.29, bf16[8,100,32,32]{1,0,3,2:T(8,128)(2,1)} %reshape.393), kind=kOutput, calls=%fused_computation.8 | convolution fusion | flops 171494400 | bytes 23961600 | tf_op jit(solution)/shard_map/wihd,wjhd->whij/dot_general | solution.py:597
  339.0 11.7 %convert_reduce_fusion = (f32[32,100,100]{1,2,0:T(8,128)}, bf16[8,32,100,100]{2,3,1,0:T(8,128)(2,1)S(1)}) fusion(f32[8,32,100,100]{2,3,1,0:T(8,128)} %get-tuple-element.259, f32[8,32,100]{2,1,0:T(8,128)S(1)} %get-tuple-element.258, f32[8,32,100,100]{2,3,1,0:T(8,128)} %get-tuple-element.254, f32[8,32,100]{2,1,0:T(8,128)S(1)} %copy-done.47), kind=kLoop, calls=%fused_computation.6 | loop fusion | flops 15040000 | bytes 27084800 | tf_op jit(solution)/shard_map/reduce_sum | solution.py:614
  358.9 3.0 constant_dynamic-update-slice_fusion.2
  362.0 6.6 fusion.48
  373.8 3.1 constant_dynamic-update-slice_fusion.1
  376.9 8.6 %fusion.96 = (bf16[32,32]{1,0:T(8,128)(2,1)S(1)}, bf16[8,100,32,32]{1,3,2,0:T(8,128)(2,1)S(1)}) fusion(f32[8,32,100,100]{2,3,1,0:T(8,128)} %get-tuple-element.254, f32[8,32,100]{2,1,0:T(8,128)S(1)} %copy-done.47, bf16[8,100,32,32]{1,0,3,2:T(8,128)(2,1)S(1)} %copy-done.30), kind=kOutput, calls=%fused_computation.212 | convolution fusion | flops 170597376 | bytes 13621248 | tf_op jit(solution)/shard_map/whij,wihd->wjhd/dot_general | solution.py:610
  385.5 3.8 copy.180
  389.3 4.6 reshape.396
  396.7 11.8 %multiply_reduce_fusion.2 = (bf16[1024]{0:T(1024)(128)(2,1)S(1)}, f32[800]{0:T(1024)S(1)}, f32[800]{0:T(1024)S(1)}, bf16[1024]{0:T(1024)(128)(2,1)S(1)}, f32[800,1024]{1,0:T(8,128)}) fusion(f32[800,1024]{1,0:T(8,128)S(1)} %copy-done.3, f32[800]{0:T(1024)S(1)} %div.217, f32[800]{0:T(1024)S(1)} %rsqrt.29, f32[1024]{0:T(1024)S(1)} %bitcast.117, ...), kind=kOutput, calls=%fused_computation.57 | convolution fusion | flops 5040533504 | bytes 17781248 | tf_op jit(solution)/shard_map/dot_general | solution.py:66
  409.7 30.0 %spread_count.1 = f32[32,8,128]{2,1,0:T(8,128)} custom-call(f32[8,128]{1,0:T(8,128)} %pad_bitcast_fusion.1.own), custom_call_target="tpu_custom_call" | custom-call | tf_op jit(solution)/shard_map/spread_count/pallas_call | solution.py:470
  441.2 5.4 add_divide_fusion
  449.2 3.6 copy.185
  452.8 12.1 %convolution_convert_fusion.2 = bf16[1024,3072]{1,0:T(8,128)(2,1)} fusion(bf16[800,3072]{0,1:T(8,128)(2,1)} %constant_dynamic-update-slice_fusion, f32[800,1024]{1,0:T(8,128)S(1)} %copy-done.4, f32[1024]{0:T(1024)S(1)} %bitcast.125, f32[800]{0:T(1024)S(1)} %div.217, f32[1024]{0:T(1024)S(1)} %bitcast.119, f32[800]{0:T(1024)S(1)} %rsqrt.29), kind=kOutput, calls=%fused_computation.44 | convolution fusion | flops 5040406528 | bytes 14498048 | tf_op jit(solution)/shard_map/dot_general | solution.py:60
  464.9 3.6 convolution_convert_fusion.3
  468.6 11.7 %convolution_convert_fusion.1 = bf16[1024,4096]{1,0:T(8,128)(2,1)} fusion(bf16[800,4096]{1,0:T(8,128)(2,1)S(1)} %bitcast.145, f32[800,1024]{1,0:T(8,128)S(1)} %copy-done.7, f32[1024]{0:T(1024)S(1)} %bitcast.131, f32[1024]{0:T(1024)S(1)} %bitcast.123, f32[800]{0:T(1024)S(1)} %add_rsqrt_fusion, f32[800]{0:T(1024)S(1)} %broadcast_multiply_fusion.4), kind=kOutput, calls=%fused_computation.39 | convolution fusion | flops 6719176704 | bytes 18233600 | tf_op jit(solution)/shard_map/dot_general | solution.py:60
  480.4 11.5 %convolution_convert_fusion = bf16[4096,1024]{1,0:T(8,128)(2,1)} fusion(bf16[800,4096]{1,0:T(8,128)(2,1)S(1)} %bitcast.147, f32[800,1024]{1,0:T(8,128)S(1)} %copy-done.8, f32[800]{0:T(1024)S(1)} %mul.579), kind=kOutput, calls=%fused_computation.38 | convolution fusion | flops 6716719104 | bytes 18222208 | tf_op jit(solution)/shard_map/dot_general | solution.py:60
  493.2 5.3 fusion.60
  499.9 124.3 %scatter_grads.1 = (f32[32,3072]{1,0:T(8,128)}, f32[32,1024]{1,0:T(8,128)}, f32[32,4096]{1,0:T(8,128)}, f32[128,1024]{1,0:T(8,128)}, f32[32,128]{1,0:T(8,128)}) custom-call(bf16[4,2,2,2,32,3072]{5,4,3,2,1,0:T(8,128)(2,1)} %bitcast.113, bf16[4,2,2,2,32,1024]{5,4,3,2,1,0:T(8,128)(2,1)} %bitcast.114, bf16[4,2,2,2,32,4096]{5,4,3,2,1,0:T(8,128)(2,1)} %bitcast.109, ...), custom_call_target="tpu_custom_call" | custom-call | tf_op jit(solution)/shard_map/scatter_grads/pallas_call | solution.py:413
  624.3 3.1 multiply_reduce_fusion.18
  630.2 3.1 multiply_reduce_fusion.15
  633.4 3.2 multiply_reduce_fusion.14
  639.3 5.3 concatenate.20
  645.2 15.2 %spread_small.1 = f32[32,40,128]{2,1,0:T(8,128)} custom-call(f32[40,128]{1,0:T(8,128)} %pad_maximum_fusion.own), custom_call_target="tpu_custom_call" | custom-call | tf_op jit(solution)/shard_map/spread_small/pallas_call | solution.py:470
  671.2 3.1 multiply_reduce_fusion.16
  680.5 3.3 fusion.70.own
  683.8 14.3 %spread_updates.1 = f32[32,8,128]{2,1,0:T(8,128)} custom-call(f32[8,128]{1,0:T(8,128)} %fusion.70.own), custom_call_target="tpu_custom_call" | custom-call | tf_op jit(solution)/shard_map/spread_updates/pallas_call | solution.py:470
  (267 shorter events, 89.6 us)
Async XLA Ops:
  2.3 9.5 %copy-start.56 = (f32[1,1024]{1,0:T(1,128)}, f32[1,1024]{1,0:T(1,128)S(1)}, u32[]{:S(2)}) copy-start(f32[1,1024]{1,0:T(1,128)S(1)} %get-tuple-element.237) | copy-start | bytes 12292
  2.3 9.5 %copy-start.62 = (f32[1,1024]{1,0:T(1,128)}, f32[1,1024]{1,0:T(1,128)S(1)}, u32[]{:S(2)}) copy-start(f32[1,1024]{1,0:T(1,128)S(1)} %get-tuple-element.236) | copy-start | bytes 12292
  2.3 220.2 %copy-start.69 = (f32[1,1024]{1,0:T(1,128)}, f32[1,1024]{1,0:T(1,128)S(1)}, u32[]{:S(2)}) copy-start(f32[1,1024]{1,0:T(1,128)S(1)} %get-tuple-element.232) | copy-start | bytes 12292
  152.6 5.8 copy-start.42
  158.4 10.6 %copy-start.54 = (s32[10000]{0:T(1024)}, s32[10000]{0:T(1024)S(1)}, u32[]{:S(2)}) copy-start(s32[10000]{0:T(1024)S(1)} %add.304) | copy-start | bytes 120004
  179.6 9.2 %copy-start.11 = (bf16[8,100,32,32]{1,0,3,2:T(8,128)(2,1)}, bf16[8,100,32,32]{1,0,3,2:T(8,128)(2,1)S(1)}, u32[]{:S(2)}) copy-start(bf16[8,100,32,32]{1,0,3,2:T(8,128)(2,1)S(1)} %reshape.387) | copy-start | bytes 4915204
  208.2 8.6 %copy-start.2 = (f32[800,1024]{1,0:T(8,128)S(1)}, f32[800,1024]{1,0:T(8,128)}, u32[]{:S(2)}) copy-start(f32[800,1024]{1,0:T(8,128)} %reshape.409) | copy-start | bytes 9830404
  221.2 38.6 %copy-start.5 = (f32[800,1024]{1,0:T(8,128)}, f32[800,1024]{1,0:T(8,128)S(1)}, u32[]{:S(2)}) copy-start(f32[800,1024]{1,0:T(8,128)S(1)} %get-tuple-element.256) | copy-start | bytes 9830404
  222.6 39.9 %copy-start.71 = (f32[1,1024]{1,0:T(1,128)S(1)}, f32[1,1024]{1,0:T(1,128)}, u32[]{:S(2)}) copy-start(f32[1,1024]{1,0:T(1,128)} %get-tuple-element.231) | copy-start | bytes 12292
  222.6 39.9 %copy-start.72 = (bf16[4,2,2,2,128,1024]{5,4,3,2,1,0:T(8,128)(2,1)S(1)}, bf16[4,2,2,2,128,1024]{5,4,3,2,1,0:T(8,128)(2,1)}, u32[]{:S(2)}) copy-start(bf16[4,2,2,2,128,1024]{5,4,3,2,1,0:T(8,128)(2,1)} %get-tuple-element.44) | copy-start | bytes 25165828
  276.9 14.9 %copy-start.6 = (f32[800,1024]{1,0:T(8,128)S(1)}, f32[800,1024]{1,0:T(8,128)}, u32[]{:S(2)}) copy-start(f32[800,1024]{1,0:T(8,128)} %copy-done.5) | copy-start | bytes 9830404
  291.8 14.5 %copy-start.73 = (bf16[800,4096]{1,0:T(8,128)(2,1)}, bf16[800,4096]{1,0:T(8,128)(2,1)S(1)}, u32[]{:S(2)}) copy-start(bf16[800,4096]{1,0:T(8,128)(2,1)S(1)} %get-tuple-element.268) | copy-start | bytes 19660804
  291.8 14.5 %copy-start.19 = (bf16[8,100,1024]{2,0,1:T(8,128)(2,1)S(1)}, bf16[8,100,1024]{2,0,1:T(8,128)(2,1)}, u32[]{:S(2)}) copy-start(bf16[8,100,1024]{2,0,1:T(8,128)(2,1)} %param.22) | copy-start | bytes 4915204
  313.9 5.8 copy-start.9
  319.7 8.9 %copy-start.47 = (f32[8,32,100]{2,1,0:T(8,128)S(1)}, f32[8,32,100]{2,1,0:T(8,128)}, u32[]{:S(2)}) copy-start(f32[8,32,100]{2,1,0:T(8,128)} %copy-done.46) | copy-start | bytes 307204
  339.0 11.7 %copy-start.12 = (bf16[8,100,32,32]{1,0,3,2:T(8,128)(2,1)S(1)}, bf16[8,100,32,32]{1,0,3,2:T(8,128)(2,1)}, u32[]{:S(2)}) copy-start(bf16[8,100,32,32]{1,0,3,2:T(8,128)(2,1)} %copy-done.11) | copy-start | bytes 4915204
  389.3 7.5 %copy-start.3 = (f32[800,1024]{1,0:T(8,128)S(1)}, f32[800,1024]{1,0:T(8,128)}, u32[]{:S(2)}) copy-start(f32[800,1024]{1,0:T(8,128)} %reshape.409) | copy-start | bytes 9830404
  389.3 7.5 %copy-start.57 = (f32[1,1024]{1,0:T(1,128)S(1)}, f32[1,1024]{1,0:T(1,128)}, u32[]{:S(2)}) copy-start(f32[1,1024]{1,0:T(1,128)} %copy-done.56) | copy-start | bytes 12292
  449.1 19.4 %slice-start.2 = ((s8[6553600]{0:T(1024)(128)(4,1)}), s8[4194304]{0:T(1024)(128)(4,1)S(1)}, s32[]{:S(2)}) async-start(s8[6553600]{0:T(1024)(128)(4,1)} %bitcast.144), calls=%async_computation.2 | async-start | bytes 8388608
  452.8 12.1 %copy-start.10 = (f32[800,1024]{1,0:T(8,128)S(1)}, f32[800,1024]{1,0:T(8,128)}, u32[]{:S(2)}) copy-start(f32[800,1024]{1,0:T(8,128)} %copy-done.9) | copy-start | bytes 9830404
  452.8 12.1 %copy-start.31 = (bf16[800,1024]{0,1:T(8,128)(2,1)S(1)}, bf16[800,1024]{0,1:T(8,128)(2,1)}, u32[]{:S(2)}) copy-start(bf16[800,1024]{0,1:T(8,128)(2,1)} %convert_element_type.166) | copy-start | bytes 4915204
  452.8 15.8 %slice-start.3 = ((s8[6553600]{0:T(1024)(128)(4,1)}), s8[2359296]{0:T(1024)(128)(4,1)S(1)}, s32[]{:S(2)}) async-start(s8[6553600]{0:T(1024)(128)(4,1)} %bitcast.144), calls=%async_computation.3 | async-start | bytes 4718592
  464.9 15.4 %slice-start.4 = ((s8[6553600]{0:T(1024)(128)(4,1)}), s8[4194304]{0:T(1024)(128)(4,1)S(1)}, s32[]{:S(2)}) async-start(s8[6553600]{0:T(1024)(128)(4,1)} %bitcast.146), calls=%async_computation.4 | async-start | bytes 8388608
  468.6 11.7 %copy-start.8 = (f32[800,1024]{1,0:T(8,128)S(1)}, f32[800,1024]{1,0:T(8,128)}, u32[]{:S(2)}) copy-start(f32[800,1024]{1,0:T(8,128)} %reshape.410) | copy-start | bytes 9830404
  468.6 11.7 %slice-start.5 = ((s8[6553600]{0:T(1024)(128)(4,1)}), s8[2359296]{0:T(1024)(128)(4,1)S(1)}, s32[]{:S(2)}) async-start(s8[6553600]{0:T(1024)(128)(4,1)} %bitcast.146), calls=%async_computation.5 | async-start | bytes 4718592
  480.3 11.5 %copy-start.17 = (f32[32,100,100]{1,2,0:T(8,128)S(1)}, f32[32,100,100]{1,2,0:T(8,128)}, u32[]{:S(2)}) copy-start(f32[32,100,100]{1,2,0:T(8,128)} %get-tuple-element.224) | copy-start | bytes 3840004
  493.2 5.8 copy-start.68
  493.2 5.8 copy-start.67
  624.2 12.3 %copy-start.20 = (f32[32,3072]{1,0:T(8,128)S(1)}, f32[32,3072]{1,0:T(8,128)}, u32[]{:S(2)}) copy-start(f32[32,3072]{1,0:T(8,128)} %refs_0_.1) | copy-start | bytes 1179652
  624.2 13.0 %copy-start.27 = (f32[32,1024]{1,0:T(8,128)S(1)}, f32[32,1024]{1,0:T(8,128)}, u32[]{:S(2)}) copy-start(f32[32,1024]{1,0:T(8,128)} %refs_1_.1) | copy-start | bytes 393220
  624.2 13.6 %copy-start.13 = (f32[32,4096]{1,0:T(8,128)S(1)}, f32[32,4096]{1,0:T(8,128)}, u32[]{:S(2)}) copy-start(f32[32,4096]{1,0:T(8,128)} %refs_2_.1) | copy-start | bytes 1572868
  624.3 14.4 %copy-start.14 = (f32[128,1024]{1,0:T(8,128)S(1)}, f32[128,1024]{1,0:T(8,128)}, u32[]{:S(2)}) copy-start(f32[128,1024]{1,0:T(8,128)} %refs_3_.1) | copy-start | bytes 1572868
  624.3 20.3 %copy-start.64 = (f32[32,128]{1,0:T(8,128)S(1)}, f32[32,128]{1,0:T(8,128)}, u32[]{:S(2)}) copy-start(f32[32,128]{1,0:T(8,128)} %get-tuple-element.49) | copy-start | bytes 49156
  668.7 8.5 %copy-start.22 = (f32[32,4096]{1,0:T(8,128)S(1)}, f32[32,4096]{1,0:T(8,128)}, u32[]{:S(2)}) copy-start(f32[32,4096]{1,0:T(8,128)} %get-tuple-element.217) | copy-start | bytes 1572868
  671.2 6.1 copy-start.35
  671.2 6.1 copy-start.36
  677.3 33.0 %copy-start.23 = (f32[128,1024]{1,0:T(8,128)}, f32[128,1024]{1,0:T(8,128)S(1)}, u32[]{:S(2)}) copy-start(f32[128,1024]{1,0:T(8,128)S(1)} %get-tuple-element.212) | copy-start | bytes 1572868
  677.3 33.0 %copy-start.24 = (f32[128,1024]{1,0:T(8,128)}, f32[128,1024]{1,0:T(8,128)S(1)}, u32[]{:S(2)}) copy-start(f32[128,1024]{1,0:T(8,128)S(1)} %get-tuple-element.213) | copy-start | bytes 1572868
  679.1 32.3 %copy-start.25 = (f32[32,4096]{1,0:T(8,128)}, f32[32,4096]{1,0:T(8,128)S(1)}, u32[]{:S(2)}) copy-start(f32[32,4096]{1,0:T(8,128)S(1)} %get-tuple-element.209) | copy-start | bytes 1572868
  679.1 28.6 %copy-start.26 = (f32[32,4096]{1,0:T(8,128)S(1)}, f32[32,4096]{1,0:T(8,128)}, u32[]{:S(2)}) copy-start(f32[32,4096]{1,0:T(8,128)} %get-tuple-element.210) | copy-start | bytes 1572868
  701.0 10.5 %copy-start.33 = (f32[12,1024]{1,0:T(8,128)S(1)}, f32[12,1024]{1,0:T(8,128)}, u32[]{:S(2)}) copy-start(f32[12,1024]{1,0:T(8,128)} %copy-done.32) | copy-start | bytes 147460
  701.0 10.5 %copy-start.37 = (f32[12,1024]{1,0:T(8,128)S(1)}, f32[12,1024]{1,0:T(8,128)}, u32[]{:S(2)}) copy-start(f32[12,1024]{1,0:T(8,128)} %param.36) | copy-start | bytes 147460
  701.0 10.4 %copy-start.50 = (f32[12,1024]{1,0:T(8,128)S(1)}, f32[12,1024]{1,0:T(8,128)}, u32[]{:S(2)}) copy-start(f32[12,1024]{1,0:T(8,128)} %param.38) | copy-start | bytes 147460
  701.0 10.4 %copy-start.51 = (f32[12,1024]{1,0:T(8,128)S(1)}, f32[12,1024]{1,0:T(8,128)}, u32[]{:S(2)}) copy-start(f32[12,1024]{1,0:T(8,128)} %param.37) | copy-start | bytes 147460
  703.2 9.1 %copy-start.39 = (f32[361,32]{0,1:T(8,128)S(1)}, f32[361,32]{0,1:T(8,128)}, u32[]{:S(2)}) copy-start(f32[361,32]{0,1:T(8,128)} %copy-done.38) | copy-start | bytes 138628
  703.2 9.1 %copy-start.43 = (f32[361,32]{0,1:T(8,128)S(1)}, f32[361,32]{0,1:T(8,128)}, u32[]{:S(2)}) copy-start(f32[361,32]{0,1:T(8,128)} %param.39) | copy-start | bytes 138628
  703.2 9.2 %copy-start.52 = (f32[361,32]{0,1:T(8,128)S(1)}, f32[361,32]{0,1:T(8,128)}, u32[]{:S(2)}) copy-start(f32[361,32]{0,1:T(8,128)} %param.41) | copy-start | bytes 138628
  703.2 9.2 %copy-start.53 = (f32[361,32]{0,1:T(8,128)S(1)}, f32[361,32]{0,1:T(8,128)}, u32[]{:S(2)}) copy-start(f32[361,32]{0,1:T(8,128)} %param.40) | copy-start | bytes 138628
  (33 other events, 115.2 us)

commit v2 on v1

v2 whole, which is shorter than its diff:
```python
import functools

import jax
import jax.numpy as jnp
from jax import lax
from jax.experimental import pallas as pl
from jax.experimental.pallas import tpu as pltpu
from jax.sharding import PartitionSpec as P

MESH = pl.DeviceIdType.MESH
AXES = ("dp", "fsdp")
VMEM_LIMIT = 60 * 1024 * 1024

HEADS = 32
WS = 10
STEP = 10


EPSILON = 1e-05
MOMENT_ONE = 0.9
MOMENT_TWO = 0.999
LEARN_RATE = 0.3
DECAY = 0.01
ADAM_EPS = 1e-06
CLIP_LIMIT = 0.05
MASK_FILL = 10000.0
HIGH = lax.Precision.HIGHEST
BF, F32 = jnp.bfloat16, jnp.float32


def position_index(size):
    cells = jnp.arange(size * size, dtype=jnp.int32)
    rows = cells // size
    cols = cells % size
    drow = rows[:, None] - rows[None, :] + size - 1
    dcol = cols[:, None] - cols[None, :] + size - 1
    return drow * (2 * size - 1) + dcol


def moments(grad, first, second, weight, factor):
    clipped = grad * factor
    first_new = MOMENT_ONE * first + (1.0 - MOMENT_ONE) * clipped
    second_new = MOMENT_TWO * second + (1.0 - MOMENT_TWO) * clipped * clipped
    update = (
        first_new
        / (1.0 - MOMENT_ONE**STEP)
        / (jnp.sqrt(second_new / (1.0 - MOMENT_TWO**STEP)) + ADAM_EPS)
        + DECAY * weight
    )
    return (first_new, second_new, update)


def whole(shape):
    zeros = (0,) * len(shape)
    return pl.BlockSpec(shape, lambda *s: zeros, pipeline_mode=pl.Buffered(1))


def whole_out(shape):
    zeros = (0,) * len(shape)
    return pl.BlockSpec(shape, lambda *s: zeros)


def struct(shape, dtype):
    return jax.ShapeDtypeStruct(shape, dtype)


HOP = 2.0


def link_us(shape, dtype):
    return 2 * shape[0] * shape[1] * jnp.dtype(dtype).itemsize / 95e3


class Place:
    def __init__(self, nz, sems):
        dp = lax.axis_index("dp")
        fsdp = lax.axis_index("fsdp")
        self.nz = nz
        self.z, self.x = dp // 2, dp % 2
        self.y, self.c = fsdp // 2, fsdp % 2
        self.sems = sems
        self.used = 0

    def sem(self):
        self.used += 1
        return self.sems.at[self.used - 1]

    def zplus(self, k):
        return lax.rem(self.z + k, self.nz)

    def to(self, z=None, x=None, y=None, c=None):
        z = self.z if z is None else z
        x = self.x if x is None else x
        y = self.y if y is None else y
        c = self.c if c is None else c
        return (z * 2 + x, y * 2 + c)

    def peers(self):
        found = [self.to(z=self.zplus(k)) for k in range(1, self.nz)]
        found.append(self.to(x=1 - self.x))
        found.append(self.to(y=1 - self.y))
        found.append(self.to(c=1 - self.c))
        return found

    def greet(self):
        barrier = pltpu.get_barrier_semaphore()
        peers = self.peers()
        for peer in peers:
            pl.semaphore_signal(barrier, inc=1, device_id=peer, device_id_type=MESH)
        pl.semaphore_wait(barrier, len(peers))

    def send(self, source, target, device):
        return pltpu.make_async_remote_copy(
            src_ref=source,
            dst_ref=target,
            send_sem=self.sem(),
            recv_sem=self.sem(),
            device_id=device,
            device_id_type=MESH,
        )

    def move(self, source, target):
        return pltpu.make_async_copy(source, target, self.sem())


def gather_sems(nz):
    return 2 * (nz - 1) + 18 * nz + 1


def gather_events(place, own, out):
    nz, z, x, y, c = place.nz, place.z, place.x, place.y, place.c
    half = own.shape[0] // 2
    ox, oy, oc = 1 - x, 1 - y, 1 - c
    xp, yp, cp = place.to(x=ox), place.to(y=oy), place.to(c=oc)
    zs = [lax.rem(z - k + nz, nz) for k in range(nz)]
    low, high = pl.ds(0, half), pl.ds(half, half)

    def forward(slot, device, part=None, source=None):
        if part is not None:
            slot = slot.at[part]
        return place.send(slot if source is None else source, slot, device)

    mine = place.move(own, out.at[z, x, y, c])
    along = [None] + [
        place.send(own, out.at[z, x, y, c], place.to(z=place.zplus(k))) for k in range(1, nz)
    ]
    line = [out.at[zs[k], x, y, c] for k in range(nz)]
    beside = [out.at[zs[k], ox, y, c] for k in range(nz)]
    across = [out.at[zs[k], x, oy, c] for k in range(nz)]
    corner = [out.at[zs[k], ox, oy, c] for k in range(nz)]
    first = lambda k: own if k == 0 else None
    x_full = [forward(line[k], xp, source=first(k)) for k in range(nz)]
    y_full = [forward(line[k], yp, source=first(k)) for k in range(nz)]
    c_line = [forward(line[k], cp, source=first(k)) for k in range(nz)]
    x_half = [forward(beside[k], yp, low) for k in range(nz)]
    y_half = [forward(across[k], xp, high) for k in range(nz)]
    c_beside = [forward(beside[k], cp) for k in range(nz)]
    c_across = [forward(across[k], cp) for k in range(nz)]
    c_low = [forward(corner[k], cp, low) for k in range(nz)]
    c_high = [forward(corner[k], cp, high) for k in range(nz)]

    def begin():
        for k in range(1, nz):
            along[k].start()
        x_full[0].start()
        y_full[0].start()
        c_line[0].start()
        mine.start()

    def on_line(k):
        along[k].wait_recv()
        x_full[k].start()
        y_full[k].start()
        c_line[k].start()

    def on_beside(k):
        x_full[k].wait_recv()
        x_half[k].start()
        c_beside[k].start()

    def on_across(k):
        y_full[k].wait_recv()
        y_half[k].start()
        c_across[k].start()

    def on_corner(k):
        x_half[k].wait_recv()
        c_low[k].start()
        y_half[k].wait_recv()
        c_high[k].start()

    def finish():
        mine.wait()
        for copies in (c_line, c_beside, c_across, c_low, c_high):
            for copy in copies:
                copy.wait_recv()
        for copies in (along[1:], x_full, y_full, c_line, x_half, y_half, c_beside, c_across, c_low, c_high):
            for copy in copies:
                copy.wait_send()

    unit = link_us(own.shape, own.dtype)
    events = [(0.0, begin)]
    for k in range(nz):
        if k:
            events.append((HOP + (1 + k) * unit, functools.partial(on_line, k)))
        near = HOP + unit if k == 0 else 2 * HOP + (2.5 + k) * unit
        events.append((near, functools.partial(on_beside, k)))
        events.append((near, functools.partial(on_across, k)))
        events.append((near + HOP + (1 + k * 0.3) * unit, functools.partial(on_corner, k)))
    return events, (4 * HOP + 7.5 * unit, finish)


def scatter_sems(nz):
    return 4 * nz + 8 * nz + 8 * nz + 2 * (nz - 1)


def scatter_scratch(nz, rows, columns):
    shape = lambda *lead: pltpu.VMEM(lead + (columns,), jnp.bfloat16)
    return [
        shape(nz, 2, 2, rows),
        shape(nz, 2, 2, rows),
        shape(nz, rows // 2),
        shape(nz, rows // 2),
        shape(nz, rows),
        shape(nz, rows),
        shape(max(nz - 1, 1), rows),
    ]


def scatter_events(place, grads, part, total, scratch):
    nz, z, x, y, c = place.nz, place.z, place.x, place.y, place.c
    held, twin, corner_low, corner_high, from_x, from_y, from_z = scratch
    rows, columns = total.shape
    half = rows // 2
    part = pl.ds(*part)
    ox, oy, oc = 1 - x, 1 - y, 1 - c
    xp, yp, cp = place.to(x=ox), place.to(y=oy), place.to(c=oc)
    order = list(range(1, nz)) + [0]
    zs = [place.zplus(k) for k in range(nz)]
    cell = {(0, 0): (x, y), (1, 0): (ox, y), (0, 1): (x, oy), (1, 1): (ox, oy)}
    quads = [(1, 1), (1, 0), (0, 1), (0, 0)]
    loads, twins = {}, {}
    for k in order:
        for q in quads:
            cx, cy = cell[q]
            loads[q, k] = place.move(grads.at[zs[k], cx, cy, c, part], held.at[zs[k], q[0], q[1]])
            twins[q, k] = place.send(grads.at[zs[k], cx, cy, oc, part], twin.at[zs[k], q[0], q[1]], cp)
    low, high = pl.ds(0, half), pl.ds(half, half)
    out_low = [place.send(held.at[zs[k], 1, 1, low], corner_low.at[zs[k]], xp) for k in range(nz)]
    out_high = [place.send(held.at[zs[k], 1, 1, high], corner_high.at[zs[k]], yp) for k in range(nz)]
    out_x = [place.send(held.at[zs[k], 1, 0], from_x.at[zs[k]], xp) for k in range(nz)]
    out_y = [place.send(held.at[zs[k], 0, 1], from_y.at[zs[k]], yp) for k in range(nz)]
    out_z = [None] + [
        place.send(held.at[zs[k], 0, 0], from_z.at[k - 1], place.to(z=zs[k])) for k in range(1, nz)
    ]

    def summed(target, parts):
        lo, n = target[1], target[2]

        def step(i, carry):
            at = pl.multiple_of(i * 16, 16)
            value = parts[0](at)
            for part in parts[1:]:
                value = value + part(at)
            target[0](lo + at, value)
            return carry

        lax.fori_loop(0, n // 16, step, 0)

    def read(ref, *index, lo=0):
        return lambda at: ref[index + (pl.ds(lo + at, 16),)].astype(jnp.float32)

    def write(ref, *index):
        def store(at, value):
            ref[index + (pl.ds(at, 16),)] = value.astype(ref.dtype)

        return store

    def begin():
        for q in quads[:1]:
            for k in order:
                twins[q, k].start()
                loads[q, k].start()
        for k in order:
            for q in quads[1:]:
                twins[q, k].start()
                loads[q, k].start()

    def arrived(q, k):
        loads[q, k].wait()
        twins[q, k].wait_recv()

    def on_corner(k):
        arrived((1, 1), k)
        at = (zs[k], 1, 1)
        summed((write(held, *at), 0, rows), [read(held, *at), read(twin, *at)])
        out_low[k].start()
        out_high[k].start()

    def on_beside(k):
        arrived((1, 0), k)
        at = (zs[k], 1, 0)
        summed((write(held, *at), 0, half), [read(held, *at), read(twin, *at)])
        out_high[k].wait_recv()
        summed(
            (write(held, *at), half, half),
            [read(held, *at, lo=half), read(twin, *at, lo=half), read(corner_high, zs[k])],
        )
        out_x[k].start()

    def on_across(k):
        arrived((0, 1), k)
        at = (zs[k], 0, 1)
        summed((write(held, *at), half, half), [read(held, *at, lo=half), read(twin, *at, lo=half)])
        out_low[k].wait_recv()
        summed(
            (write(held, *at), 0, half),
            [read(held, *at), read(twin, *at), read(corner_low, zs[k])],
        )
        out_y[k].start()

    def on_line(k):
        arrived((0, 0), k)
        out_x[k].wait_recv()
        out_y[k].wait_recv()
        at = (zs[k], 0, 0)
        parts = [read(held, *at), read(twin, *at), read(from_x, zs[k]), read(from_y, zs[k])]
        if k:
            summed((write(held, *at), 0, rows), parts)
            out_z[k].start()
        else:
            for j in range(1, nz):
                out_z[j].wait_recv()
            parts = parts + [read(from_z, j) for j in range(nz - 1)]
            summed((write(total), 0, rows), parts)

    def finish():
        for copies in (list(twins.values()), out_low, out_high, out_x, out_y, out_z[1:]):
            for copy in copies:
                copy.wait_send()

    unit = link_us((rows, columns), grads.dtype)
    core = 0.2 * unit
    events = [(0.0, begin)]
    for i, k in enumerate(order):
        early = 2 + core * (1 + 0.5 * i)
        events.append((early, functools.partial(on_corner, k)))
        events.append((early + HOP + (1 + 0.5 * i) * unit, functools.partial(on_beside, k)))
        events.append((early + HOP + (1 + 0.5 * i) * unit, functools.partial(on_across, k)))
        events.append((2 * HOP + 2 + core + (3 + i) * unit, functools.partial(on_line, k)))
    return events, (0.0, finish)


def plan_of(lists, steps, step_us):
    timed, ends = [], []
    for (events, end), offset in lists:
        timed += [(offset + at, i, event) for i, (at, event) in enumerate(events)]
        ends.append(end[1])
    timed.sort(key=lambda e: e[:2])
    before, after = {}, []
    for at, _, event in timed:
        step = -int(-at // step_us)
        if step < steps:
            before.setdefault(step, []).append(event)
        else:
            after.append(event)
    return before, after + ends


def fused_kernel(body, nz, counts, kinds, steps, step_us, *refs):
    n_in, n_out, n_scratch = counts
    n = len(kinds)
    ins, given = refs[:n_in], refs[n_in : n_in + n]
    refs = refs[n_in + n :]
    outs, made = refs[:n_out], refs[n_out : n_out + n]
    refs = refs[n_out + n :]
    scratch, spare = refs[:n_scratch], list(refs[n_scratch:-1])
    step = pl.program_id(0)
    place = Place(nz, refs[-1])
    lists, lows = [], []
    for kind, source, target in zip(kinds, given, made):
        if kind[0] == "gather":
            low = spare.pop(0)
            lows.append((source, low))
            events = gather_events(place, low, target)
        else:
            events = scatter_events(place, source, kind[2], target, [spare.pop(0) for _ in range(7)])
        lists.append((events, kind[1]))
    before, after = plan_of(lists, steps, step_us)

    @pl.when(step == 0)
    def _():
        for source, low in lows:
            low[...] = source[...].astype(low.dtype)
        place.greet()

    for at in sorted(before):

        @pl.when(step == at)
        def _(events=before[at]):
            for event in events:
                event()

    body(*ins, *outs, *scratch)

    @pl.when(step == steps - 1)
    def _():
        for event in after:
            event()


def call(body, name, steps, ins, in_specs, outs, out_specs, scratch=(), moves=(), nz=0, collective=None, step_us=1.0):
    scratch = list(scratch)
    params = dict(vmem_limit_bytes=VMEM_LIMIT)
    kinds = [m[:3] for m in moves]
    counts = (len(ins), len(outs), len(scratch))
    kernel = body
    if moves:
        params.update(collective_id=collective, has_side_effects=True)
        kernel = functools.partial(fused_kernel, body, nz, counts, kinds, steps, step_us)
    ins, in_specs, outs, out_specs = list(ins), list(in_specs), list(outs), list(out_specs)
    sems = 0
    for move in moves:
        array = move[3]
        ins.append(array)
        if move[0] == "gather":
            in_specs.append(whole(array.shape))
            outs.append(struct((nz, 2, 2, 2) + array.shape, move[2]))
            out_specs.append(pl.BlockSpec(memory_space=pl.ANY))
            scratch.append(pltpu.VMEM(array.shape, move[2]))
            sems += gather_sems(nz)
        else:
            in_specs.append(pl.BlockSpec(memory_space=pl.ANY))
            shape = (move[2][1], array.shape[5])
            outs.append(struct(shape, F32))
            out_specs.append(whole_out(shape))
            scratch += scatter_scratch(nz, *shape)
            sems += scatter_sems(nz)
    if moves:
        scratch.append(pltpu.SemaphoreType.DMA((sems,)))
    made = pl.pallas_call(
        kernel,
        name=name,
        grid=(steps,),
        out_shape=outs,
        in_specs=in_specs,
        out_specs=out_specs,
        scratch_shapes=scratch,
        compiler_params=pltpu.CompilerParams(**params),
    )(*ins)
    return made[: counts[1]], made[counts[1] :]


def times(left, right):
    return jnp.dot(left, right, preferred_element_type=jnp.float32)


def times_transpose(left, right):
    return lax.dot_general(
        left, right, (((1,), (1,)), ((), ())), preferred_element_type=jnp.float32
    )


def transpose_times(left, right):
    return lax.dot_general(
        left, right, (((0,), (0,)), ((), ())), preferred_element_type=jnp.float32
    )


def normalize(value):
    centre = value - jnp.mean(value, axis=-1, keepdims=True)
    rstd = lax.rsqrt(jnp.mean(centre * centre, axis=-1, keepdims=True) + EPSILON)
    return centre * rstd, rstd


def norm_back(grad_out, normed, rstd, gain):
    scaled = grad_out * gain
    mean_one = jnp.mean(scaled, axis=-1, keepdims=True)
    mean_two = jnp.mean(scaled * normed, axis=-1, keepdims=True)
    return rstd * (scaled - mean_one - normed * mean_two)


def eight(value):
    rows, columns = value.shape
    return jnp.sum(value.reshape(rows // 8, 8, columns), axis=0)


def gelu_parts(value):
    bell = jnp.exp(-0.5 * value * value)
    size = jnp.abs(value)
    t = 1.0 / (1.0 + 0.23164189 * size)
    tail = t * (
        0.127414796
        + t * (-0.142248368 + t * (0.7107068705 + t * (-0.7265760135 + t * 0.5307027145)))
    )
    tail = tail * bell
    phi_big = jnp.where(value >= 0.0, 1.0 - tail, tail)
    return phi_big, bell * 0.3989422804014327


STRIP = 32


def strips(rows, body, carry, unroll=2):
    def step(i, value):
        return body(pl.ds(pl.multiple_of(i * STRIP, STRIP), STRIP), value)

    return lax.fori_loop(0, rows // STRIP, step, carry, unroll=unroll)


def enter_kernel(patches, cotangent, keep, vec, hidden, source, upstream, bias_sum, spare):
    pair = pl.program_id(0)
    cells, width = patches.shape[1:]
    high = hidden.shape[0] // 2
    gain, shift = vec[0:1], vec[1:2]
    spare[...] = jnp.zeros_like(spare)
    for w in range(2):
        value = patches[w].astype(F32)
        spare[pl.ds(w * high, cells)] = value
    source[...] = spare[...].astype(BF)
    for w in range(2):
        normed, _ = normalize(spare[pl.ds(w * high, cells)])
        spare[pl.ds(w * high, cells)] = normed * gain + shift
    hidden[...] = spare[...].astype(BF)

    @pl.when(pair == 0)
    def _():
        bias_sum[...] = jnp.zeros_like(bias_sum)

    spare[...] = jnp.zeros_like(spare)
    for w in range(2):
        mask = jnp.concatenate([keep[w]] * (width // 128), axis=1)
        spare[pl.ds(w * high, cells)] = cotangent[w].astype(F32) * mask[:cells]
    bias_sum[...] += eight(spare[...])
    upstream[...] = spare[...].astype(BF)


def enter(patches, cotangent, keep, vec, **comm):
    windows, cells, width = patches.shape
    high = -(-cells // 8) * 8
    rows = windows * high
    block = pl.BlockSpec((2, cells, width), lambda s: (s, 0, 0))
    flat = pl.BlockSpec((2 * high, width), lambda s: (s, 0))
    return call(
        enter_kernel,
        "enter",
        steps=windows // 2,
        outs=[struct((rows, width), BF)] * 3 + [struct((8, width), F32)],
        in_specs=[
            block,
            block,
            pl.BlockSpec((2, high, 128), lambda s: (s, 0, 0)),
            whole(vec.shape),
        ],
        out_specs=[flat, flat, flat, whole_out((8, width))],
        scratch=[pltpu.VMEM((2 * high, width), F32)],
        ins=[patches, cotangent, keep, vec],
        **comm,
    )


def lanes_of(head):
    lane = lax.broadcasted_iota(jnp.int32, (1, 128), 1)
    return (lane // 32) == head


def pick(value, head):
    return jnp.where(lanes_of(head), value, jnp.zeros_like(value))


def attend_kernel(hidden, wq, wk, wv, vec, bias, mask, query, keys, values, probs, out):
    windows, high, columns = query.shape
    pairs = windows // 2
    group, pair = pl.program_id(0) // pairs, lax.rem(pl.program_id(0), pairs)

    @pl.when(pair == 0)
    def _():
        at = pl.ds(pl.multiple_of(group * columns, columns), columns)
        for weight, target, bias_row in ((wq, query, 2), (wk, keys, None), (wv, values, 3)):
            product = times(hidden[...], weight[...])
            if bias_row is not None:
                product = product + vec[bias_row : bias_row + 1, at]
            for w in range(windows):
                target[w] = product[w * high : (w + 1) * high].astype(BF)

    scale = 32 ** (-0.5)
    done = []
    for w in range(2):
        window = pair * 2 + w
        parts = []
        for g in range(columns // 128):
            at = pl.ds(g * 128, 128)
            q, k, v = query[window, :, at], keys[window, :, at], values[window, :, at]
            vt = v.T
            heads = []
            for h in range(4):
                score = times_transpose(pick(k, h), q) * scale
                score = score + bias[g * 4 + h, :, :high] + mask[window, :, :high]
                score = jnp.exp(score - jnp.max(score, axis=0, keepdims=True))
                prob = (score * (1.0 / jnp.sum(score, axis=0, keepdims=True))).astype(BF)
                probs[w, g * 4 + h, :, :high] = prob
                heads.append(times(vt[32 * h : 32 * h + 32], prob))
            parts.append(jnp.concatenate(heads, axis=0).T)
        done.append(jnp.concatenate(parts, axis=1))
    out[...] = jnp.concatenate(done, axis=0).astype(BF)


def attend(hidden, weight, vec, bias, mask, **comm):
    rows, width = hidden.shape
    windows, high, _ = mask.shape
    heads = bias.shape[0]
    columns = 256
    groups = width // columns
    per = columns // 32
    pairs = windows // 2
    cols = [
        pl.BlockSpec((width, columns), functools.partial(lambda j, s: (0, j * groups + s // pairs), j))
        for j in range(3)
    ]
    seen = pl.BlockSpec((windows, high, columns), lambda s: (0, 0, s // pairs))
    return call(
        attend_kernel,
        "attend",
        steps=groups * pairs,
        outs=[struct((windows, high, width), BF)] * 3
        + [struct((windows, heads, high, 128), BF), struct((rows, width), BF)],
        in_specs=[whole((rows, width))]
        + cols
        + [
            whole(vec.shape),
            pl.BlockSpec((per, high, 128), lambda s: (s // pairs, 0, 0)),
            whole(mask.shape),
        ],
        out_specs=[seen] * 3
        + [
            pl.BlockSpec((2, per, high, 128), lambda s: (lax.rem(s, pairs), s // pairs, 0, 0)),
            pl.BlockSpec((2 * high, columns), lambda s: (lax.rem(s, pairs), s // pairs)),
        ],
        ins=[hidden, weight, weight, weight, vec, bias, mask],
        **comm,
    )


def expand_kernel(attended, source, upstream, wo, we, vec, be, middle, hidden_t, act, slope, grad, hidden, spare):
    step = pl.program_id(0)
    rows, width = hidden.shape

    @pl.when(step == 0)
    def _():
        for j in range(2):
            at = pl.ds(j * (width // 2), width // 2)
            middle[:, at] = times(attended[...], wo[:, at]) + vec[4:5, at]

        def strip(at, carry):
            value = middle[at] + source[at].astype(F32)
            middle[at] = value
            normed, _ = normalize(value)
            hidden[at] = (normed * vec[5:6] + vec[6:7]).astype(BF)
            return carry

        strips(rows, strip, 0)
        hidden_t[...] = hidden[...].T

    @pl.when(step > 0)
    def _():
        spare[...] = times(hidden[...], we[...])

        def strip(at, carry):
            value = spare[at] + be[...]
            big, small = gelu_parts(value)
            act[at] = (value * big).astype(BF)
            slope[at] = (big + value * small).astype(BF)
            return carry

        strips(rows, strip, 0)
        grad[...] = transpose_times(act[...], upstream[...]).astype(BF)


def expand(attended, source, upstream, w_output, w_expand, vec, be, **comm):
    rows, width = attended.shape
    ff = w_expand.shape[1]
    chunk = 512
    at = lambda s: jnp.maximum(s - 1, 0)
    wide = pl.BlockSpec((rows, chunk), lambda s: (0, at(s)))
    return call(
        expand_kernel,
        "expand",
        steps=1 + ff // chunk,
        outs=[
            struct((rows, width), F32),
            struct((width, rows), BF),
            struct((rows, ff), BF),
            struct((rows, ff), BF),
            struct((ff, width), BF),
        ],
        in_specs=[whole((rows, width))] * 3
        + [
            whole((width, width)),
            pl.BlockSpec((width, chunk), lambda s: (0, at(s))),
            whole(vec.shape),
            pl.BlockSpec((1, chunk), lambda s: (0, at(s))),
        ],
        out_specs=[
            whole_out((rows, width)),
            whole_out((width, rows)),
            wide,
            wide,
            pl.BlockSpec((chunk, width), lambda s: (at(s), 0)),
        ],
        scratch=[pltpu.VMEM((rows, width), BF), pltpu.VMEM((rows, chunk), F32)],
        ins=[attended, source, upstream, w_output, w_expand, vec, be],
        **comm,
    )


def shrink_kernel(act, slope, ws, upstream, hidden_t, middle, vec, result, back, back_sum, grad, total):
    step = pl.program_id(0)
    rows, width = total.shape
    windows, cells, _ = result.shape
    high = rows // windows

    @pl.when(step == 0)
    def _():
        total[...] = middle[...] + vec[7:8]

    total[...] += times(act[...], ws[...])
    product = times_transpose(upstream[...], ws[...])
    back[...] = (product * slope[...].astype(F32)).astype(BF)
    back_sum[...] = jnp.sum(back[...].astype(F32), axis=0, keepdims=True)
    grad[...] = times(hidden_t[...], back[...]).astype(BF)

    @pl.when(step == pl.num_programs(0) - 1)
    def _():
        for w in range(windows):
            result[w] = total[pl.ds(w * high, cells)].astype(BF)


def shrink(act, slope, w_shrink, upstream, hidden_t, middle, vec, windows, cells, **comm):
    rows, ff = act.shape
    width = middle.shape[1]
    chunk = 512
    wide = pl.BlockSpec((rows, chunk), lambda s: (0, s))
    return call(
        shrink_kernel,
        "shrink",
        steps=ff // chunk,
        outs=[
            struct((windows, cells, width), BF),
            struct((rows, ff), BF),
            struct((1, ff), F32),
            struct((width, ff), BF),
        ],
        in_specs=[
            wide,
            wide,
            pl.BlockSpec((chunk, width), lambda s: (s, 0)),
            whole((rows, width)),
            whole((width, rows)),
            whole((rows, width)),
            whole(vec.shape),
        ],
        out_specs=[
            whole_out((windows, cells, width)),
            wide,
            pl.BlockSpec((1, chunk), lambda s: (0, s)),
            pl.BlockSpec((width, chunk), lambda s: (0, s)),
        ],
        scratch=[pltpu.VMEM((rows, width), F32)],
        ins=[act, slope, w_shrink, upstream, hidden_t, middle, vec],
        **comm,
    )


def inner_kernel(back, we, middle, upstream, attended, wo, vec, mid, grad, dout, sums, total, branch):
    step = pl.program_id(0)
    rows, width = total.shape
    windows, high, _ = dout.shape

    @pl.when(step == 0)
    def _():
        total[...] = jnp.zeros_like(total)

    total[...] += times_transpose(back[...], we[...])

    @pl.when(step == pl.num_programs(0) - 1)
    def _():
        zero = jnp.zeros((8, width), F32)

        def strip(at, carry):
            gain_sum, shift_sum, out_sum = carry
            normed, rstd = normalize(middle[at])
            value = total[at]
            grad_mid = upstream[at].astype(F32) + norm_back(value, normed, rstd, vec[5:6])
            mid[at] = grad_mid
            low = grad_mid.astype(BF)
            branch[at] = low
            return (
                gain_sum + eight(value * normed),
                shift_sum + eight(value),
                out_sum + eight(low.astype(F32)),
            )

        found = strips(rows, strip, (zero, zero, zero), unroll=1)
        for i in range(3):
            sums[i] = found[i]
        for j in range(2):
            at = pl.ds(j * (width // 2), width // 2)
            grad[:, at] = transpose_times(attended[...], branch[:, at]).astype(BF)
            product = times_transpose(branch[...], wo[at])
            for w in range(windows):
                dout[w, :, at] = product[w * high : (w + 1) * high].astype(BF)


def inner(back, w_expand, middle, upstream, attended, w_output, vec, windows, **comm):
    rows, ff = back.shape
    width = middle.shape[1]
    high = rows // windows
    chunk = 512
    return call(
        inner_kernel,
        "inner",
        steps=ff // chunk,
        outs=[
            struct((rows, width), F32),
            struct((width, width), BF),
            struct((windows, high, width), BF),
            struct((3, 8, width), F32),
        ],
        in_specs=[
            pl.BlockSpec((rows, chunk), lambda s: (0, s)),
            pl.BlockSpec((width, chunk), lambda s: (0, s)),
            whole((rows, width)),
            whole((rows, width)),
            whole((rows, width)),
            whole((width, width)),
            whole(vec.shape),
        ],
        out_specs=[
            whole_out((rows, width)),
            whole_out((width, width)),
            whole_out((windows, high, width)),
            whole_out((3, 8, width)),
        ],
        scratch=[pltpu.VMEM((rows, width), F32), pltpu.VMEM((rows, width), BF)],
        ins=[back, w_expand, middle, upstream, attended, w_output, vec],
        **comm,
    )


def unattend_kernel(query, keys, values, dout, probs, hidden, joint, grad, bias_low, sums, hidden_t, bias):
    step = pl.program_id(0)
    windows, high, columns = query.shape
    rows, width = hidden.shape
    pairs = windows // 2
    groups = width // columns
    pair = lax.rem(step, pairs)
    group = step // pairs
    scale = 32 ** (-0.5)

    @pl.when(step == 0)
    def _():
        hidden_t[...] = hidden[...].T

    @pl.when(step < pairs * groups)
    def _():
        @pl.when(pair == 0)
        def _():
            bias[...] = jnp.zeros_like(bias)

        done = []
        for w in range(2):
            window = pair * 2 + w
            parts = []
            for g in range(columns // 128):
                at = pl.ds(g * 128, 128)
                q, k, v = query[window, :, at], keys[window, :, at], values[window, :, at]
                d = dout[window, :, at]
                kt = k.T
                dq, dk, dv = [], None, None
                for h in range(4):
                    prob = probs[w, g * 4 + h, :, :high]
                    dp = times_transpose(pick(v, h), d)
                    soft = prob.astype(F32)
                    both = soft * dp
                    ds = (both - soft * jnp.sum(both, axis=0, keepdims=True)).astype(BF)
                    bias[g * 4 + h, :, :high] += ds.astype(F32)
                    dq.append(times(kt[32 * h : 32 * h + 32], ds))
                    one, two = pick(times(ds, q), h), pick(times(prob, d), h)
                    dk = one if dk is None else dk + one
                    dv = two if dv is None else dv + two
                parts.append((jnp.concatenate(dq, axis=0).T * scale, dk * scale, dv))
            done.append([jnp.concatenate([p[j] for p in parts], axis=1) for j in range(3)])

        @pl.when(pair == pairs - 1)
        def _():
            bias_low[...] = jnp.zeros_like(bias_low)
            bias_low[:, :high] = bias[...].astype(BF)

        at_rows = pl.ds(pl.multiple_of(pair * 2 * high, 16), 2 * high)
        for j in range(3):
            at = pl.ds(pl.multiple_of(j * width + group * columns, columns), columns)
            joint[at_rows, at] = jnp.concatenate([done[0][j], done[1][j]], axis=0).astype(BF)

    @pl.when(step >= pairs * groups)
    def _():
        chunk = grad.shape[1]
        at = pl.ds(pl.multiple_of((step - pairs * groups) * chunk, chunk), chunk)
        grad[...] = times(hidden_t[...], joint[:, at]).astype(BF)
        sums[...] = jnp.sum(joint[:, at].astype(F32), axis=0, keepdims=True)


def unattend(query, keys, values, dout, probs, hidden, **comm):
    windows, high, width = query.shape
    rows = hidden.shape[0]
    heads = probs.shape[1]
    columns, chunk = 256, 512
    groups, pairs = width // columns, windows // 2
    per = columns // 32
    steps = groups * pairs
    group = lambda s: jnp.minimum(s // pairs, groups - 1)
    pair = lambda s: jnp.where(s < steps, lax.rem(s, pairs), pairs - 1)
    later = lambda s: jnp.maximum(s - steps, 0)
    seen = pl.BlockSpec((windows, high, columns), lambda s: (0, 0, group(s)))
    return call(
        unattend_kernel,
        "unattend",
        steps=steps + 3 * width // chunk,
        outs=[
            struct((rows, 3 * width), BF),
            struct((width, 3 * width), BF),
            struct((heads, 128, 128), BF),
            struct((1, 3 * width), F32),
        ],
        in_specs=[seen] * 4
        + [
            pl.BlockSpec((2, per, high, 128), lambda s: (pair(s), group(s), 0, 0)),
            whole((rows, width)),
        ],
        out_specs=[
            whole_out((rows, 3 * width)),
            pl.BlockSpec((width, chunk), lambda s: (0, later(s))),
            pl.BlockSpec((per, 128, 128), lambda s: (group(s), 0, 0)),
            pl.BlockSpec((1, chunk), lambda s: (0, later(s))),
        ],
        scratch=[pltpu.VMEM((width, rows), BF), pltpu.VMEM((per, high, 128), F32)],
        ins=[query, keys, values, dout, probs, hidden],
        **comm,
    )


def leave_kernel(joint, wa, source, mid, vec, inverse, out, sums, total):
    step = pl.program_id(0)
    rows, width = total.shape
    windows, cells, _ = out.shape
    high = rows // windows

    @pl.when(step == 0)
    def _():
        total[...] = jnp.zeros_like(total)

    total[...] += times_transpose(joint[...], wa[...])

    @pl.when(step == pl.num_programs(0) - 1)
    def _():
        zero = jnp.zeros((8, width), F32)

        def strip(at, carry):
            gain_sum, shift_sum = carry
            normed, rstd = normalize(source[at].astype(F32))
            value = total[at]
            full = mid[at] + norm_back(value, normed, rstd, vec[0:1])
            total[at] = full * inverse[0, 0]
            return gain_sum + eight(value * normed), shift_sum + eight(value)

        found = strips(rows, strip, (zero, zero), unroll=1)
        for i in range(2):
            sums[i] = found[i]
        for w in range(windows):
            out[w] = total[pl.ds(w * high, cells)]


def leave(joint, w_attend, source, mid, vec, inverse, windows, cells, **comm):
    rows, width = source.shape
    chunk = 512
    return call(
        leave_kernel,
        "leave",
        steps=3 * width // chunk,
        outs=[struct((windows, cells, width), F32), struct((2, 8, width), F32)],
        in_specs=[
            pl.BlockSpec((rows, chunk), lambda s: (0, s)),
            pl.BlockSpec((width, chunk), lambda s: (0, s)),
            whole((rows, width)),
            whole((rows, width)),
            whole(vec.shape),
            pl.BlockSpec(memory_space=pltpu.SMEM),
        ],
        out_specs=[whole_out((windows, cells, width)), whole_out((2, 8, width))],
        scratch=[pltpu.VMEM((rows, width), F32)],
        ins=[joint, w_attend, source, mid, vec, inverse],
        **comm,
    )


def update_kernel(nz, pieces, step_number, *refs):
    refs = list(refs)
    take = lambda n: [refs.pop(0) for _ in range(n)]
    inverse, leave_sums, bias_sum, small = take(4)
    sums = take(len(pieces))
    masters, firsts, seconds = take(4), take(4), take(4)
    vec, vec_first, vec_second, table, table_first, table_second = take(6)
    grads_out, firsts_out, seconds_out, news_out, copies_out = (take(4) for _ in range(5))
    vec_out, table_out = take(4), take(4)
    (norms_out,) = take(1)
    message, got, message_two, got_two, vec_grad, heads_grad, sems = refs
    place = Place(nz, sems)
    place.greet()
    devices = nz * 8
    scale = inverse[0, 0]
    lane = lax.broadcasted_iota(jnp.int32, (8, 128), 1)
    top = lax.broadcasted_iota(jnp.int32, (8, 128), 0) == 0

    def rows_of(ref):
        return 8 if ref.shape[0] % 16 else 16

    def over(piece, body, carry):
        k, low, count = piece

        def step(i, value):
            at = pl.multiple_of(i * 16, 16)
            return body(k, pl.ds(low + at, 16), pl.ds(at, 16), value)

        return lax.fori_loop(0, count // 16, step, carry)

    def fold(value):
        value = eight(value)
        return functools.reduce(
            jnp.add, [value[:, i : i + 128] for i in range(0, value.shape[1], 128)]
        )

    zero = jnp.zeros((8, 128), F32)
    squares = [zero] * 8
    for p, piece in enumerate(pieces):

        def body(k, at, source, carry):
            grad = sums[p][source] * scale
            grads_out[k][at] = grad
            weight = masters[k][at]
            return carry[0] + fold(grad * grad), carry[1] + fold(weight * weight)

        k = piece[0]
        squares[k], squares[4 + k] = over(piece, body, (squares[k], squares[4 + k]))

    def packed(values):
        row = zero
        for i, value in enumerate(values):
            row = jnp.where((lane == i) & top, jnp.sum(value), row)
        return row

    message[pl.ds(0, 8)] = packed(squares)
    message[pl.ds(8, 8)] = zero
    message[pl.ds(8, 3)] = small[pl.ds(0, 3)]
    side = 2 * WS - 1
    cell = lax.broadcasted_iota(jnp.int32, (128, 384), 0)
    spot = lax.broadcasted_iota(jnp.int32, (128, 384), 1)
    put = ((cell // WS) * side + lax.rem(cell, WS) == spot) & (cell < WS * WS)
    wide = jnp.dot(bias_sum[...], put.astype(F32), precision=HIGH, preferred_element_type=F32)
    middle = (WS - 1) * side + WS - 1
    column = jnp.zeros((1, 384), F32)
    for j in range(WS * WS):
        shift = middle - (j // WS) * side - j % WS
        column = column + pltpu.roll(wide[j : j + 1], shift, axis=1)
    for b in range(3):
        message[pl.ds(11 + b, 1)] = column[:, 128 * b : 128 * b + 128]
    for i in range(2):
        line = jnp.sum(leave_sums[i], axis=0, keepdims=True)
        for b in range(8):
            message[pl.ds(16 + 8 * i + b, 1)] = line[:, 128 * b : 128 * b + 128]

    events, end = gather_events(place, message, got)
    for event in sorted(events, key=lambda e: e[0]):
        event[1]()
    end[1]()

    place_of = lambda d: (d // 8, (d // 4) % 2, (d // 2) % 2, d % 2)
    found = functools.reduce(jnp.add, [got[place_of(d) + (pl.ds(0, 8),)] for d in range(devices)])
    late = functools.reduce(jnp.add, [got[place_of(d) + (pl.ds(16, 16),)] for d in range(devices)])
    for i in range(2):
        for b in range(8):
            vec_grad[pl.ds(i, 1), pl.ds(128 * b, 128)] = late[8 * i + b : 8 * i + b + 1] * scale
    for d in range(devices):
        block = got[place_of(d) + (pl.ds(8, 8),)] * scale
        q, b = d % 4, d // 4
        rows = block[:3] if q else block[2:3]
        vec_grad[pl.ds(3 * q if q else 2, rows.shape[0]), pl.ds(128 * b, 128)] = rows
        for j in range(3):
            heads_grad[pl.ds(d, 1), pl.ds(128 * j, 128)] = block[3 + j : 4 + j]
    entries = table.shape[0]
    small_grad = vec_grad[...]
    table_grad = heads_grad[...].T[:entries]

    total = lambda value: jnp.sum(value, keepdims=True)
    scalar = lambda k: total(jnp.where(top & (lane == k), found, 0.0))
    grad_square = scalar(0) + scalar(1) + scalar(2) + scalar(3)
    clip_norm = jnp.sqrt(
        grad_square + total(small_grad * small_grad) + total(table_grad * table_grad)
    )
    factor = jnp.minimum(1.0, CLIP_LIMIT / clip_norm)

    def moments(grad, first, second, weight):
        clipped = grad * factor
        first_new = MOMENT_ONE * first + (1.0 - MOMENT_ONE) * clipped
        second_new = MOMENT_TWO * second + (1.0 - MOMENT_TWO) * clipped * clipped
        update = (first_new * (1.0 / (1.0 - MOMENT_ONE**step_number))) / (
            jnp.sqrt(second_new * (1.0 / (1.0 - MOMENT_TWO**step_number))) + ADAM_EPS
        ) + DECAY * weight
        return first_new, second_new, update

    squares = [zero] * 4
    for piece in pieces:

        def body(k, at, source, carry):
            first, second, change = moments(
                grads_out[k][at], firsts[k][at], seconds[k][at], masters[k][at]
            )
            firsts_out[k][at] = first
            seconds_out[k][at] = second
            news_out[k][at] = change
            return carry + fold(change * change)

        squares[piece[0]] = over(piece, body, squares[piece[0]])
    message_two[pl.ds(0, 8)] = packed(squares)
    message_two[pl.ds(8, 8)] = zero

    events, end = gather_events(place, message_two, got_two)
    events = [event for _, event in sorted(events, key=lambda e: e[0])]
    events[0]()

    first, second, change = moments(small_grad, vec_first[...], vec_second[...], vec[...])
    rows = lambda value: jnp.sqrt(jnp.sum(value * value, axis=1, keepdims=True))
    vec_out[0][...] = small_grad
    vec_out[1][...] = first
    vec_out[2][...] = second
    vec_out[3][...] = vec[...] - LEARN_RATE * (rows(vec[...]) / rows(change)) * change
    first, second, change = moments(table_grad, table_first[...], table_second[...], table[...])
    table_out[0][...] = table_grad
    table_out[1][...] = first
    table_out[2][...] = second
    ratio = jnp.sqrt(total(table[...] * table[...])) / jnp.sqrt(total(change * change))
    table_out[3][...] = table[...] - LEARN_RATE * ratio * change

    for event in events[1:]:
        event()
    end[1]()
    second_found = functools.reduce(
        jnp.add, [got_two[place_of(d) + (pl.ds(0, 8),)] for d in range(devices)]
    )
    norms = jnp.where(top & (lane == 8), clip_norm, 0.0)
    for k in range(4):
        weight_norm = jnp.sqrt(scalar(4 + k))
        update_norm = jnp.sqrt(total(jnp.where(top & (lane == k), second_found, 0.0)))
        norms = jnp.where(top & (lane == k), weight_norm, norms)
        norms = jnp.where(top & (lane == 4 + k), update_norm, norms)
        ratio = LEARN_RATE * (weight_norm / update_norm)
        for piece in pieces:
            if piece[0] != k:
                continue

            def body(k, at, source, carry):
                fresh = masters[k][at] - ratio * news_out[k][at]
                news_out[k][at] = fresh
                copies_out[k][at] = fresh.astype(BF)
                return carry

            over(piece, body, 0)
    norms_out[...] = norms


def update(nz, collective, inverse, leave_sums, bias_sum, small, pieces, masters, firsts, seconds, vectors, tables):
    vmem = pl.BlockSpec(memory_space=pltpu.VMEM)
    ins = [inverse, leave_sums, bias_sum, small] + [p[3] for p in pieces]
    ins += list(masters) + list(firsts) + list(seconds) + list(vectors) + list(tables)
    like = lambda arrays, dtype=F32: [struct(a.shape, dtype) for a in arrays]
    outs = like(masters) * 4 + like(masters, BF)
    outs += [struct(vectors[0].shape, F32)] * 4 + [struct(tables[0].shape, F32)] * 4
    outs += [struct((8, 128), F32)]
    made = pl.pallas_call(
        functools.partial(update_kernel, nz, [p[:3] for p in pieces], STEP),
        name="update",
        out_shape=outs,
        in_specs=[pl.BlockSpec(memory_space=pltpu.SMEM)] + [vmem] * (len(ins) - 1),
        out_specs=[vmem] * len(outs),
        scratch_shapes=[
            pltpu.VMEM((32, 128), F32),
            pltpu.VMEM((nz, 2, 2, 2, 32, 128), F32),
            pltpu.VMEM((16, 128), F32),
            pltpu.VMEM((nz, 2, 2, 2, 16, 128), F32),
            pltpu.VMEM(vectors[0].shape, F32),
            pltpu.VMEM((nz * 8, 384), F32),
            pltpu.SemaphoreType.DMA((2 * gather_sems(nz),)),
        ],
        compiler_params=pltpu.CompilerParams(
            collective_id=collective, has_side_effects=True, vmem_limit_bytes=VMEM_LIMIT
        ),
    )(*ins)
    matrices = [[made[4 * j + k] for j in range(5)] for k in range(4)]
    norms = made[-1]
    return matrices, made[20:24], made[24:28], norms[0, 8], norms[0, :8].reshape(2, 4)


def local(
    ndp,
    nfs,
    patches,
    cotangent,
    pad_mask,
    attend_weight,
    attend_first,
    attend_second,
    output_weight,
    output_first,
    output_second,
    expand_weight,
    expand_first,
    expand_second,
    shrink_weight,
    shrink_first,
    shrink_second,
    vector_params,
    vector_first,
    vector_second,
    position_table,
    table_first,
    table_second,
):
    windows, cells, width = patches.shape
    keep = pad_mask.astype(jnp.float32)
    local_count = jnp.sum(keep)
    devices = ndp * nfs
    nz = ndp // 2
    shard_rows = min(attend_weight.shape[0], shrink_weight.shape[0])
    direct = nfs == 4 and devices == HEADS and shard_rows % 32 == 0
    masters = (attend_weight, output_weight, expand_weight, shrink_weight)
    part_rows = shrink_weight.shape[0] // 2

    def with_moves(collective, step_us, *moves):
        if not direct:
            return {}
        return dict(moves=moves, nz=nz, collective=collective, step_us=step_us)

    def gathered(k, made):
        if direct:
            return made.reshape(-1, made.shape[-1])
        return lax.all_gather(masters[k].astype(BF), AXES, axis=0, tiled=True)

    def parts(grad):
        return grad.reshape(nz, 2, 2, 2, -1, grad.shape[-1])

    def scattered(grad):
        return lax.psum_scatter(grad.astype(F32), AXES, scatter_dimension=0, tiled=True)

    high = -(-cells // 8) * 8
    keep_rows = jnp.pad(keep, ((0, 0), (0, high - cells)))[:, :, None]
    keep_rows = jnp.broadcast_to(keep_rows, (windows, high, 128))
    there = (jnp.arange(high) < cells)[None, :, None]
    mask = jnp.where(there, (keep_rows - 1.0) * MASK_FILL, -1e30)
    relative = position_table.shape[0]
    index = jnp.pad(position_index(WS).T, ((0, high - cells), (0, 128 - cells)), constant_values=-1)
    onehot = (
        index.reshape(-1)[None, :] == jnp.arange(relative, dtype=jnp.int32)[:, None]
    ).astype(BF)
    terms, rest = [], position_table.T
    for _ in range(3):
        term = lax.reduce_precision(rest, 8, 7)
        terms.append(term.astype(BF))
        rest = rest - term
    bias = times(jnp.concatenate(terms), onehot).reshape(3, -1, high, 128)
    bias = bias[0] + bias[1] + bias[2]
    expand_bias = vector_params[8:].reshape(1, -1)
    (hidden_one, source, upstream, shrink_sum), made = enter(
        patches,
        cotangent,
        keep_rows,
        vector_params,
        **with_moves(
            1,
            1.5,
            ("gather", 0.0, F32, jnp.full((16, 128), local_count, F32)),
            ("gather", 0.0, BF, attend_weight),
        ),
    )
    made = made or (None,) * 2
    if direct:
        total = jnp.sum(made[0][..., 0, 0])
    else:
        total = lax.psum(local_count, AXES)
    w_attend = gathered(0, made[1])
    (query, keys, values, probs, attended), made = attend(
        hidden_one,
        w_attend,
        vector_params,
        bias,
        mask,
        **with_moves(
            2, 3.2, ("gather", 0.0, BF, output_weight), ("gather", 8.0, BF, expand_weight)
        ),
    )
    made = made or (None,) * 2
    w_output, w_expand = gathered(1, made[0]), gathered(2, made[1])
    (middle, hidden_t, activated, slope, grad_shrink), made = expand(
        attended,
        source,
        upstream,
        w_output,
        w_expand,
        vector_params,
        expand_bias,
        **with_moves(3, 4.9, ("gather", 0.0, BF, shrink_weight)),
    )
    made = made or (None,)
    w_shrink = gathered(3, made[0])
    (block_out, grad_before, grad_expand_bias, grad_expand), made = shrink(
        activated,
        slope,
        w_shrink,
        upstream,
        hidden_t,
        middle,
        vector_params,
        windows,
        cells,
        **with_moves(4, 4.0, ("scatter", 0.0, (0, part_rows), parts(grad_shrink))),
    )
    made = made or (None,)
    shrink_low = made[0]
    (grad_middle, grad_output, dout, inner_sums), made = inner(
        grad_before,
        w_expand,
        middle,
        upstream,
        attended,
        w_output,
        vector_params,
        windows,
        **with_moves(5, 3.7, ("scatter", 0.0, (part_rows, part_rows), parts(grad_shrink))),
    )
    made = made or (None,)
    shrink_high = made[0]
    (joint, grad_attend, grad_bias, joint_sums), made = unattend(
        query,
        keys,
        values,
        dout,
        probs,
        hidden_one,
        **with_moves(
            6,
            3.2,
            ("scatter", 0.0, (0, expand_weight.shape[0]), parts(grad_expand)),
            ("scatter", 8.0, (0, output_weight.shape[0]), parts(grad_output)),
        ),
    )
    made = made or (None,) * 2
    expand_owned, output_owned = made
    inner_rows = jnp.sum(inner_sums, axis=1)
    vector_local = jnp.concatenate(
        [
            jnp.zeros((2, width), F32),
            joint_sums[:, :width],
            joint_sums[:, 2 * width :],
            inner_rows[2:3],
            inner_rows[:2],
            jnp.sum(shrink_sum, axis=0, keepdims=True),
            grad_expand_bias.reshape(-1, width),
        ],
        axis=0,
    )
    moves = ()
    if direct:
        small = vector_local.astype(BF).reshape(4, -1, 8, 128).transpose(2, 0, 1, 3)
        small = small.reshape(devices, -1, 128)
        small = jnp.pad(small, ((0, 0), (0, 32 - small.shape[1]), (0, 0)))
        moves = (
            ("scatter", 0.0, (0, attend_weight.shape[0]), parts(grad_attend)),
            ("scatter", 1.0, (0, 32), small.reshape(nz, 2, 2, 2, 32, 128)),
            ("scatter", 1.0, (0, 128), grad_bias.reshape(nz, 2, 2, 2, 128, 128)),
        )
    inverse = (1.0 / total).reshape(1, 1)
    (input_grad, leave_sums), made = leave(
        joint,
        w_attend,
        source,
        grad_middle,
        vector_params,
        inverse,
        windows,
        cells,
        **with_moves(7, 3.3, *moves),
    )
    firsts = (attend_first, output_first, expand_first, shrink_first)
    seconds = (attend_second, output_second, expand_second, shrink_second)
    if direct:
        attend_owned, small_owned, bias_owned = made
        pieces = [
            (0, 0, attend_weight.shape[0], attend_owned),
            (1, 0, output_weight.shape[0], output_owned),
            (2, 0, expand_weight.shape[0], expand_owned),
            (3, 0, part_rows, shrink_low),
            (3, part_rows, part_rows, shrink_high),
        ]
        matrices, vector_outs, table_outs, clip_norm, matrix_norms = update(
            nz,
            8,
            inverse,
            leave_sums,
            bias_owned,
            small_owned,
            pieces,
            masters,
            firsts,
            seconds,
            (vector_params, vector_first, vector_second),
            (position_table, table_first, table_second),
        )
        outs = [block_out, input_grad]
        for matrix in matrices:
            outs += matrix
        return (*outs, *vector_outs, *table_outs, clip_norm, matrix_norms)
    owned = [
        scattered(g) for g in (grad_attend, grad_output, grad_expand, grad_shrink)
    ]
    grad_table = lax.dot_general(
        onehot.astype(F32),
        grad_bias[:, :high].astype(F32).reshape(HEADS, -1),
        (((1,), (1,)), ((), ())),
        precision=HIGH,
    )
    vector_local = vector_local.at[:2].set(jnp.sum(leave_sums, axis=1))
    vector_sum, table_sum = lax.psum((vector_local, grad_table), AXES)
    vector_grad, table_grad = vector_sum / total, table_sum / total
    matrix_grads = tuple((g / total for g in owned))
    grad_squares = jnp.stack([jnp.sum(g * g) for g in matrix_grads])
    weight_squares = jnp.stack([jnp.sum(m * m) for m in masters])
    grad_total, weight_total = lax.psum((grad_squares, weight_squares), AXES)
    clip_norm = jnp.sqrt(
        jnp.sum(grad_total) + jnp.sum(vector_grad * vector_grad) + jnp.sum(table_grad * table_grad)
    )
    factor = jnp.minimum(1.0, CLIP_LIMIT / clip_norm)
    sectioned = [
        moments(matrix_grads[k], firsts[k], seconds[k], masters[k], factor) for k in range(4)
    ]
    update_squares = jnp.stack([jnp.sum(s[2] * s[2]) for s in sectioned])
    update_total = lax.psum(update_squares, AXES)
    weight_norms = jnp.sqrt(weight_total)
    update_norms = jnp.sqrt(update_total)
    matrix_outs = []
    for k in range(4):
        fresh = masters[k] - LEARN_RATE * (weight_norms[k] / update_norms[k]) * sectioned[k][2]
        matrix_outs.append(
            (matrix_grads[k], sectioned[k][0], sectioned[k][1], fresh, fresh.astype(jnp.bfloat16))
        )
    vec_first, vec_second, vec_update = moments(
        vector_grad, vector_first, vector_second, vector_params, factor
    )
    vec_ratio = jnp.sqrt(jnp.sum(vector_params * vector_params, axis=1, keepdims=True)) / jnp.sqrt(
        jnp.sum(vec_update * vec_update, axis=1, keepdims=True)
    )
    vec_fresh = vector_params - LEARN_RATE * vec_ratio * vec_update
    tab_first, tab_second, tab_update = moments(
        table_grad, table_first, table_second, position_table, factor
    )
    tab_ratio = jnp.sqrt(jnp.sum(position_table * position_table)) / jnp.sqrt(
        jnp.sum(tab_update * tab_update)
    )
    tab_fresh = position_table - LEARN_RATE * tab_ratio * tab_update
    matrix_norms = jnp.stack([weight_norms, update_norms])
    attend_o, output_o, expand_o, shrink_o = matrix_outs
    return (
        block_out,
        input_grad,
        attend_o[0],
        attend_o[1],
        attend_o[2],
        attend_o[3],
        attend_o[4],
        output_o[0],
        output_o[1],
        output_o[2],
        output_o[3],
        output_o[4],
        expand_o[0],
        expand_o[1],
        expand_o[2],
        expand_o[3],
        expand_o[4],
        shrink_o[0],
        shrink_o[1],
        shrink_o[2],
        shrink_o[3],
        shrink_o[4],
        vector_grad,
        vec_first,
        vec_second,
        vec_fresh,
        table_grad,
        tab_first,
        tab_second,
        tab_fresh,
        clip_norm,
        matrix_norms,
    )


def solution(mesh):
    in_specs = (
        P(("dp", "fsdp"), None, None),
        P(("dp", "fsdp"), None, None),
        P(("dp", "fsdp"), None),
        P(("dp", "fsdp"), None),
        P(("dp", "fsdp"), None),
        P(("dp", "fsdp"), None),
        P(("dp", "fsdp"), None),
        P(("dp", "fsdp"), None),
        P(("dp", "fsdp"), None),
        P(("dp", "fsdp"), None),
        P(("dp", "fsdp"), None),
        P(("dp", "fsdp"), None),
        P(("dp", "fsdp"), None),
        P(("dp", "fsdp"), None),
        P(("dp", "fsdp"), None),
        P(),
        P(),
        P(),
        P(),
        P(),
        P(),
    )
    out_specs = (
        P(("dp", "fsdp"), None, None),
        P(("dp", "fsdp"), None, None),
        P(("dp", "fsdp"), None),
        P(("dp", "fsdp"), None),
        P(("dp", "fsdp"), None),
        P(("dp", "fsdp"), None),
        P(("dp", "fsdp"), None),
        P(("dp", "fsdp"), None),
        P(("dp", "fsdp"), None),
        P(("dp", "fsdp"), None),
        P(("dp", "fsdp"), None),
        P(("dp", "fsdp"), None),
        P(("dp", "fsdp"), None),
        P(("dp", "fsdp"), None),
        P(("dp", "fsdp"), None),
        P(("dp", "fsdp"), None),
        P(("dp", "fsdp"), None),
        P(("dp", "fsdp"), None),
        P(("dp", "fsdp"), None),
        P(("dp", "fsdp"), None),
        P(("dp", "fsdp"), None),
        P(("dp", "fsdp"), None),
        P(),
        P(),
        P(),
        P(),
        P(),
        P(),
        P(),
        P(),
        P(),
        P(),
    )
    sizes = (mesh.shape["dp"], mesh.shape["fsdp"])
    return jax.shard_map(functools.partial(local, *sizes), mesh=mesh, in_specs=in_specs, out_specs=out_specs, check_vma=False)
```

time: 728 us -> 522 us (0.72)
  matrix products: 205 us -> 3.85 us
  Pallas kernels: 311 us -> 460 us
  local copies, waits for them, and re-layouts: 117 us -> 44.8 us
  other arithmetic: 72.6 us -> 5.1 us
  between operations: 11.8 us -> 1.98 us
    dot_general x19 -> x1, matrix products: 193 us -> 3.85 us  [times(): return jnp.dot(left, right, preferred_element_type=jnp.float32)]
    pallas_call x5 -> x8, Pallas kernels: 311 us -> 460 us  [the longest x7 423 us: call(): pl.pallas_call(kernel, name=name, grid=(steps,), out_shape=outs, in_specs...]
    reduce_sum x25 -> x3, other arithmetic: 48 us -> 1.6 us  [the longest x1 1.54 us: local(): total = jnp.sum(made[0][..., 0, 0])]
    convert_element_type x17 -> x1, local copies, waits for them, and re-layouts: 40 us -> 0.01 us  [local(): small = vector_local.astype(BF).reshape(4, -1, 8, 128).transpose(2, 0, 1, 3)]
    reshape x15 -> x0, local copies, waits for them, and re-layouts: 35.1 us -> none  [the longest x1 5.15 us: local(): grad_attended = times_transpose(grad_branch, w_output).astype(jnp.bfloat1...]
    unnamed x169 -> x110, local copies, waits for them, and re-layouts: 20.6 us -> 39.2 us
    sub x1 -> x0, matrix products: 11.2 us -> none  [local(): probs = jax.nn.softmax(scores, axis=-1)]
    convert_element_type x6 -> x1, other arithmetic: 9.67 us -> 0.82 us  [local(): terms.append(term.astype(BF))]
where the time goes in v2:
time: 522 us; the launch traced here: 516 us
  Pallas kernels  460 us (88%)
  local copies, waits for them, and re-layouts  44.8 us (9%)
    pallas_call x7, Pallas kernels, call(): pl.pallas_call(kernel, name=name, grid=(steps,), out_shape=outs, in_specs...  423 us
    unnamed x110, local copies, waits for them, and re-layouts  39.2 us
    pallas_call x1, Pallas kernels, update(): pl.pallas_call(functools.partial(update_kernel, nz, [p[:3] for p in piece...  37.6 us

profile of v2, /device:TPU:0, one launch (start us, length us, event | category | flops | bytes accessed | tf_op | source)
XLA Modules:
  0.0 516.2 jit_solution(15681339271796926733)
XLA Ops:
  0.8 0.8 reduce-precision_convert_fusion.1
  1.6 3.8 fusion
  5.7 1.5 copy.65
  7.3 0.9 broadcast_in_dim.36.refs_2_
  8.2 2.1 copy.53.refs_0_
  10.3 2.2 copy.54.refs_1_
  13.0 1.2 broadcast_in_dim.37.refs_4_
  14.3 47.2 %enter.1 = (bf16[832,1024]{1,0:T(8,128)(2,1)}, bf16[832,1024]{1,0:T(8,128)(2,1)}, bf16[832,1024]{1,0:T(8,128)(2,1)}, f32[8,1024]{1,0:T(8,128)}, f32[4,2,2,2,16,1...) custom-call(bf16[8,100,1024]{2,1,0:T(8,128)(2,1)} %copy.53.refs_0_, bf16[8,100,1024]{2,1,0:T(8,128)(2,1)} %copy.54.refs_1_, ...), custom_call_target="tpu_custom_call" | custom-call | tf_op jit(solution)/shard_map/enter/pallas_call | solution.py:441
  61.5 0.9 broadcast_select_fusion.refs_6_
  62.4 71.1 %attend.1 = (bf16[8,104,1024]{2,1,0:T(8,128)(2,1)}, bf16[8,104,1024]{2,1,0:T(8,128)(2,1)}, bf16[8,104,1024]{2,1,0:T(8,128)(2,1)}, bf16[8,32,104,128]{3,2,1,0:T(8...) custom-call(bf16[832,1024]{1,0:T(8,128)(2,1)} %get-tuple-element.101, ...), custom_call_target="tpu_custom_call" | custom-call | tf_op jit(solution)/shard_map/attend/pallas_call | solution.py:441
  133.6 0.8 slice_bitcast_fusion
  134.9 51.8 %expand.1 = (f32[832,1024]{1,0:T(8,128)}, bf16[1024,832]{1,0:T(8,128)(2,1)}, bf16[832,4096]{1,0:T(8,128)(2,1)}, bf16[832,4096]{1,0:T(8,128)(2,1)}, bf16[4096,102...) custom-call(bf16[832,1024]{1,0:T(8,128)(2,1)} %get-tuple-element.103.refs_0_.refs_4_, ...), custom_call_target="tpu_custom_call" | custom-call | tf_op jit(solution)/shard_map/expand/pallas_call | solution.py:441
  186.8 47.7 %shrink.1 = (bf16[8,100,1024]{2,1,0:T(8,128)(2,1)}, bf16[832,4096]{1,0:T(8,128)(2,1)}, f32[1,4096]{1,0:T(1,128)}, bf16[1024,4096]{1,0:T(8,128)(2,1)}, f32[64,1024]{1,0:T(8,128)}) custom-call(bf16[832,4096]{1,0:T(8,128)(2,1)} %get-tuple-element.108.refs_0_, bf16[832,4096]{1,0:T(8,128)(2,1)} %get-tuple-element.109.refs_1_, bf16[4096,1024]{1,0:T(8,128)(2,1)} %bitcast.46, ...), custom_call_target="tpu_custom_call" | custom-call | tf_op jit(solution)/shard_map/shrink/pallas_call | solution.py:441
  234.4 48.1 %inner.1 = (f32[832,1024]{1,0:T(8,128)}, bf16[1024,1024]{1,0:T(8,128)(2,1)}, bf16[8,104,1024]{2,1,0:T(8,128)(2,1)}, f32[3,8,1024]{2,1,0:T(8,128)}, f32[64,1024]{1,0:T(8,128)}) custom-call(bf16[832,4096]{1,0:T(8,128)(2,1)} %get-tuple-element.118.refs_0_, bf16[1024,4096]{1,0:T(8,128)(2,1)} %bitcast.40, f32[832,1024]{1,0:T(8,128)} %get-tuple-element.112.refs_5_.refs_2_, ...), custom_call_target="tpu_custom_call" | custom-call | tf_op jit(solution)/shard_map/inner/pallas_call | solution.py:441
  282.5 95.2 %unattend.1 = (bf16[832,3072]{1,0:T(8,128)(2,1)}, bf16[1024,3072]{1,0:T(8,128)(2,1)}, bf16[32,128,128]{2,1,0:T(8,128)(2,1)}, f32[1,3072]{1,0:T(1,128)}, f32[32,4096]{1,0:T(8,128)}, /*index=5*/f32[32,1024]{1,0:T(8,128)}) custom-call(bf16[8,104,1024]{2,1,0:T(8,128)(2,1)} %get-tuple-element.115.refs_0_, bf16[8,104,1024]{2,1,0:T(8,128)(2,1)} %get-tuple-element.116.refs_1_, ...), custom_call_target="tpu_custom_call" | custom-call | tf_op jit(solution)/shard_map/unattend/pallas_call | solution.py:441
  377.7 0.7 convert.22
  378.8 0.7 pad.14
  379.5 1.5 slice_reduce_fusion
  381.8 61.9 %leave.1 = (f32[8,100,1024]{2,1,0:T(8,128)}, f32[2,8,1024]{2,1,0:T(8,128)}, f32[32,3072]{1,0:T(8,128)}, f32[32,128]{1,0:T(8,128)}, f32[128,128]{1,0:T(8,128)}) custom-call(bf16[832,3072]{1,0:T(8,128)(2,1)} %get-tuple-element.123.refs_0_, bf16[1024,3072]{1,0:T(8,128)(2,1)} %bitcast.38, bf16[832,1024]{1,0:T(8,128)(2,1)} %get-tuple-element.104.refs_1_.refs_2_, ...), custom_call_target="tpu_custom_call" | custom-call | tf_op jit(solution)/shard_map/leave/pallas_call | solution.py:441
  443.7 0.8 copy.56.refs_24_
  444.5 0.8 copy.57.refs_25_
  445.3 0.8 copy.58.refs_26_
  446.1 37.6 %update.1 = (f32[32,3072]{1,0:T(8,128)}, f32[32,1024]{1,0:T(8,128)}, f32[32,4096]{1,0:T(8,128)}, f32[128,1024]{1,0:T(8,128)}, f32[32,3072]{1,0:T(8,128)}, /*inde...) custom-call(f32[1,1]{1,0:T(1,128)} %bitcast.9.refs_5_.refs_0_, ...), custom_call_target="tpu_custom_call" | custom-call | tf_op jit(solution)/shard_map/update/pallas_call | solution.py:1187
  483.7 1.7 copy.61
  485.3 1.7 copy.62
  487.0 1.7 copy.63
  488.6 1.7 copy.64
  490.3 0.7 slice_reduce_fusion.1
  491.6 1.3 slice.49
  492.9 3.6 copy.60
  496.5 2.1 copy.59
  498.6 0.7 copy.92
  499.3 0.7 copy.93
  500.1 0.7 copy.94
  500.8 0.7 copy.95
  501.6 0.7 copy.96
  502.9 0.7 copy.98
  503.6 0.7 copy.99
  505.5 0.8 copy.102
  506.3 0.8 copy.103
  507.1 0.8 copy.104
  507.9 0.8 copy.105
  508.7 0.7 copy.106
  509.4 0.8 copy.107
  510.3 0.8 copy.108
  511.1 0.8 copy.109
  511.9 0.8 copy.110
  512.7 0.7 copy.111
  (100 shorter events, 7.1 us)
Async XLA Ops:
  5.7 1.5 copy-start.34
  5.7 2.5 copy-start.2
  7.2 3.0 copy-start.3
  282.5 96.0 %copy-start.24 = (f32[3,8,1024]{2,1,0:T(8,128)S(1)}, f32[3,8,1024]{2,1,0:T(8,128)}, u32[]{:S(2)}) copy-start(f32[3,8,1024]{2,1,0:T(8,128)} %get-tuple-element.128) | copy-start | bytes 294916
  282.5 96.0 %copy-start.33 = (f32[1,4096]{1,0:T(1,128)S(1)}, f32[1,4096]{1,0:T(1,128)}, u32[]{:S(2)}) copy-start(f32[1,4096]{1,0:T(1,128)} %get-tuple-element.130) | copy-start | bytes 49156
  282.5 96.1 %copy-start.32 = (f32[8,1024]{1,0:T(8,128)S(1)}, f32[8,1024]{1,0:T(8,128)}, u32[]{:S(2)}) copy-start(f32[8,1024]{1,0:T(8,128)} %get-tuple-element.129) | copy-start | bytes 98308
  381.8 61.9 %copy-start.19 = (f32[361,32]{0,1:T(8,128)S(1)}, f32[361,32]{0,1:T(8,128)}, u32[]{:S(2)}) copy-start(f32[361,32]{0,1:T(8,128)} %param.39) | copy-start | bytes 138628
  381.8 62.7 %copy-start.30 = (f32[361,32]{0,1:T(8,128)S(1)}, f32[361,32]{0,1:T(8,128)}, u32[]{:S(2)}) copy-start(f32[361,32]{0,1:T(8,128)} %param.40) | copy-start | bytes 138628
  381.8 63.5 %copy-start.31 = (f32[361,32]{0,1:T(8,128)S(1)}, f32[361,32]{0,1:T(8,128)}, u32[]{:S(2)}) copy-start(f32[361,32]{0,1:T(8,128)} %param.41) | copy-start | bytes 138628
  446.1 46.8 %copy-start = (f32[8,100,1024]{2,1,0:T(8,128)S(1)}, f32[8,100,1024]{2,1,0:T(8,128)}, u32[]{:S(2)}) copy-start(f32[8,100,1024]{2,1,0:T(8,128)} %get-tuple-element.171) | copy-start | bytes 9830404
  492.9 3.6 copy-start.1
  496.5 2.1 copy-start.15
  496.5 2.9 copy-start.14
  496.5 3.6 copy-start.13
  496.5 4.4 copy-start.12
  498.6 3.0 copy-start.18
  498.6 3.7 copy-start.23
  498.6 4.4 copy-start.22
  498.6 5.0 copy-start.21
  498.6 5.7 %copy-start.20 = (f32[32,1024]{1,0:T(8,128)S(1)}, f32[32,1024]{1,0:T(8,128)}, u32[]{:S(2)}) copy-start(f32[32,1024]{1,0:T(8,128)} %get-tuple-element.253) | copy-start | bytes 393220
  498.6 6.3 %copy-start.29 = (bf16[32,1024]{1,0:T(8,128)(2,1)S(1)}, bf16[32,1024]{1,0:T(8,128)(2,1)}, u32[]{:S(2)}) copy-start(bf16[32,1024]{1,0:T(8,128)(2,1)} %get-tuple-element.254) | copy-start | bytes 196612
  499.3 6.2 %copy-start.11 = (f32[32,4096]{1,0:T(8,128)S(1)}, f32[32,4096]{1,0:T(8,128)}, u32[]{:S(2)}) copy-start(f32[32,4096]{1,0:T(8,128)} %get-tuple-element.255) | copy-start | bytes 1572868
  500.1 6.2 %copy-start.10 = (f32[32,4096]{1,0:T(8,128)S(1)}, f32[32,4096]{1,0:T(8,128)}, u32[]{:S(2)}) copy-start(f32[32,4096]{1,0:T(8,128)} %get-tuple-element.256) | copy-start | bytes 1572868
  500.8 6.3 %copy-start.9 = (f32[32,4096]{1,0:T(8,128)S(1)}, f32[32,4096]{1,0:T(8,128)}, u32[]{:S(2)}) copy-start(f32[32,4096]{1,0:T(8,128)} %get-tuple-element.257) | copy-start | bytes 1572868
  502.3 5.7 %copy-start.8 = (f32[32,4096]{1,0:T(8,128)S(1)}, f32[32,4096]{1,0:T(8,128)}, u32[]{:S(2)}) copy-start(f32[32,4096]{1,0:T(8,128)} %get-tuple-element.258) | copy-start | bytes 1572868
  505.5 3.2 copy-start.17
  506.3 3.1 copy-start.7
  507.1 3.1 copy-start.6
  507.9 3.1 copy-start.5
  508.7 3.1 copy-start.4
  509.4 3.2 copy-start.16
  510.2 3.1 copy-start.28
  510.2 3.7 copy-start.27
  510.2 4.4 copy-start.26
  510.3 5.0 copy-start.25

commit v3 on v2

v3 whole, which is shorter than its diff:
```python
import functools

import jax
import jax.numpy as jnp
from jax import lax
from jax.experimental import pallas as pl
from jax.experimental.pallas import tpu as pltpu
from jax.sharding import PartitionSpec as P

MESH = pl.DeviceIdType.MESH
AXES = ("dp", "fsdp")
VMEM_LIMIT = 60 * 1024 * 1024

HEADS = 32
WS = 10
STEP = 10


EPSILON = 1e-05
MOMENT_ONE = 0.9
MOMENT_TWO = 0.999
LEARN_RATE = 0.3
DECAY = 0.01
ADAM_EPS = 1e-06
CLIP_LIMIT = 0.05
MASK_FILL = 10000.0
HIGH = lax.Precision.HIGHEST
BF, F32 = jnp.bfloat16, jnp.float32


def position_index(size):
    cells = jnp.arange(size * size, dtype=jnp.int32)
    rows = cells // size
    cols = cells % size
    drow = rows[:, None] - rows[None, :] + size - 1
    dcol = cols[:, None] - cols[None, :] + size - 1
    return drow * (2 * size - 1) + dcol


def moments(grad, first, second, weight, factor):
    clipped = grad * factor
    first_new = MOMENT_ONE * first + (1.0 - MOMENT_ONE) * clipped
    second_new = MOMENT_TWO * second + (1.0 - MOMENT_TWO) * clipped * clipped
    update = (
        first_new
        / (1.0 - MOMENT_ONE**STEP)
        / (jnp.sqrt(second_new / (1.0 - MOMENT_TWO**STEP)) + ADAM_EPS)
        + DECAY * weight
    )
    return (first_new, second_new, update)


def whole(shape):
    zeros = (0,) * len(shape)
    return pl.BlockSpec(shape, lambda *s: zeros, pipeline_mode=pl.Buffered(1))


def whole_out(shape):
    zeros = (0,) * len(shape)
    return pl.BlockSpec(shape, lambda *s: zeros, pipeline_mode=pl.Buffered(1))


def struct(shape, dtype):
    return jax.ShapeDtypeStruct(shape, dtype)


class Place:
    def __init__(self, sems):
        dp = lax.axis_index("dp")
        fsdp = lax.axis_index("fsdp")
        self.z, self.x = dp // 2, dp % 2
        self.y, self.c = fsdp // 2, fsdp % 2
        self.mate = self.z + 1 - 2 * lax.rem(self.z, 2)
        self.far = lax.rem(self.z + 2, 4)
        self.cross = 3 - self.z
        self.inner = (self.z == 1) | (self.z == 2)
        self.pair = 2 * (self.z // 2)
        self.sems = sems
        self.used = 0

    def sem(self):
        self.used += 1
        return self.sems.at[self.used - 1]

    def to(self, z=None, x=None, y=None, c=None):
        z = self.z if z is None else z
        x = self.x if x is None else x
        y = self.y if y is None else y
        c = self.c if c is None else c
        return (z * 2 + x, y * 2 + c)

    def peers(self):
        return [
            self.to(z=self.mate),
            self.to(z=self.far),
            self.to(z=self.cross),
            self.to(x=1 - self.x),
            self.to(y=1 - self.y),
            self.to(c=1 - self.c),
        ]

    def greet(self):
        barrier = pltpu.get_barrier_semaphore()
        peers = self.peers()
        for peer in peers:
            pl.semaphore_signal(barrier, inc=1, device_id=peer, device_id_type=MESH)
        pl.semaphore_wait(barrier, len(peers))

    def send(self, source, target, device, recv_sem=None):
        return pltpu.make_async_remote_copy(
            src_ref=source,
            dst_ref=target,
            send_sem=self.sem(),
            recv_sem=self.sem() if recv_sem is None else recv_sem,
            device_id=device,
            device_id_type=MESH,
        )

    def move(self, source, target):
        return pltpu.make_async_copy(source, target, self.sem())


def gather_sems(groups):
    return 1 + 2 * 5 + 2 * 5 * groups


def gather_events(place, own, out, groups, relay):
    z, x, y, c = place.z, place.x, place.y, place.c
    half = own.shape[0] // 2
    ox, oy, oc = 1 - x, 1 - y, 1 - c
    xp, yp, cp = place.to(x=ox), place.to(y=oy), place.to(c=oc)
    mate, cross = place.to(z=place.mate), place.to(z=place.cross)
    first = jnp.where(place.inner, place.cross, place.far)
    second = jnp.where(place.inner, place.far, place.cross)
    low, high = pl.ds(0, half), pl.ds(half, half)
    slot = lambda at: out.at[at, x, y, c]
    mine = place.move(own, slot(z))
    to_mate = place.send(own, slot(z), mate)
    if relay:
        came_one, came_two = place.sem(), place.sem()
        across_one = place.send(own, slot(z), cross, came_one)
        across_two = place.send(slot(place.mate), slot(place.mate), cross, came_two)
        on_one = place.send(slot(first), slot(first), mate, came_one)
        on_two = place.send(slot(second), slot(second), mate, came_two)
    else:
        to_far = place.send(own, slot(z), place.to(z=place.far))
        to_cross = place.send(own, slot(z), cross)
    if groups == 1:
        spans = [pl.ds(0, 4)]
    elif groups == 2:
        spans = [pl.ds(place.pair, 2), pl.ds(2 - place.pair, 2)]
    elif relay:
        spans = [pl.ds(at, 1) for at in (z, place.mate, first, second)]
    else:
        spans = [pl.ds(at, 1) for at in (z, place.mate, place.far, place.cross)]

    def forward(ref, device):
        return place.send(ref, ref, device)

    x_full = [forward(out.at[s, x, y, c], xp) for s in spans]
    y_full = [forward(out.at[s, x, y, c], yp) for s in spans]
    x_half = [forward(out.at[s, ox, y, c, low], yp) for s in spans]
    y_half = [forward(out.at[s, x, oy, c, high], xp) for s in spans]
    to_twin = [forward(out.at[s, :, :, c], cp) for s in spans]

    def begin():
        mine.start()
        to_mate.start()
        if relay:

            @pl.when(place.inner)
            def _():
                across_one.start()

        else:
            to_far.start()
            to_cross.start()
        mine.wait()
        if groups == 4:
            send_line(0)

    def send_line(g):
        x_full[g].start()
        y_full[g].start()

    def on_line():
        for copy in (to_mate, to_far, to_cross):
            copy.wait_recv()
        send_line(0)

    def on_place(g):
        (None, to_mate, to_far, to_cross)[g].wait_recv()
        send_line(g)

    def on_mate():
        to_mate.wait_recv()

        @pl.when(place.inner)
        def _():
            across_two.start()

        if groups == 2:
            send_line(0)
        if groups == 4:
            send_line(1)

    def relay_one():
        @pl.when(place.inner)
        def _():
            across_one.wait_recv()
            on_one.start()

    def on_first():
        @pl.when(jnp.logical_not(place.inner))
        def _():
            on_one.wait_recv()

        if groups == 4:
            send_line(2)

    def relay_two():
        @pl.when(place.inner)
        def _():
            across_two.wait_recv()
            on_two.start()

    def on_second():
        @pl.when(jnp.logical_not(place.inner))
        def _():
            on_two.wait_recv()

        send_line(groups - 1)

    def on_side(g):
        x_full[g].wait_recv()
        x_half[g].start()
        y_full[g].wait_recv()
        y_half[g].start()

    def on_corner(g):
        x_half[g].wait_recv()
        y_half[g].wait_recv()
        to_twin[g].start()

    def arrive():
        for copy in to_twin:
            copy.wait_recv()

    def finish():
        for copies in (to_twin, x_full, y_full, x_half, y_half, [to_mate]):
            for copy in copies:
                copy.wait_send()
        if relay:

            @pl.when(place.inner)
            def _():
                for copy in (across_one, across_two, on_one, on_two):
                    copy.wait_send()

        else:
            to_far.wait_send()
            to_cross.wait_send()

    size = 4 // groups
    lines = lambda g: [("x", size, ("xf", g)), ("y", size, ("yf", g))]
    if relay:
        one = {1: [], 2: [], 4: lines(0)}[groups]
        events = [
            (begin, [], [("z", 1, "mate"), ("w", 1, "a1")] + one),
            (on_mate, ["mate"], [("w", 1, "a2")] + {1: [], 2: lines(0), 4: lines(1 % groups)}[groups]),
            (relay_one, ["a1"], [("z", 1, "o1")]),
            (on_first, ["o1"], lines(2) if groups == 4 else []),
            (relay_two, ["a2"], [("z", 1, "o2")]),
            (on_second, ["o2"], lines(groups - 1)),
        ]
    elif groups == 4:
        events = [(begin, [], [("z", 1.33, ("z", g)) for g in (1, 2, 3)] + lines(0))]
        for g in (1, 2, 3):
            events.append((functools.partial(on_place, g), [("z", g)], lines(g)))
    else:
        events = [(begin, [], [("z", 4, "z")]), (on_line, ["z"], lines(0))]
    for g in range(groups):
        half_size = 0.5 * size
        halves = [("y", half_size, ("xh", g)), ("x", half_size, ("yh", g))]
        events.append((functools.partial(on_side, g), [("xf", g), ("yf", g)], halves))
    for g in range(groups):
        twins = [("c", size * 4, ("t", g))]
        events.append((functools.partial(on_corner, g), [("xh", g), ("yh", g)], twins))
    events.append((arrive, [("t", g) for g in range(groups)], []))
    return events, finish


def scatter_sems(groups):
    return groups * (1 + 2 * 5) + 2 * 3


def scatter_scratch(rows, columns):
    shape = lambda *lead: pltpu.VMEM(lead + (columns,), jnp.bfloat16)
    return [
        shape(4, 2, 2, rows),
        shape(4, 2, 2, rows),
        shape(4, rows // 2),
        shape(4, rows // 2),
        shape(4, rows),
        shape(4, rows),
        shape(3, rows),
    ]


def scatter_events(place, grads, part, total, scratch, groups):
    z, x, y, c = place.z, place.x, place.y, place.c
    held, twin, corner_low, corner_high, from_x, from_y, from_z = scratch
    rows, columns = total.shape
    half = rows // 2
    part = pl.ds(*part)
    ox, oy, oc = 1 - x, 1 - y, 1 - c
    xp, yp, cp = place.to(x=ox), place.to(y=oy), place.to(c=oc)
    if groups == 1:
        spans, lines = [(0, 4)], [[0, 1, 2, None]]
    elif groups == 2:
        spans = [(2 - place.pair, 2), (place.pair, 2)]
        lines = [[0, 1], [2, None]]
    else:
        spans = [(place.far, 1), (place.cross, 1), (place.mate, 1), (z, 1)]
        lines = [[0], [1], [2], [None]]
    ds = [pl.ds(*span) for span in spans]
    low, high = pl.ds(0, half), pl.ds(half, half)
    loads = [place.move(grads.at[d, :, :, c, part], held.at[d]) for d in ds]
    twins = [place.send(grads.at[d, :, :, oc, part], twin.at[d], cp) for d in ds]
    out_low = [place.send(held.at[d, ox, oy, low], corner_low.at[d], xp) for d in ds]
    out_high = [place.send(held.at[d, ox, oy, high], corner_high.at[d], yp) for d in ds]
    out_x = [place.send(held.at[d, ox, y], from_x.at[d], xp) for d in ds]
    out_y = [place.send(held.at[d, x, oy], from_y.at[d], yp) for d in ds]
    line = [place.far, place.cross, place.mate]
    out_z = [place.send(held.at[at, x, y], from_z.at[i], place.to(z=at)) for i, at in enumerate(line)]

    def summed(store, first, count, parts):
        def step(i, carry):
            at = pl.ds(pl.multiple_of(first + i * 16, 16), 16)
            store(at, functools.reduce(jnp.add, [part(at).astype(jnp.float32) for part in parts]))
            return carry

        lax.fori_loop(0, count // 16, step, 0)

    def read(ref, *index, lo=0):
        if lo:
            return lambda at: ref[index + (pl.ds(at.start - lo, 16),)]
        return lambda at: ref[index + (at,)]

    def write(ref, *index):
        def store(at, value):
            ref[index + (at,)] = value.astype(ref.dtype)

        return store

    def each(g, body):
        start, size = spans[g]

        def step(i, carry):
            body(start + i)
            return carry

        lax.fori_loop(0, size, step, 0)

    def begin():
        for g in range(len(spans)):
            twins[g].start()
            loads[g].start()

    def on_corner(g):
        loads[g].wait()
        twins[g].wait_recv()

        def body(at):
            here = (at, ox, oy)
            summed(write(held, *here), 0, rows, [read(held, *here), read(twin, *here)])

        each(g, body)
        out_low[g].start()
        out_high[g].start()

    def on_side(g):
        out_high[g].wait_recv()

        def body(at):
            here = (at, ox, y)
            own = [read(held, *here), read(twin, *here)]
            summed(write(held, *here), 0, half, own)
            summed(write(held, *here), half, half, own + [read(corner_high, at, lo=half)])

        each(g, body)
        out_x[g].start()
        out_low[g].wait_recv()

        def body(at):
            here = (at, x, oy)
            own = [read(held, *here), read(twin, *here)]
            summed(write(held, *here), half, half, own)
            summed(write(held, *here), 0, half, own + [read(corner_low, at)])

        each(g, body)
        out_y[g].start()

    def on_line(g):
        out_x[g].wait_recv()
        out_y[g].wait_recv()
        for i in lines[g]:
            at = z if i is None else line[i]
            here = (at, x, y)
            parts = [read(held, *here), read(twin, *here), read(from_x, at), read(from_y, at)]
            if i is None:
                for copy in out_z:
                    copy.wait_recv()
                parts += [read(from_z, j) for j in range(3)]
                summed(write(total), 0, rows, parts)
            else:
                summed(write(held, *here), 0, rows, parts)
                out_z[i].start()

    def finish():
        for copies in (twins, out_low, out_high, out_x, out_y, out_z):
            for copy in copies:
                copy.wait_send()

    size = 4 // groups
    events = [(begin, [], [("c", 4 * size, ("t", g)) for g in range(groups)])]
    for g in range(groups):
        halves = [("x", 0.5 * size, ("l", g)), ("y", 0.5 * size, ("h", g))]
        events.append((functools.partial(on_corner, g), [("t", g)], halves))
    for g in range(groups):
        fulls = [("x", size, ("x", g)), ("y", size, ("y", g))]
        events.append((functools.partial(on_side, g), [("l", g), ("h", g)], fulls))
    for g in range(groups):
        sent = [("z", 1.33, ("z", i)) for i in lines[g] if i is not None]
        waits = [("x", g), ("y", g)]
        if groups > 1 and g == groups - 1:
            waits += [("z", i) for i in range(2)]
        events.append((functools.partial(on_line, g), waits, sent))
    if groups == 4:
        events[-1][1].append(("z", 2))
    return events, finish


HOP = 2.5
LINK = 90e3
CORE = 500e3
BACKLOG = (0.5, 10.0)


def plan_of(lists, starts):
    free = {"x": 0.0, "y": 0.0, "z": 0.0, "w": 0.0, "c": 0.0}
    arrival, pending = {}, []
    for number, ((events, finish), move) in enumerate(lists):
        for order, (event, waits, sends) in enumerate(events):
            pending.append((number, order, event, [(number, w) for w in waits], sends, move))

    def ready(item):
        number, order, _, waits, _, move = item
        if any(w not in arrival for w in waits):
            return None
        if order:
            if any(p[0] == number and p[1] == 0 for p in pending):
                return None
        return max([arrival[w] for w in waits], default=0.0)

    def run(item, now):
        number, _, event, _, sends, move = item
        pending.remove(item)
        for link, units, name in sends:
            rate = CORE if link == "c" else LINK
            cores = 1 if link == "c" else 2
            took = units * cores * move["bytes"] / rate
            free[link] = max(free[link], now) + took
            arrival[number, name] = free[link] + HOP
        return event

    before, now = {}, 3.0
    for step in range(len(starts) + 1):
        last = step == len(starts)
        while True:
            found, forced_found = None, None
            top = min([p[0] for p in pending if p[5]["step"] <= step], default=0)
            pressed = any(p[5]["need"] is not None and p[5]["need"] <= step for p in pending)
            for item in pending:
                number, order, _, _, sends, move = item
                if move["step"] > step:
                    continue
                at = ready(item)
                if at is None:
                    continue
                if last or (move["need"] is not None and move["need"] <= step):
                    if forced_found is None or at < forced_found[0]:
                        forced_found = (at, item)
                elif number > top:
                    backlog = max((free[k] - now for k, _, _ in sends if k != "c"), default=0.0)
                    if backlog > BACKLOG[0 if pressed else 1]:
                        continue
                if at <= now and (found is None or number < found[1][0]):
                    found = (at, item)
            if found is None:
                found = forced_found
            if found is None:
                break
            now = max(now, found[0])
            before.setdefault(step, []).append(run(found[1], now))
        if not last:
            now += starts[step]
    after = before.pop(len(starts), [])
    assert not pending
    return before, after + [finish for (_, finish), _ in lists]


def gather(array, dtype, groups=4, relay=True, need=None, step=0, columns=None):
    columns = ((0, array.shape[1]),) if columns is None else columns
    shape = (array.shape[0], sum(n for _, n in columns))
    return dict(
        kind="gather",
        array=array,
        dtype=dtype,
        groups=groups,
        relay=relay,
        bytes=shape[0] * shape[1] * jnp.dtype(dtype).itemsize,
        need=need,
        step=step,
        columns=columns,
        shape=shape,
    )


def scatter(array, shape=None, groups=4, step=0):
    shape = array.shape[4:] if shape is None else shape
    size = 2 * shape[0] * shape[1]
    return dict(kind="scatter", array=array, shape=shape, groups=groups, bytes=size, need=None, step=step)


def fused_kernel(body, counts, moves, starts, *refs):
    n_in, n_out, n_scratch = counts
    numbers = []
    for move in moves:
        if isinstance(move["array"], int):
            numbers.append(None)
        else:
            same = [i for i, m in enumerate(moves) if m["array"] is move["array"]][0]
            known = numbers[same] if same < len(numbers) else None
            numbers.append(max([n for n in numbers if n is not None], default=-1) + 1 if known is None else known)
    n_given = max([n for n in numbers if n is not None], default=-1) + 1
    ins, given = refs[:n_in], list(refs[n_in : n_in + n_given])
    refs = refs[n_in + n_given :]
    outs, made = refs[:n_out], refs[n_out : n_out + len(moves)]
    refs = refs[n_out + len(moves) :]
    scratch, spare = refs[:n_scratch], list(refs[n_scratch:-1])
    step = pl.program_id(0)
    place = Place(refs[-1])
    lists, lows = [], []
    for move, target, number in zip(moves, made, numbers):
        source = scratch[move["array"]] if number is None else given[number]
        if move["kind"] == "gather":
            low = spare.pop(0)
            lows.append((source, low, move["columns"]))
            events = gather_events(place, low, target, move["groups"], move["relay"])
        else:
            buffers = [spare.pop(0) for _ in range(7)]
            rows = (0, move["shape"][0])
            events = scatter_events(place, source, rows, target, buffers, move["groups"])
        lists.append((events, move))
    before, after = plan_of(lists, starts)

    @pl.when(step == 0)
    def _():
        for source, low, columns in lows:
            put = 0
            for first, size in columns:
                low[:, put : put + size] = source[:, first : first + size].astype(low.dtype)
                put += size
        place.greet()

    for at in sorted(before):

        @pl.when(step == at)
        def _(events=before[at]):
            for event in events:
                event()

    body(made, *ins, *outs, *scratch)

    @pl.when(step == len(starts) - 1)
    def _():
        for event in after:
            event()


def call(body, name, steps, ins, in_specs, outs, out_specs, scratch=(), moves=(), collective=None, starts=()):
    scratch = list(scratch)
    params = dict(vmem_limit_bytes=VMEM_LIMIT)
    counts = (len(ins), len(outs), len(scratch))
    kernel = functools.partial(body, ())
    if moves:
        params.update(collective_id=collective, has_side_effects=True)
        kernel = functools.partial(fused_kernel, body, counts, moves, starts)
        assert len(starts) == steps
    ins, in_specs, outs, out_specs = list(ins), list(in_specs), list(outs), list(out_specs)
    sems = 0
    for move in moves:
        array = move["array"]
        if move["kind"] == "gather":
            if not any(array is other for other in ins[counts[0] :]):
                ins.append(array)
                in_specs.append(whole(array.shape))
            outs.append(struct((4, 2, 2, 2) + move["shape"], move["dtype"]))
            out_specs.append(pl.BlockSpec(memory_space=pl.ANY))
            scratch.append(pltpu.VMEM(move["shape"], move["dtype"]))
            sems += gather_sems(move["groups"])
        else:
            if not isinstance(array, int):
                ins.append(array)
                in_specs.append(pl.BlockSpec(memory_space=pl.ANY))
            outs.append(struct(move["shape"], F32))
            out_specs.append(whole_out(move["shape"]))
            scratch += scatter_scratch(*move["shape"])
            sems += scatter_sems(move["groups"])
    if moves:
        scratch.append(pltpu.SemaphoreType.DMA((sems,)))
    made = pl.pallas_call(
        kernel,
        name=name,
        grid=(steps,),
        out_shape=outs,
        in_specs=in_specs,
        out_specs=out_specs,
        scratch_shapes=scratch,
        compiler_params=pltpu.CompilerParams(**params),
    )(*ins)
    return made[: counts[1]], made[counts[1] :]


def times(left, right):
    return jnp.dot(left, right, preferred_element_type=jnp.float32)


def times_transpose(left, right):
    return lax.dot_general(
        left, right, (((1,), (1,)), ((), ())), preferred_element_type=jnp.float32
    )


def transpose_times(left, right):
    return lax.dot_general(
        left, right, (((0,), (0,)), ((), ())), preferred_element_type=jnp.float32
    )


def normalize(value):
    centre = value - jnp.mean(value, axis=-1, keepdims=True)
    rstd = lax.rsqrt(jnp.mean(centre * centre, axis=-1, keepdims=True) + EPSILON)
    return centre * rstd, rstd


def norm_back(grad_out, normed, rstd, gain):
    scaled = grad_out * gain
    mean_one = jnp.mean(scaled, axis=-1, keepdims=True)
    mean_two = jnp.mean(scaled * normed, axis=-1, keepdims=True)
    return rstd * (scaled - mean_one - normed * mean_two)


def eight(value):
    rows, columns = value.shape
    return jnp.sum(value.reshape(rows // 8, 8, columns), axis=0)


def gelu_parts(value):
    bell = jnp.exp(-0.5 * value * value)
    size = jnp.abs(value)
    t = 1.0 / (1.0 + 0.23164189 * size)
    tail = t * (
        0.127414796
        + t * (-0.142248368 + t * (0.7107068705 + t * (-0.7265760135 + t * 0.5307027145)))
    )
    tail = tail * bell
    phi_big = jnp.where(value >= 0.0, 1.0 - tail, tail)
    return phi_big, bell * 0.3989422804014327


STRIP = 32


def strips(rows, body, carry, unroll=2):
    def step(i, value):
        return body(pl.ds(pl.multiple_of(i * STRIP, STRIP), STRIP), value)

    return lax.fori_loop(0, rows // STRIP, step, carry, unroll=unroll)


def enter_step(pair, patches, cotangent, keep, vec, hidden, source, upstream, bias_sum, spare):
    cells, width = patches.shape[1:]
    high = spare.shape[0] // 2
    at = pl.ds(pl.multiple_of(pair * 2 * high, 16), 2 * high)
    gain, shift = vec[0:1], vec[1:2]
    spare[...] = jnp.zeros_like(spare)
    for w in range(2):
        spare[pl.ds(w * high, cells)] = patches[w].astype(F32)
    source[at] = spare[...].astype(BF)
    for w in range(2):
        normed, _ = normalize(spare[pl.ds(w * high, cells)])
        spare[pl.ds(w * high, cells)] = normed * gain + shift
    hidden[at] = spare[...].astype(BF)

    @pl.when(pair == 0)
    def _():
        bias_sum[...] = jnp.zeros_like(bias_sum)

    spare[...] = jnp.zeros_like(spare)
    for w in range(2):
        mask = jnp.concatenate([keep[w]] * (width // 128), axis=1)
        spare[pl.ds(w * high, cells)] = cotangent[w].astype(F32) * mask[:cells]
    bias_sum[...] += eight(spare[...])
    upstream[at] = spare[...].astype(BF)


def lanes_of(head):
    lane = lax.broadcasted_iota(jnp.int32, (1, 128), 1)
    return (lane // 32) == head


def pick(value, head):
    return jnp.where(lanes_of(head), value, jnp.zeros_like(value))


def attend_step(group, pair, hidden, weights, vec, bias, mask, query, keys, values, probs, out):
    windows, high, columns = query.shape

    @pl.when(pair == 0)
    def _():
        at = pl.ds(pl.multiple_of(group * columns, columns), columns)
        for j, (target, bias_row) in enumerate(((query, 2), (keys, None), (values, 3))):
            product = times(hidden[...], weights(j))
            if bias_row is not None:
                product = product + vec[bias_row : bias_row + 1, at]
            for w in range(windows):
                target[w] = product[w * high : (w + 1) * high].astype(BF)

    scale = 32 ** (-0.5)
    done = []
    for w in range(2):
        window = pair * 2 + w
        parts = []
        for g in range(columns // 128):
            at = pl.ds(g * 128, 128)
            q, k, v = query[window, :, at], keys[window, :, at], values[window, :, at]
            vt = v.T
            heads = []
            for h in range(4):
                score = times_transpose(pick(k, h), q) * scale
                score = score + bias[g * 4 + h, :, :high] + mask[window, :, :high]
                score = jnp.exp(score - jnp.max(score, axis=0, keepdims=True))
                prob = (score * (1.0 / jnp.sum(score, axis=0, keepdims=True))).astype(BF)
                probs[w, g * 4 + h, :, :high] = prob
                heads.append(times(vt[32 * h : 32 * h + 32], prob))
            parts.append(jnp.concatenate(heads, axis=0).T)
        done.append(jnp.concatenate(parts, axis=1))
    rows = pl.ds(pl.multiple_of(pair * 2 * high, 16), 2 * high)
    at = pl.ds(pl.multiple_of(group * columns, columns), columns)
    out[rows, at] = jnp.concatenate(done, axis=0).astype(BF)


def flat(value):
    return value.reshape(-1, value.shape[-1])


def forward_body(direct, made, *refs):
    refs = list(refs)
    take = lambda n: [refs.pop(0) for _ in range(n)]
    patches, cotangent, keep, vec, bias, mask, be = take(7)
    *w_attend, w_output, w_expand = made[:6] if direct else take(6)
    hidden_t, source, upstream, bias_sum, query, keys, values, probs = take(8)
    attended, middle, hidden_two_t, act, slope, grad = take(6)
    spare, hidden, wqkv, wo, we, hidden_two, before, sems = refs
    step = pl.program_id(0)
    rows, width = hidden.shape
    windows, high, columns = query.shape
    pairs, groups = windows // 2, width // columns
    enters, attends = pairs, pairs * groups
    chunk = act.shape[1]
    chunks = w_expand.shape[-1] // chunk

    @pl.when(step < enters)
    def _():
        enter_step(step, patches, cotangent, keep, vec, hidden, source, upstream, bias_sum, spare)

    inner_step = step - enters
    group, pair = inner_step // pairs, lax.rem(inner_step, pairs)

    def load_qkv(number):
        slot = number % 2
        return pltpu.make_async_copy(w_attend[number], wqkv.at[slot], sems.at[slot])

    load_wo = pltpu.make_async_copy(w_output, wo, sems.at[2])

    def load_we(index):
        slot = lax.rem(index, 2)
        at = pl.ds(pl.multiple_of(index * chunk, chunk), chunk)
        return pltpu.make_async_copy(w_expand.at[:, :, :, :, :, at], we.at[slot], sems.at[3 + slot])

    @pl.when((inner_step >= 0) & (inner_step < attends))
    def _():
        @pl.when(inner_step == 0)
        def _():
            hidden_t[...] = hidden[...].T

        for number in range(groups):

            @pl.when(inner_step == number * pairs)
            def _(number=number):
                copy = load_qkv(number)
                copy.start()
                copy.wait()

        slot = lax.rem(group, 2)
        weights = lambda j: flat(wqkv[slot, :, :, :, :, :, pl.ds(j * columns, columns)])
        attend_step(group, pair, hidden, weights, vec, bias, mask, query, keys, values, probs, attended)

    @pl.when(inner_step == attends)
    def _():
        load_wo.start()
        load_we(0).start()
        load_wo.wait()
        for j in range(2):
            at = pl.ds(j * (width // 2), width // 2)
            middle[:, at] = times(attended[...], flat(wo[:, :, :, :, :, at])) + vec[4:5, at]

        def strip(at, carry):
            value = middle[at] + source[at].astype(F32)
            middle[at] = value
            normed, _ = normalize(value)
            hidden_two[at] = (normed * vec[5:6] + vec[6:7]).astype(BF)
            return carry

        strips(rows, strip, 0)
        hidden_two_t[...] = hidden_two[...].T

    @pl.when(inner_step > attends)
    def _():
        index = inner_step - attends - 1
        load_we(index).wait()

        @pl.when(index + 1 < chunks)
        def _():
            load_we(index + 1).start()

        before[...] = times(hidden_two[...], flat(we[lax.rem(index, 2)]))

        def strip(at, carry):
            value = before[at] + be[...]
            big, small = gelu_parts(value)
            act[at] = (value * big).astype(BF)
            slope[at] = (big + value * small).astype(BF)
            return carry

        strips(rows, strip, 0)
        grad[...] = transpose_times(act[...], upstream[...]).astype(BF)


def forward(patches, cotangent, keep, vec, bias, mask, be, gathered, moves, collective):
    windows, cells, width = patches.shape
    high = mask.shape[1]
    rows = windows * high
    heads = bias.shape[0]
    ff = be.shape[1]
    columns, chunk = 256, 512
    groups, pairs = width // columns, windows // 2
    per = columns // 32
    direct = bool(moves)
    enters, attends = pairs, pairs * groups
    steps = enters + attends + 1 + ff // chunk
    group = lambda s: jnp.clip((s - enters) // pairs, 0, groups - 1)
    pair = lambda s: jnp.where(
        s < enters, 0, jnp.where(s < enters + attends, lax.rem(s - enters, pairs), pairs - 1)
    )
    later = lambda s: jnp.maximum(s - enters - attends - 1, 0)
    first = lambda s: (jnp.minimum(s, enters - 1), 0, 0)
    seen = pl.BlockSpec((windows, high, columns), lambda s: (0, 0, group(s)))
    wide = pl.BlockSpec((rows, chunk), lambda s: (0, later(s)))
    any_place = pl.BlockSpec(memory_space=pl.ANY)
    starts = [1.5] * enters + [4.4, 2.7, 2.7, 2.7] * groups + [5.0] + [4.9] * (ff // chunk)
    lead = (4, 2, 2, 2, width // 32)
    return call(
        functools.partial(forward_body, direct),
        "forward",
        steps=steps,
        ins=[patches, cotangent, keep, vec, bias, mask, be] + list(gathered),
        in_specs=[
            pl.BlockSpec((2, cells, width), first),
            pl.BlockSpec((2, cells, width), first),
            pl.BlockSpec((2, high, 128), first),
            whole(vec.shape),
            pl.BlockSpec((per, high, 128), lambda s: (group(s), 0, 0)),
            whole(mask.shape),
            pl.BlockSpec((1, chunk), lambda s: (0, later(s))),
        ]
        + [any_place] * len(gathered),
        outs=[
            struct((width, rows), BF),
            struct((rows, width), BF),
            struct((rows, width), BF),
            struct((8, width), F32),
            struct((windows, high, width), BF),
            struct((windows, high, width), BF),
            struct((windows, high, width), BF),
            struct((windows, heads, high, 128), BF),
            struct((rows, width), BF),
            struct((rows, width), F32),
            struct((width, rows), BF),
            struct((rows, ff), BF),
            struct((rows, ff), BF),
            struct((ff, width), BF),
        ],
        out_specs=[
            whole_out((width, rows)),
            whole_out((rows, width)),
            whole_out((rows, width)),
            whole_out((8, width)),
            seen,
            seen,
            seen,
            pl.BlockSpec((2, per, high, 128), lambda s: (pair(s), group(s), 0, 0)),
            whole_out((rows, width)),
            whole_out((rows, width)),
            whole_out((width, rows)),
            wide,
            wide,
            pl.BlockSpec((chunk, width), lambda s: (later(s), 0)),
        ],
        scratch=[
            pltpu.VMEM((2 * high, width), F32),
            pltpu.VMEM((rows, width), BF),
            pltpu.VMEM((2,) + lead + (3 * columns,), BF),
            pltpu.VMEM(lead + (width,), BF),
            pltpu.VMEM((2,) + lead + (chunk,), BF),
            pltpu.VMEM((rows, width), BF),
            pltpu.VMEM((rows, chunk), F32),
            pltpu.SemaphoreType.DMA((5,)),
        ],
        moves=moves,
        collective=collective,
        starts=starts,
    )


def middle_body(made, *refs):
    refs = list(refs)
    take = lambda n: [refs.pop(0) for _ in range(n)]
    act, slope, ws, we, wo, upstream, hidden_t, middle, attended, vec = take(10)
    result, back_sum, grad_e, mid, grad_o, dout, sums = take(7)
    total, back, branch = refs
    step = pl.program_id(0)
    chunks = back.shape[0]
    rows, width = total.shape
    windows, cells, _ = result.shape
    high = rows // windows

    @pl.when(step == 0)
    def _():
        total[...] = middle[...] + vec[7:8]

    @pl.when(step < chunks)
    def _():
        total[...] += times(act[...], ws[...])
        product = times_transpose(upstream[...], ws[...])
        here = (product * slope[...].astype(F32)).astype(BF)
        back[step] = here
        back_sum[...] = jnp.sum(here.astype(F32), axis=0, keepdims=True)
        grad_e[...] = times(hidden_t[...], here).astype(BF)

    @pl.when(step == chunks - 1)
    def _():
        for w in range(windows):
            result[w] = total[pl.ds(w * high, cells)].astype(BF)
        total[...] = jnp.zeros_like(total)

    @pl.when(step >= chunks)
    def _():
        total[...] += times_transpose(back[step - chunks], we[...])

    @pl.when(step == 2 * chunks - 1)
    def _():
        zero = jnp.zeros((8, width), F32)

        def strip(at, carry):
            gain_sum, shift_sum, out_sum = carry
            normed, rstd = normalize(middle[at])
            value = total[at]
            grad_mid = upstream[at].astype(F32) + norm_back(value, normed, rstd, vec[5:6])
            mid[at] = grad_mid
            low = grad_mid.astype(BF)
            branch[at] = low
            return (
                gain_sum + eight(value * normed),
                shift_sum + eight(value),
                out_sum + eight(low.astype(F32)),
            )

        found = strips(rows, strip, (zero, zero, zero), unroll=1)
        for i in range(3):
            sums[i] = found[i]
        for j in range(2):
            at = pl.ds(j * (width // 2), width // 2)
            grad_o[:, at] = transpose_times(attended[...], branch[:, at]).astype(BF)
            product = times_transpose(branch[...], wo[at])
            for w in range(windows):
                dout[w, :, at] = product[w * high : (w + 1) * high].astype(BF)


def middle_part(act, slope, w_shrink, w_expand, w_output, upstream, hidden_t, middle, attended, vec, windows, cells, moves, collective):
    rows, ff = act.shape
    width = middle.shape[1]
    high = rows // windows
    chunk = 512
    chunks = ff // chunk
    early = lambda s: jnp.minimum(s, chunks - 1)
    later = lambda s: jnp.maximum(s - chunks, 0)
    wide = pl.BlockSpec((rows, chunk), lambda s: (0, early(s)))
    starts = [4.0] * chunks + [1.6] * chunks
    return call(
        middle_body,
        "middle",
        steps=2 * chunks,
        ins=[act, slope, w_shrink, w_expand, w_output, upstream, hidden_t, middle, attended, vec],
        in_specs=[
            wide,
            wide,
            pl.BlockSpec((chunk, width), lambda s: (early(s), 0)),
            pl.BlockSpec((width, chunk), lambda s: (0, later(s))),
            whole((width, width)),
            whole((rows, width)),
            whole((width, rows)),
            whole((rows, width)),
            whole((rows, width)),
            whole(vec.shape),
        ],
        outs=[
            struct((windows, cells, width), BF),
            struct((1, ff), F32),
            struct((width, ff), BF),
            struct((rows, width), F32),
            struct((width, width), BF),
            struct((windows, high, width), BF),
            struct((3, 8, width), F32),
        ],
        out_specs=[
            whole_out((windows, cells, width)),
            pl.BlockSpec((1, chunk), lambda s: (0, early(s))),
            pl.BlockSpec((width, chunk), lambda s: (0, early(s))),
            whole_out((rows, width)),
            whole_out((width, width)),
            whole_out((windows, high, width)),
            whole_out((3, 8, width)),
        ],
        scratch=[
            pltpu.VMEM((rows, width), F32),
            pltpu.VMEM((chunks, rows, chunk), BF),
            pltpu.VMEM((rows, width), BF),
        ],
        moves=moves,
        collective=collective,
        starts=starts,
    )


def backward_body(groups, made, *refs):
    refs = list(refs)
    take = lambda n: [refs.pop(0) for _ in range(n)]
    query, keys, values, dout, probs, hidden_t, source, mid, vec, inverse = take(10)
    w_attend = take(groups)
    out, late = take(2)
    pieces = take(groups)
    bias_low, joint, bias, total, wa, sems = refs
    step = pl.program_id(0)
    windows, high, columns = query.shape
    width, rows = hidden_t.shape
    cells = out.shape[1]
    pairs = windows // 2
    pair = lax.rem(step, pairs)
    group = step // pairs
    scale = 32 ** (-0.5)

    @pl.when(step == 0)
    def _():
        bias_low[...] = jnp.zeros_like(bias_low)
        total[...] = jnp.zeros_like(total)

    @pl.when(step < pairs * groups)
    def _():
        @pl.when(pair == 0)
        def _():
            bias[...] = jnp.zeros_like(bias)

        done = []
        for w in range(2):
            window = pair * 2 + w
            parts = []
            for g in range(columns // 128):
                at = pl.ds(g * 128, 128)
                q, k, v = query[window, :, at], keys[window, :, at], values[window, :, at]
                d = dout[window, :, at]
                kt = k.T
                dq, dk, dv = [], None, None
                for h in range(4):
                    prob = probs[w, g * 4 + h, :, :high]
                    dp = times_transpose(pick(v, h), d)
                    soft = prob.astype(F32)
                    both = soft * dp
                    ds = (both - soft * jnp.sum(both, axis=0, keepdims=True)).astype(BF)
                    bias[g * 4 + h, :, :high] += ds.astype(F32)
                    dq.append(times(kt[32 * h : 32 * h + 32], ds))
                    one, two = pick(times(ds, q), h), pick(times(prob, d), h)
                    dk = one if dk is None else dk + one
                    dv = two if dv is None else dv + two
                parts.append((jnp.concatenate(dq, axis=0).T * scale, dk * scale, dv))
            done.append([jnp.concatenate([p[j] for p in parts], axis=1) for j in range(3)])
        at_rows = pl.ds(pl.multiple_of(pair * 2 * high, 16), 2 * high)
        for j in range(3):
            joint[group, at_rows, pl.ds(j * columns, columns)] = jnp.concatenate([done[0][j], done[1][j]], axis=0).astype(BF)

    for g in range(groups):

        @pl.when(step == pairs * (g + 1) - 1)
        def _(g=g):
            per = columns // 32
            for h in range(per):
                d = g * per + h
                bias_low[d // 8, (d // 4) % 2, (d // 2) % 2, d % 2, :high] = bias[h].astype(BF)
            for j in range(3):
                here = joint[g, :, j * columns : (j + 1) * columns]
                product = times(hidden_t[...], here).astype(BF)
                at = pl.ds(j * columns, columns)
                pieces[g][:, :, :, :, :, at] = product.reshape(pieces[g].shape[:5] + (columns,))
                if j != 1:
                    row = pl.ds(2 if j == 0 else 3, 1)
                    here = jnp.sum(here.astype(F32), axis=0, keepdims=True)
                    late[row, pl.ds(g * columns, columns)] = here

    load = lambda g: pltpu.make_async_copy(w_attend[g], wa.at[g % 2], sems.at[g % 2])

    @pl.when(step == pairs * groups - 1)
    def _():
        load(0).start()

    for g in range(groups):

        @pl.when(step == pairs * groups + g)
        def _(g=g):
            load(g).wait()
            if g + 1 < groups:
                load(g + 1).start()
            total[...] += times_transpose(joint[g], flat(wa[g % 2]))

    @pl.when(step == pl.num_programs(0) - 1)
    def _():
        zero = jnp.zeros((8, width), F32)

        def strip(at, carry):
            gain_sum, shift_sum = carry
            normed, rstd = normalize(source[at].astype(F32))
            value = total[at]
            full = mid[at] + norm_back(value, normed, rstd, vec[0:1])
            total[at] = full * inverse[0, 0]
            return gain_sum + eight(value * normed), shift_sum + eight(value)

        found = strips(rows, strip, (zero, zero), unroll=1)
        for i in range(2):
            late[pl.ds(i, 1)] = jnp.sum(found[i], axis=0, keepdims=True)
        for w in range(windows):
            out[w] = total[pl.ds(w * high, cells)]


def backward_part(query, keys, values, dout, probs, hidden_t, w_attend, source, mid, vec, inverse, cells, moves, collective):
    windows, high, width = query.shape
    rows = hidden_t.shape[1]
    columns = 256
    groups, pairs = width // columns, windows // 2
    per = columns // 32
    steps = groups * pairs
    group = lambda s: jnp.minimum(s // pairs, groups - 1)
    pair = lambda s: jnp.where(s < steps, lax.rem(s, pairs), pairs - 1)
    seen = pl.BlockSpec((windows, high, columns), lambda s: (0, 0, group(s)))
    lead = (4, 2, 2, 2)
    pieces = [(lead + (width // 32, 3 * columns), BF)] * groups + [(lead + (128, 128), BF)]
    outs = [struct((windows, cells, width), F32), struct((4, width), F32)]
    out_specs = [whole_out((windows, cells, width)), whole_out((4, width))]
    scratch = [
        pltpu.VMEM((groups, rows, 3 * columns), BF),
        pltpu.VMEM((per, high, 128), F32),
        pltpu.VMEM((rows, width), F32),
        pltpu.VMEM((2,) + lead + (width // 32, 3 * columns), BF),
        pltpu.SemaphoreType.DMA((2,)),
    ]
    if moves:
        scratch = [pltpu.VMEM(*p) for p in pieces] + scratch
    else:
        outs += [struct(*p) for p in pieces]
        out_specs += [whole_out(p[0]) for p in pieces]
    starts = [4.0, 4.0, 4.0, 6.0] * groups + [2.2] * (groups - 1) + [8.0]
    return call(
        functools.partial(backward_body, groups),
        "backward",
        steps=steps + groups,
        ins=[query, keys, values, dout, probs, hidden_t, source, mid, vec, inverse] + list(w_attend),
        in_specs=[seen] * 4
        + [
            pl.BlockSpec((2, per, high, 128), lambda s: (pair(s), group(s), 0, 0)),
            whole((width, rows)),
            whole((rows, width)),
            whole((rows, width)),
            whole(vec.shape),
            pl.BlockSpec(memory_space=pltpu.SMEM),
        ]
        + [pl.BlockSpec(memory_space=pl.ANY)] * groups,
        outs=outs,
        out_specs=out_specs,
        scratch=scratch,
        moves=moves,
        collective=collective,
        starts=starts,
    )


def update_kernel(pieces, step_number, *refs):
    refs = list(refs)
    take = lambda n: [refs.pop(0) for _ in range(n)]
    inverse, late_sums, bias_sum, small = take(4)
    sums = take(1 + max(p[4] for p in pieces))
    masters, firsts, seconds = take(4), take(4), take(4)
    vec, vec_first, vec_second, table, table_first, table_second = take(6)
    grads_out, firsts_out, seconds_out, news_out, copies_out = (take(4) for _ in range(5))
    vec_out, table_out = take(4), take(4)
    (norms_out,) = take(1)
    message, got, message_two, got_two, vec_grad, heads_grad, sems = refs
    place = Place(sems)
    place.greet()
    devices = got.shape[0] * 8
    scale = inverse[0, 0]
    lane = lax.broadcasted_iota(jnp.int32, (8, 128), 1)
    top = lax.broadcasted_iota(jnp.int32, (8, 128), 0) == 0

    def over(rows, body, carry):
        def step(i, value):
            return body(pl.multiple_of(i * 16, 16), value)

        return lax.fori_loop(0, rows // 16, step, carry)

    def fold(value):
        value = eight(value)
        return functools.reduce(
            jnp.add, [value[:, i : i + 128] for i in range(0, value.shape[1], 128)]
        )

    zero = jnp.zeros((8, 128), F32)
    squares = [zero] * 8
    for k, (row, rows), (column, columns), source_column, number in pieces:
        columns_at = pl.ds(column, columns)

        def body(at, carry):
            here = (pl.ds(row + at, 16), columns_at)
            grad = sums[number][pl.ds(at, 16), pl.ds(source_column, columns)] * scale
            grads_out[k][here] = grad
            weight = masters[k][here]
            return carry[0] + fold(grad * grad), carry[1] + fold(weight * weight)

        squares[k], squares[4 + k] = over(rows, body, (squares[k], squares[4 + k]))

    def packed(values):
        row = zero
        for i, value in enumerate(values):
            row = jnp.where((lane == i) & top, jnp.sum(value), row)
        return row

    message[pl.ds(0, 8)] = packed(squares)
    message[pl.ds(8, 8)] = zero
    message[pl.ds(8, 2)] = small[pl.ds(0, 2)]
    side = 2 * WS - 1
    cell = lax.broadcasted_iota(jnp.int32, (128, 384), 0)
    spot = lax.broadcasted_iota(jnp.int32, (128, 384), 1)
    put = ((cell // WS) * side + lax.rem(cell, WS) == spot) & (cell < WS * WS)
    wide = jnp.dot(bias_sum[...], put.astype(F32), precision=HIGH, preferred_element_type=F32)
    middle = (WS - 1) * side + WS - 1
    column = jnp.zeros((1, 384), F32)
    for j in range(WS * WS):
        shift = middle - (j // WS) * side - j % WS
        column = column + pltpu.roll(wide[j : j + 1], shift, axis=1)
    for b in range(3):
        message[pl.ds(11 + b, 1)] = column[:, 128 * b : 128 * b + 128]
    late_rows = late_sums.shape[0]
    for i in range(late_rows):
        for b in range(8):
            message[pl.ds(16 + 8 * i + b, 1)] = late_sums[i : i + 1, 128 * b : 128 * b + 128]

    events, end = gather_events(place, message, got, 1, False)
    for event, _, _ in events:
        event()
    end()

    place_of = lambda d: (d // 8, (d // 4) % 2, (d // 2) % 2, d % 2)
    found = functools.reduce(jnp.add, [got[place_of(d) + (pl.ds(0, 8),)] for d in range(devices)])
    late = functools.reduce(jnp.add, [got[place_of(d) + (pl.ds(16, 8 * late_rows),)] for d in range(devices)])
    for i in range(late_rows):
        for b in range(8):
            vec_grad[pl.ds(i, 1), pl.ds(128 * b, 128)] = late[8 * i + b : 8 * i + b + 1] * scale
    for d in range(devices):
        block = got[place_of(d) + (pl.ds(8, 8),)] * scale
        vec_grad[pl.ds(4 + 2 * (d % 4), 2), pl.ds(128 * (d // 4), 128)] = block[:2]
        for j in range(3):
            heads_grad[pl.ds(d, 1), pl.ds(128 * j, 128)] = block[3 + j : 4 + j]
    entries = table.shape[0]
    small_grad = vec_grad[...]
    table_grad = heads_grad[...].T[:entries]

    total = lambda value: jnp.sum(value, keepdims=True)
    scalar = lambda k: total(jnp.where(top & (lane == k), found, 0.0))
    grad_square = scalar(0) + scalar(1) + scalar(2) + scalar(3)
    clip_norm = jnp.sqrt(
        grad_square + total(small_grad * small_grad) + total(table_grad * table_grad)
    )
    factor = jnp.minimum(1.0, CLIP_LIMIT / clip_norm)

    def moments(grad, first, second, weight):
        clipped = grad * factor
        first_new = MOMENT_ONE * first + (1.0 - MOMENT_ONE) * clipped
        second_new = MOMENT_TWO * second + (1.0 - MOMENT_TWO) * clipped * clipped
        update = (first_new * (1.0 / (1.0 - MOMENT_ONE**step_number))) / (
            jnp.sqrt(second_new * (1.0 / (1.0 - MOMENT_TWO**step_number))) + ADAM_EPS
        ) + DECAY * weight
        return first_new, second_new, update

    squares = [zero] * 4
    for k in range(4):

        def body(at, carry):
            at = pl.ds(at, 16)
            first, second, change = moments(
                grads_out[k][at], firsts[k][at], seconds[k][at], masters[k][at]
            )
            firsts_out[k][at] = first
            seconds_out[k][at] = second
            news_out[k][at] = change
            return carry + fold(change * change)

        squares[k] = over(masters[k].shape[0], body, squares[k])
    message_two[pl.ds(0, 8)] = packed(squares)
    message_two[pl.ds(8, 8)] = zero

    events, end = gather_events(place, message_two, got_two, 1, False)
    events = [event for event, _, _ in events]
    events[0]()

    first, second, change = moments(small_grad, vec_first[...], vec_second[...], vec[...])
    rows = lambda value: jnp.sqrt(jnp.sum(value * value, axis=1, keepdims=True))
    vec_out[0][...] = small_grad
    vec_out[1][...] = first
    vec_out[2][...] = second
    vec_out[3][...] = vec[...] - LEARN_RATE * (rows(vec[...]) / rows(change)) * change
    first, second, change = moments(table_grad, table_first[...], table_second[...], table[...])
    table_out[0][...] = table_grad
    table_out[1][...] = first
    table_out[2][...] = second
    ratio = jnp.sqrt(total(table[...] * table[...])) / jnp.sqrt(total(change * change))
    table_out[3][...] = table[...] - LEARN_RATE * ratio * change

    for event in events[1:]:
        event()
    end()
    second_found = functools.reduce(
        jnp.add, [got_two[place_of(d) + (pl.ds(0, 8),)] for d in range(devices)]
    )
    norms = jnp.where(top & (lane == 8), clip_norm, 0.0)
    for k in range(4):
        weight_norm = jnp.sqrt(scalar(4 + k))
        update_norm = jnp.sqrt(total(jnp.where(top & (lane == k), second_found, 0.0)))
        norms = jnp.where(top & (lane == k), weight_norm, norms)
        norms = jnp.where(top & (lane == 4 + k), update_norm, norms)
        ratio = LEARN_RATE * (weight_norm / update_norm)

        def body(at, carry):
            at = pl.ds(at, 16)
            fresh = masters[k][at] - ratio * news_out[k][at]
            news_out[k][at] = fresh
            copies_out[k][at] = fresh.astype(BF)
            return carry

        over(masters[k].shape[0], body, 0)
    norms_out[...] = norms


def update(collective, inverse, late_sums, bias_sum, small, sums, pieces, masters, firsts, seconds, vectors, tables):
    vmem = pl.BlockSpec(memory_space=pltpu.VMEM)
    ins = [inverse, late_sums, bias_sum, small] + list(sums)
    ins += list(masters) + list(firsts) + list(seconds) + list(vectors) + list(tables)
    like = lambda arrays, dtype=F32: [struct(a.shape, dtype) for a in arrays]
    outs = like(masters) * 4 + like(masters, BF)
    outs += [struct(vectors[0].shape, F32)] * 4 + [struct(tables[0].shape, F32)] * 4
    outs += [struct((8, 128), F32)]
    made = pl.pallas_call(
        functools.partial(update_kernel, pieces, STEP),
        name="update",
        out_shape=outs,
        in_specs=[pl.BlockSpec(memory_space=pltpu.SMEM)] + [vmem] * (len(ins) - 1),
        out_specs=[vmem] * len(outs),
        scratch_shapes=[
            pltpu.VMEM((48, 128), F32),
            pltpu.VMEM((4, 2, 2, 2, 48, 128), F32),
            pltpu.VMEM((16, 128), F32),
            pltpu.VMEM((4, 2, 2, 2, 16, 128), F32),
            pltpu.VMEM(vectors[0].shape, F32),
            pltpu.VMEM((32, 384), F32),
            pltpu.SemaphoreType.DMA((2 * gather_sems(1),)),
        ],
        compiler_params=pltpu.CompilerParams(
            collective_id=collective, has_side_effects=True, vmem_limit_bytes=VMEM_LIMIT
        ),
    )(*ins)
    matrices = [[made[4 * j + k] for j in range(5)] for k in range(4)]
    norms = made[-1]
    return matrices, made[20:24], made[24:28], norms[0, 8], norms[0, :8].reshape(2, 4)


def local(
    ndp,
    nfs,
    patches,
    cotangent,
    pad_mask,
    attend_weight,
    attend_first,
    attend_second,
    output_weight,
    output_first,
    output_second,
    expand_weight,
    expand_first,
    expand_second,
    shrink_weight,
    shrink_first,
    shrink_second,
    vector_params,
    vector_first,
    vector_second,
    position_table,
    table_first,
    table_second,
):
    windows, cells, width = patches.shape
    keep = pad_mask.astype(jnp.float32)
    local_count = jnp.sum(keep)
    devices = ndp * nfs
    shard_rows = min(attend_weight.shape[0], shrink_weight.shape[0])
    direct = nfs == 4 and ndp == 8 and shard_rows % 32 == 0
    masters = (attend_weight, output_weight, expand_weight, shrink_weight)
    part_rows = shrink_weight.shape[0] // 2

    high = -(-cells // 8) * 8
    keep_rows = jnp.pad(keep, ((0, 0), (0, high - cells)))[:, :, None]
    keep_rows = jnp.broadcast_to(keep_rows, (windows, high, 128))
    there = (jnp.arange(high) < cells)[None, :, None]
    mask = jnp.where(there, (keep_rows - 1.0) * MASK_FILL, -1e30)
    relative = position_table.shape[0]
    index = jnp.pad(position_index(WS).T, ((0, high - cells), (0, 128 - cells)), constant_values=-1)
    onehot = (
        index.reshape(-1)[None, :] == jnp.arange(relative, dtype=jnp.int32)[:, None]
    ).astype(BF)
    terms, rest = [], position_table.T
    for _ in range(3):
        term = lax.reduce_precision(rest, 8, 7)
        terms.append(term.astype(BF))
        rest = rest - term
    bias = times(jnp.concatenate(terms), onehot).reshape(3, -1, high, 128)
    bias = bias[0] + bias[1] + bias[2]
    expand_bias = vector_params[8:].reshape(1, -1)
    lead = (4, 2, 2, 2, -1)
    group_columns = [[(j * width + g * 256, 256) for j in range(3)] for g in range(4)]
    gathered, moves = [], []
    if direct:
        moves = [
            *[
                gather(attend_weight, BF, relay=False, need=4 + 4 * g, columns=columns)
                for g, columns in enumerate(group_columns)
            ],
            gather(output_weight, BF, need=20),
            gather(expand_weight, BF, need=20),
            gather(shrink_weight, BF),
            gather(jnp.full((16, 128), local_count, F32), F32, 1, False),
        ]
    else:
        gathered = [
            lax.all_gather(m.astype(BF), AXES, axis=0, tiled=True).reshape(lead + m.shape[1:])
            for m in masters
        ]
        w_attend = [
            jnp.concatenate([gathered[0][..., a : a + n] for a, n in columns], axis=-1)
            for columns in group_columns
        ]
        gathered = w_attend + gathered[1:]
    forward_outs, made = forward(
        patches,
        cotangent,
        keep_rows,
        vector_params,
        bias,
        mask,
        expand_bias,
        () if direct else gathered[:6],
        moves,
        1,
    )
    hidden_t, source, upstream, shrink_sum, query, keys, values, probs = forward_outs[:8]
    attended, middle, hidden_two_t, activated, slope, grad_shrink = forward_outs[8:]
    if direct:
        total = jnp.sum(made[-1][..., 0, 0])
        gathered = made[:-1]
    else:
        total = lax.psum(local_count, AXES)
    w_attend = gathered[:4]
    w_output, w_expand, w_shrink = (w.reshape(-1, w.shape[-1]) for w in gathered[4:])
    inverse = (1.0 / total).reshape(1, 1)

    def parts(grad):
        return grad.reshape(lead + grad.shape[-1:])

    if direct:
        moves = [scatter(parts(grad_shrink))]
    middle_outs, owned_shrink = middle_part(
        activated,
        slope,
        w_shrink,
        w_expand,
        w_output,
        upstream,
        hidden_two_t,
        middle,
        attended,
        vector_params,
        windows,
        cells,
        moves,
        2,
    )
    block_out, grad_expand_bias, grad_expand, grad_middle, grad_output, dout, inner_sums = middle_outs
    inner_rows = jnp.sum(inner_sums, axis=1)
    early_sums = jnp.concatenate(
        [
            inner_rows[2:3],
            inner_rows[:2],
            jnp.sum(shrink_sum, axis=0, keepdims=True),
            grad_expand_bias.reshape(-1, width),
        ],
        axis=0,
    )
    if direct:
        small = early_sums.astype(BF).reshape(4, 2, 8, 128).transpose(2, 0, 1, 3)
        small = jnp.pad(small.reshape(devices, 2, 128), ((0, 0), (0, 30), (0, 0)))
        piece_shape = (width // 32, 3 * 256)
        moves = [
            scatter(parts(grad_expand)),
            scatter(parts(grad_output)),
            scatter(parts(small), groups=1),
        ]
        moves += [scatter(g, piece_shape, step=4 * (g + 1)) for g in range(4)]
        moves.append(scatter(4, (128, 128), groups=1, step=16))
    backward_outs, made = backward_part(
        query,
        keys,
        values,
        dout,
        probs,
        hidden_t,
        w_attend,
        source,
        grad_middle,
        vector_params,
        inverse,
        cells,
        moves,
        3,
    )
    input_grad, late_sums = backward_outs[:2]
    grad_pieces, grad_bias = backward_outs[2:-1], backward_outs[-1]

    def finish_direct(block_out, input_grad, late_sums, made, owned_shrink, firsts, seconds):
        expand_owned, output_owned, small_owned = made[:3]
        bias_owned = made[-1]
        sums = list(made[3:-1]) + [output_owned, expand_owned, owned_shrink[0]]
        pieces = [
            (0, (0, attend_weight.shape[0]), (j * width + g * 256, 256), j * 256, g)
            for g in range(4)
            for j in range(3)
        ]
        pieces += [
            (k, (0, masters[k].shape[0]), (0, masters[k].shape[1]), 0, 3 + k) for k in (1, 2, 3)
        ]
        matrices, vector_outs, table_outs, clip_norm, matrix_norms = update(
            4,
            inverse,
            late_sums,
            bias_owned,
            small_owned,
            sums,
            pieces,
            masters,
            firsts,
            seconds,
            (vector_params, vector_first, vector_second),
            (position_table, table_first, table_second),
        )
        outs = [block_out, input_grad]
        for matrix in matrices:
            outs += matrix
        return (*outs, *vector_outs, *table_outs, clip_norm, matrix_norms)

    firsts = (attend_first, output_first, expand_first, shrink_first)
    seconds = (attend_second, output_second, expand_second, shrink_second)
    if direct:
        return finish_direct(
            block_out, input_grad, late_sums, made, owned_shrink, firsts, seconds
        )
    grad_attend = jnp.stack([p.reshape(width, 3, -1) for p in grad_pieces], axis=2)
    grad_attend = grad_attend.reshape(width, -1)
    owned = [
        lax.psum_scatter(g.astype(F32), AXES, scatter_dimension=0, tiled=True)
        for g in (grad_attend, grad_output, grad_expand, grad_shrink)
    ]
    grad_table = lax.dot_general(
        onehot.astype(F32),
        grad_bias.reshape(HEADS, 128, 128)[:, :high].astype(F32).reshape(HEADS, -1),
        (((1,), (1,)), ((), ())),
        precision=HIGH,
    )
    vector_local = jnp.concatenate([late_sums, early_sums], axis=0)
    vector_sum, table_sum = lax.psum((vector_local, grad_table), AXES)
    vector_grad, table_grad = vector_sum / total, table_sum / total
    matrix_grads = tuple((g / total for g in owned))
    grad_squares = jnp.stack([jnp.sum(g * g) for g in matrix_grads])
    weight_squares = jnp.stack([jnp.sum(m * m) for m in masters])
    grad_total, weight_total = lax.psum((grad_squares, weight_squares), AXES)
    clip_norm = jnp.sqrt(
        jnp.sum(grad_total) + jnp.sum(vector_grad * vector_grad) + jnp.sum(table_grad * table_grad)
    )
    factor = jnp.minimum(1.0, CLIP_LIMIT / clip_norm)
    sectioned = [
        moments(matrix_grads[k], firsts[k], seconds[k], masters[k], factor) for k in range(4)
    ]
    update_squares = jnp.stack([jnp.sum(s[2] * s[2]) for s in sectioned])
    update_total = lax.psum(update_squares, AXES)
    weight_norms = jnp.sqrt(weight_total)
    update_norms = jnp.sqrt(update_total)
    matrix_outs = []
    for k in range(4):
        fresh = masters[k] - LEARN_RATE * (weight_norms[k] / update_norms[k]) * sectioned[k][2]
        matrix_outs.append(
            (matrix_grads[k], sectioned[k][0], sectioned[k][1], fresh, fresh.astype(jnp.bfloat16))
        )
    vec_first, vec_second, vec_update = moments(
        vector_grad, vector_first, vector_second, vector_params, factor
    )
    vec_ratio = jnp.sqrt(jnp.sum(vector_params * vector_params, axis=1, keepdims=True)) / jnp.sqrt(
        jnp.sum(vec_update * vec_update, axis=1, keepdims=True)
    )
    vec_fresh = vector_params - LEARN_RATE * vec_ratio * vec_update
    tab_first, tab_second, tab_update = moments(
        table_grad, table_first, table_second, position_table, factor
    )
    tab_ratio = jnp.sqrt(jnp.sum(position_table * position_table)) / jnp.sqrt(
        jnp.sum(tab_update * tab_update)
    )
    tab_fresh = position_table - LEARN_RATE * tab_ratio * tab_update
    matrix_norms = jnp.stack([weight_norms, update_norms])
    attend_o, output_o, expand_o, shrink_o = matrix_outs
    return (
        block_out,
        input_grad,
        attend_o[0],
        attend_o[1],
        attend_o[2],
        attend_o[3],
        attend_o[4],
        output_o[0],
        output_o[1],
        output_o[2],
        output_o[3],
        output_o[4],
        expand_o[0],
        expand_o[1],
        expand_o[2],
        expand_o[3],
        expand_o[4],
        shrink_o[0],
        shrink_o[1],
        shrink_o[2],
        shrink_o[3],
        shrink_o[4],
        vector_grad,
        vec_first,
        vec_second,
        vec_fresh,
        table_grad,
        tab_first,
        tab_second,
        tab_fresh,
        clip_norm,
        matrix_norms,
    )


def solution(mesh):
    in_specs = (
        P(("dp", "fsdp"), None, None),
        P(("dp", "fsdp"), None, None),
        P(("dp", "fsdp"), None),
        P(("dp", "fsdp"), None),
        P(("dp", "fsdp"), None),
        P(("dp", "fsdp"), None),
        P(("dp", "fsdp"), None),
        P(("dp", "fsdp"), None),
        P(("dp", "fsdp"), None),
        P(("dp", "fsdp"), None),
        P(("dp", "fsdp"), None),
        P(("dp", "fsdp"), None),
        P(("dp", "fsdp"), None),
        P(("dp", "fsdp"), None),
        P(("dp", "fsdp"), None),
        P(),
        P(),
        P(),
        P(),
        P(),
        P(),
    )
    out_specs = (
        P(("dp", "fsdp"), None, None),
        P(("dp", "fsdp"), None, None),
        P(("dp", "fsdp"), None),
        P(("dp", "fsdp"), None),
        P(("dp", "fsdp"), None),
        P(("dp", "fsdp"), None),
        P(("dp", "fsdp"), None),
        P(("dp", "fsdp"), None),
        P(("dp", "fsdp"), None),
        P(("dp", "fsdp"), None),
        P(("dp", "fsdp"), None),
        P(("dp", "fsdp"), None),
        P(("dp", "fsdp"), None),
        P(("dp", "fsdp"), None),
        P(("dp", "fsdp"), None),
        P(("dp", "fsdp"), None),
        P(("dp", "fsdp"), None),
        P(("dp", "fsdp"), None),
        P(("dp", "fsdp"), None),
        P(("dp", "fsdp"), None),
        P(("dp", "fsdp"), None),
        P(("dp", "fsdp"), None),
        P(),
        P(),
        P(),
        P(),
        P(),
        P(),
        P(),
        P(),
        P(),
        P(),
    )
    sizes = (mesh.shape["dp"], mesh.shape["fsdp"])
    return jax.shard_map(functools.partial(local, *sizes), mesh=mesh, in_specs=in_specs, out_specs=out_specs, check_vma=False)
```

time: 522 us -> 436 us (0.84)
  Pallas kernels: 460 us -> 375 us
    pallas_call x7 -> x3, Pallas kernels: 423 us -> 339 us  [call(): pl.pallas_call(kernel, name=name, grid=(steps,), out_shape=outs, in_specs...]
    unnamed x110 -> x104, local copies, waits for them, and re-layouts: 39.2 us -> 39.1 us
where the time goes in v3:
time: 436 us; the launch traced here: 431 us
  Pallas kernels  375 us (86%)
  local copies, waits for them, and re-layouts  44.7 us (10%)
  other arithmetic  6.01 us (1%)
    pallas_call x3, Pallas kernels, call(): pl.pallas_call(kernel, name=name, grid=(steps,), out_shape=outs, in_specs...  339 us
    unnamed x104, local copies, waits for them, and re-layouts  39.1 us
    pallas_call x1, Pallas kernels, update(): pl.pallas_call(functools.partial(update_kernel, pieces, STEP), name='upda...  35.4 us

profile of v3, /device:TPU:0, one launch (start us, length us, event | category | flops | bytes accessed | tf_op | source)
XLA Modules:
  0.0 430.9 jit_solution(6513033522564992601)
XLA Ops:
  0.8 0.8 reduce-precision_convert_fusion.1
  1.6 3.8 fusion
  5.7 1.5 copy.65
  7.3 0.9 broadcast_select_fusion.refs_5_
  8.2 0.9 broadcast_in_dim.33.refs_2_
  9.2 2.1 copy.53.refs_0_
  11.2 2.1 copy.54.refs_1_
  13.4 0.8 slice_bitcast_fusion
  15.3 1.2 broadcast_in_dim.37.refs_11_
  16.6 153.5 %forward.1 = (bf16[1024,832]{1,0:T(8,128)(2,1)}, bf16[832,1024]{1,0:T(8,128)(2,1)}, bf16[832,1024]{1,0:T(8,128)(2,1)}, f32[8,1024]{1,0:T(8,128)}, bf16[8,104,102...) custom-call(bf16[8,100,1024]{2,1,0:T(8,128)(2,1)} %copy.53.refs_0_, ...), custom_call_target="tpu_custom_call" | custom-call | tf_op jit(solution)/shard_map/forward/pallas_call | solution.py:623
  170.1 66.2 %middle.1 = (bf16[8,100,1024]{2,1,0:T(8,128)(2,1)}, f32[1,4096]{1,0:T(1,128)}, bf16[1024,4096]{1,0:T(8,128)(2,1)}, f32[832,1024]{1,0:T(8,128)}, bf16[1024,1024]{...) custom-call(bf16[832,4096]{1,0:T(8,128)(2,1)} %get-tuple-element.101.refs_0_, ...), custom_call_target="tpu_custom_call" | custom-call | tf_op jit(solution)/shard_map/middle/pallas_call | solution.py:623
  236.3 0.8 convert_reduce_fusion
  237.0 0.9 reduce_sum.38
  238.1 0.7 pad.14
  238.8 1.5 slice_reduce_fusion
  241.1 119.5 %backward.1 = (f32[8,100,1024]{2,1,0:T(8,128)}, f32[4,1024]{1,0:T(4,128)}, f32[32,4096]{1,0:T(8,128)}, f32[32,1024]{1,0:T(8,128)}, f32[32,128]{1,0:T(8,128)}, /*...) custom-call(bf16[8,104,1024]{2,1,0:T(8,128)(2,1)} %get-tuple-element.112, ...), custom_call_target="tpu_custom_call" | custom-call | tf_op jit(solution)/shard_map/backward/pallas_call | solution.py:623
  360.6 0.8 copy.56.refs_26_
  361.4 0.8 copy.57.refs_27_
  362.2 0.8 copy.58.refs_28_
  363.0 35.4 %update.1 = (f32[32,3072]{1,0:T(8,128)}, f32[32,1024]{1,0:T(8,128)}, f32[32,4096]{1,0:T(8,128)}, f32[128,1024]{1,0:T(8,128)}, f32[32,3072]{1,0:T(8,128)}, /*inde...) custom-call(f32[1,1]{1,0:T(1,128)} %bitcast.6.refs_9_.refs_0_, ...), custom_call_target="tpu_custom_call" | custom-call | tf_op jit(solution)/shard_map/update/pallas_call | solution.py:1400
  398.4 1.7 copy.61
  400.1 1.7 copy.62
  401.8 1.7 copy.63
  403.4 1.7 copy.64
  405.1 0.7 slice_reduce_fusion.1
  405.8 0.6 reshape_squeeze.3
  406.4 1.3 slice.39
  407.7 3.6 copy.60
  411.3 2.1 copy.59
  413.4 0.7 copy.91
  414.1 0.7 copy.92
  414.9 0.7 copy.93
  415.6 0.7 copy.94
  416.4 0.7 copy.95
  417.1 0.7 copy.96
  417.7 0.7 copy.97
  418.4 0.7 copy.98
  419.0 0.7 copy.99
  420.3 0.8 copy.101
  421.1 0.8 copy.102
  421.9 0.8 copy.103
  422.7 0.8 copy.104
  423.5 0.7 copy.105
  424.2 0.8 copy.106
  425.1 0.8 copy.107
  425.9 0.8 copy.108
  426.7 0.8 copy.109
  427.5 0.7 copy.110
  (86 shorter events, 5.0 us)
Async XLA Ops:
  5.7 1.5 copy-start.32
  5.7 3.4 copy-start.2
  9.2 2.1 copy-start.3
  170.1 67.9 %copy-start.31 = (f32[8,1024]{1,0:T(8,128)S(1)}, f32[8,1024]{1,0:T(8,128)}, u32[]{:S(2)}) copy-start(f32[8,1024]{1,0:T(8,128)} %get-tuple-element.128) | copy-start | bytes 98308
  241.1 119.5 %copy-start.19 = (f32[361,32]{0,1:T(8,128)S(1)}, f32[361,32]{0,1:T(8,128)}, u32[]{:S(2)}) copy-start(f32[361,32]{0,1:T(8,128)} %param.39) | copy-start | bytes 138628
  241.1 120.3 %copy-start.29 = (f32[361,32]{0,1:T(8,128)S(1)}, f32[361,32]{0,1:T(8,128)}, u32[]{:S(2)}) copy-start(f32[361,32]{0,1:T(8,128)} %param.40) | copy-start | bytes 138628
  241.1 121.1 %copy-start.30 = (f32[361,32]{0,1:T(8,128)S(1)}, f32[361,32]{0,1:T(8,128)}, u32[]{:S(2)}) copy-start(f32[361,32]{0,1:T(8,128)} %param.41) | copy-start | bytes 138628
  363.0 44.7 %copy-start = (f32[8,100,1024]{2,1,0:T(8,128)S(1)}, f32[8,100,1024]{2,1,0:T(8,128)}, u32[]{:S(2)}) copy-start(f32[8,100,1024]{2,1,0:T(8,128)} %get-tuple-element.171) | copy-start | bytes 9830404
  407.7 3.6 copy-start.1
  411.3 2.1 copy-start.15
  411.3 2.8 copy-start.14
  411.3 3.6 copy-start.13
  413.4 2.3 copy-start.12
  413.4 3.0 copy-start.18
  413.4 3.7 copy-start.23
  413.4 4.4 %copy-start.22 = (f32[32,1024]{1,0:T(8,128)S(1)}, f32[32,1024]{1,0:T(8,128)}, u32[]{:S(2)}) copy-start(f32[32,1024]{1,0:T(8,128)} %get-tuple-element.249) | copy-start | bytes 393220
  414.1 4.3 copy-start.21
  414.1 4.9 %copy-start.20 = (f32[32,1024]{1,0:T(8,128)S(1)}, f32[32,1024]{1,0:T(8,128)}, u32[]{:S(2)}) copy-start(f32[32,1024]{1,0:T(8,128)} %get-tuple-element.251) | copy-start | bytes 393220
  414.1 5.6 %copy-start.28 = (bf16[32,1024]{1,0:T(8,128)(2,1)S(1)}, bf16[32,1024]{1,0:T(8,128)(2,1)}, u32[]{:S(2)}) copy-start(bf16[32,1024]{1,0:T(8,128)(2,1)} %get-tuple-element.252) | copy-start | bytes 196612
  414.9 5.5 %copy-start.11 = (f32[32,4096]{1,0:T(8,128)S(1)}, f32[32,4096]{1,0:T(8,128)}, u32[]{:S(2)}) copy-start(f32[32,4096]{1,0:T(8,128)} %get-tuple-element.253) | copy-start | bytes 1572868
  415.6 5.5 %copy-start.10 = (f32[32,4096]{1,0:T(8,128)S(1)}, f32[32,4096]{1,0:T(8,128)}, u32[]{:S(2)}) copy-start(f32[32,4096]{1,0:T(8,128)} %get-tuple-element.254) | copy-start | bytes 1572868
  417.1 4.9 %copy-start.9 = (f32[32,4096]{1,0:T(8,128)S(1)}, f32[32,4096]{1,0:T(8,128)}, u32[]{:S(2)}) copy-start(f32[32,4096]{1,0:T(8,128)} %get-tuple-element.255) | copy-start | bytes 1572868
  419.0 3.7 copy-start.8
  421.1 2.4 copy-start.17
  421.1 3.1 copy-start.7
  421.9 3.1 copy-start.6
  422.7 3.1 copy-start.5
  424.2 2.4 copy-start.4
  425.0 2.4 copy-start.16
  425.0 3.1 copy-start.27
  425.0 3.7 copy-start.26
  425.0 4.4 %copy-start.25 = (f32[12,1024]{1,0:T(8,128)S(1)}, f32[12,1024]{1,0:T(8,128)}, u32[]{:S(2)}) copy-start(f32[12,1024]{1,0:T(8,128)} %get-tuple-element.265) | copy-start | bytes 147460
  425.9 4.2 copy-start.24
